TPU v7x, 32 devices: a whole 2x2x4 slice. The times are simulated.
32 devices in a mesh: rep: 8 (over y, x, core), blk: 4 (over z).
Axes of the slice: x: 2, y: 2, z: 4, core: 2. Of those that a mesh axis runs over, the one named last changes fastest.
Arguments:
- tokens: bfloat16 [4096, 1536], P(('rep', 'blk')), may hold values from -64 to 64
- attn_in: float32 [1536, 2048], P(('rep', 'blk')), may hold values from -8 to 8
- attn_out: float32 [1536, 1536], P(('rep', 'blk')), may hold values from -0.15625 to 0.15625
- expert_in: float32 [16, 1536, 1536], P(None, ('rep', 'blk')), may hold values from -0.15625 to 0.15625
- expert_out: float32 [16, 768, 1536], P(None, ('rep', 'blk')), may hold values from -0.21875 to 0.21875
- attn_gain: float32 [1536], replicated, may hold values from 0.25 to 1.75
- moe_gain: float32 [1536], replicated, may hold values from 0.25 to 1.75
- lengths: int32 [8, 6], P('rep'), may hold values from 1 to 256, 512 in all within a row
- page_table: int32 [8, 4], P('rep'), may hold values from 0 to 3, each once within a row
- routes: int32 [4096, 4], P(('rep', 'blk')), may hold values from 0 to 15, all different within a row; in each aligned block of 128 rows (0 to 127, 128 to 255, ...) at most 64 rows name the same one
- gates: bfloat16 [4096, 4], P(('rep', 'blk')), may hold values from 0.19921875 to 1
Outputs:
- mixed: bfloat16 [4096, 1536], P(('rep', 'blk'))
- kv_cache: bfloat16 [32, 128, 512], P(('rep', 'blk'))
Inputs may be any that keep to these rules, and one draw needn't show every extreme that they name: Each replica's lengths sum to 512. `page_table`: each replica's row is a permutation of its 4 pages. `routes`: a token names 4 different experts; among the rows of one device no expert is named more than 64 times.
All inputs are finite; a program needn't handle non-finite values.
Results may differ from a plain program's by a relative error of at most 0.013.
Values may be sent and summed in bfloat16 or wider, within the bound.
No kernel may reach another device: no remote copies, remote signals or barrier semaphores. Data moves between devices by JAX's collectives and lax.ppermute only.
A program may use at most 128 MiB of HBM per device.

v0:
```python
import functools
import math

import jax
import jax.numpy as jnp
from jax import lax
from jax.sharding import PartitionSpec as P

D = 1536
FF = 768
QH = 12
KVH = 2
HD = 128
E = 16
PAGE = 128
CAP = 64
QW = 1536


def rms_scale(values, gain):
    values = values.astype(jnp.float32)
    mean_sq = jnp.mean(values * values, axis=-1, keepdims=True)
    return values * lax.rsqrt(mean_sq + 1e-06) * gain


def rotate(values, position):
    half = values.shape[-1] // 2
    steps_all = jnp.arange(half, dtype=jnp.float32)
    frequency = jnp.exp(steps_all * (-2.0 * math.log(10000.0) / values.shape[-1]))
    angle = position[:, None] * frequency[None, :]
    cosine = jnp.cos(angle)[:, None, :]
    sine = jnp.sin(angle)[:, None, :]
    front = values[..., :half]
    behind = values[..., half:]
    return jnp.concatenate(
        [front * cosine - behind * sine, behind * cosine + front * sine], axis=-1
    )


def segment_info(lengths, count):
    starts = jnp.cumsum(lengths) - lengths
    index = jnp.arange(count, dtype=jnp.int32)
    member = (index[:, None] >= starts[None, :]).astype(jnp.int32)
    segment = jnp.sum(member, axis=1) - 1
    owner = segment[:, None] == jnp.arange(lengths.shape[0], dtype=jnp.int32)[None, :]
    begin = jnp.sum(jnp.where(owner, starts[None, :], 0), axis=1)
    return (segment, index - begin)


def slot_tables(weight, depth):
    member = (weight > 0).astype(jnp.int32)
    ranked = jnp.cumsum(member, axis=0) - 1
    slot_ids = jnp.arange(depth, dtype=jnp.int32)
    hit = (member.T[:, None, :] == 1) & (ranked.T[:, None, :] == slot_ids[None, :, None])
    onehot = hit.astype(jnp.bfloat16)
    gated = jnp.where(hit, weight.T[:, None, :], jnp.zeros((), jnp.bfloat16))
    return (onehot, gated)


def body(
    tokens,
    attn_in,
    attn_out,
    expert_in,
    expert_out,
    attn_gain,
    moe_gain,
    lengths,
    page_table,
    routes,
    gates,
):
    count = tokens.shape[0]
    cycle_size = lax.axis_size("blk")
    place = lax.axis_index("blk")
    group_rows = count * cycle_size
    local_experts = E // cycle_size
    heads_per = QH // KVH
    segment_all, position_all = segment_info(lengths[0], group_rows)
    first = place * count
    my_index = first + jnp.arange(count, dtype=jnp.int32)
    my_segment = lax.dynamic_slice_in_dim(segment_all, first, count)
    my_position = lax.dynamic_slice_in_dim(position_all, first, count).astype(jnp.float32)
    normed = rms_scale(tokens, attn_gain).astype(jnp.bfloat16)
    columns = normed
    projected = jnp.dot(
        columns,
        lax.all_gather(attn_in.astype(jnp.bfloat16), ("rep", "blk"), axis=0, tiled=True),
        preferred_element_type=jnp.float32,
    )
    queries = rotate(projected[:, :QW].reshape(count, QH, HD), my_position).astype(jnp.bfloat16)
    keys_here = rotate(
        projected[:, QW : QW + KVH * HD].reshape(count, KVH, HD), my_position
    ).astype(jnp.bfloat16)
    values_here = projected[:, QW + KVH * HD :].astype(jnp.bfloat16)
    cache_here = jnp.concatenate([keys_here.reshape(count, KVH * HD), values_here], axis=1)
    cache_all = lax.all_gather(cache_here, "blk", axis=0, tiled=True)
    keys_all = cache_all[:, : KVH * HD].reshape(group_rows, KVH, HD)
    values_all = cache_all[:, KVH * HD :].reshape(group_rows, KVH, HD)
    grouped = queries.reshape(count, KVH, heads_per, HD)
    scores = jnp.einsum(
        "igrd,jgd->grij", grouped, keys_all, preferred_element_type=jnp.float32
    ) / math.sqrt(HD)
    key_index = jnp.arange(group_rows, dtype=jnp.int32)
    allowed = (my_segment[:, None] == segment_all[None, :]) & (
        key_index[None, :] <= my_index[:, None]
    )
    scores = jnp.where(allowed[None, None], scores, jnp.float32(-1e30))
    highest = jnp.max(scores, axis=-1, keepdims=True)
    weights = jnp.exp(scores - highest)
    probs = (weights / jnp.sum(weights, axis=-1, keepdims=True)).astype(jnp.bfloat16)
    attended = jnp.einsum("grij,jgd->igrd", probs, values_all, preferred_element_type=jnp.float32)
    attended = attended.astype(jnp.bfloat16).reshape(count, QW)
    columns = attended
    hidden = tokens.astype(jnp.float32) + jnp.dot(
        columns,
        lax.all_gather(attn_out.astype(jnp.bfloat16), ("rep", "blk"), axis=0, tiled=True),
        preferred_element_type=jnp.float32,
    )
    page_count = count // PAGE
    targets = place * page_count + jnp.arange(page_count, dtype=jnp.int32)
    table = page_table[0]
    logical = jnp.sum(
        jnp.where(
            table[None, :] == targets[:, None],
            jnp.arange(table.shape[0], dtype=jnp.int32)[None, :],
            0,
        ),
        axis=1,
    )
    row_ids = logical[:, None] * PAGE + jnp.arange(PAGE, dtype=jnp.int32)[None, :]
    kv_pages = cache_all[row_ids]
    normed_two = rms_scale(hidden, moe_gain).astype(jnp.bfloat16)
    expert_ids = jnp.arange(E, dtype=jnp.int32)
    dense = jnp.sum(
        jnp.where(
            routes[:, :, None] == expert_ids[None, None, :],
            gates.astype(jnp.float32)[:, :, None],
            jnp.float32(0.0),
        ),
        axis=1,
    ).astype(jnp.bfloat16)
    owned_in, owned_out = (
        lax.all_to_all(
            expert_in.astype(jnp.bfloat16), "blk", split_axis=0, concat_axis=1, tiled=True
        ),
        lax.all_to_all(
            expert_out.astype(jnp.bfloat16), "blk", split_axis=0, concat_axis=1, tiled=True
        ),
    )
    rows_all, weight_all = (
        lax.all_gather(normed_two, "blk", axis=0, tiled=True),
        lax.all_gather(dense, "blk", axis=0, tiled=True),
    )
    owned_weight = lax.dynamic_slice_in_dim(weight_all, place * local_experts, local_experts, 1)
    owned_weight = owned_weight.reshape(cycle_size, count, local_experts)
    onehot, gated = jax.vmap(functools.partial(slot_tables, depth=CAP), in_axes=0, out_axes=1)(
        owned_weight
    )
    chosen = jnp.einsum(
        "jsct,stm->jscm",
        onehot,
        rows_all.reshape(cycle_size, count, D),
        preferred_element_type=jnp.float32,
    ).astype(jnp.bfloat16)
    run_chosen = chosen.reshape(local_experts, cycle_size * CAP, D)
    section = run_chosen
    gate_up = jnp.einsum(
        "erd,edf->erf",
        section,
        lax.all_gather(owned_in, "rep", axis=1, tiled=True),
        preferred_element_type=jnp.float32,
    )
    activated = (jax.nn.relu(gate_up[..., :FF]) * gate_up[..., FF:]).astype(jnp.bfloat16)
    section = activated
    summed = jnp.einsum(
        "erf,efd->erd",
        section,
        lax.all_gather(owned_out, "rep", axis=1, tiled=True),
        preferred_element_type=jnp.float32,
    )
    results = summed.astype(jnp.bfloat16)
    results = results.reshape(local_experts, cycle_size, CAP, D)
    summed = jnp.einsum("jsct,jscm->stm", gated, results, preferred_element_type=jnp.float32)
    expert_term = lax.psum_scatter(
        summed.reshape(count * lax.axis_size("blk"), D).astype(jnp.bfloat16),
        "blk",
        scatter_dimension=0,
        tiled=True,
    ).astype(jnp.float32)
    mixed = (hidden + expert_term).astype(jnp.bfloat16)
    return (mixed, kv_pages)


def solution(mesh):
    in_specs = (
        P(("rep", "blk"), None),
        P(("rep", "blk"), None),
        P(("rep", "blk"), None),
        P(None, ("rep", "blk"), None),
        P(None, ("rep", "blk"), None),
        P(),
        P(),
        P("rep", None),
        P("rep", None),
        P(("rep", "blk"), None),
        P(("rep", "blk"), None),
    )
    out_specs = (P(("rep", "blk"), None), P(("rep", "blk"), None, None))
    return jax.shard_map(body, mesh=mesh, in_specs=in_specs, out_specs=out_specs, check_vma=False)
```

profile of v0, /device:TPU:0, one launch (start us, length us, event | category | flops | bytes accessed | tf_op | source)
XLA Modules:
  0.0 454.3 jit_solution(6725364232836411242)
XLA Ops:
  10.6 4.2 convert_element_type.95
  14.8 6.4 %all-to-all-start = ((bf16[16,48,1536]{2,1,0:T(8,128)(2,1)}), bf16[16,48,1536]{2,1,0:T(8,128)(2,1)S(1)}, u32[]{:S(2)}, u32[]{:S(2)}) async-start(bf16[16,48,1536]{2,1,0:T(8,128)(2,1)} %convert_element_type.95), calls=%async_computation | async-start | bytes 4718592 | tf_op jit(solution)/shard_map/all_to_all | solution.py:144
  23.2 85.2 %all-gather.6.cloned.1.call-done = bf16[1536,2048]{1,0:T(8,128)(2,1)} async-done(((bf16[48,2048]{1,0:T(8,128)(2,1)}), bf16[1536,2048]{1,0:T(8,128)(2,1)}) %all-gather.6.cloned.1.call-update) | async-done | bytes 6291472 | tf_op jit(solution)/shard_map/all_gather | solution.py:88
  108.4 3.8 fusion.21
  113.8 17.2 %all_gather.22 = bf16[512,512]{1,0:T(8,128)(2,1)S(1)} all-gather(bf16[128,512]{1,0:T(8,128)(2,1)S(1)} %pad_maximum_fusion), channel_id=1, replica_groups=mesh['rep'=8,'blk'=4] {'blk'}, dimensions={0}, use_global_device_ids=true | all-gather | bytes 655360 | tf_op jit(solution)/shard_map/all_gather | solution.py:97
  132.8 2.3 copy.60
  135.1 2.0 subtract_convert_fusion
  137.1 1.8 copy.61
  138.9 1.8 copy.62
  140.8 1.8 copy.77
  142.6 1.8 fusion.23
  146.9 27.5 %all-gather.8.cloned.1.call-done = bf16[1536,1536]{1,0:T(8,128)(2,1)} async-done(((bf16[48,1536]{1,0:T(8,128)(2,1)}), bf16[1536,1536]{1,0:T(8,128)(2,1)}) %all-gather.8.cloned.1.call-update) | async-done | bytes 4718608 | tf_op jit(solution)/shard_map/all_gather | solution.py:117
  174.4 3.4 multiply_reduce_fusion
  183.1 57.3 %all_to_all.36 = bf16[16,24,1536]{2,1,0:T(8,128)(2,1)S(1)} all-to-all(bf16[16,24,1536]{2,1,0:T(8,128)(2,1)S(1)} %convert_element_type.97), channel_id=1, replica_groups=mesh['rep'=8,'blk'=4] {'blk'}, dimensions={0} | all-to-all | bytes 2359296 | tf_op jit(solution)/shard_map/all_to_all | solution.py:147
  241.7 12.0 %all_gather.24 = bf16[512,16]{0,1:T(8,128)(2,1)S(1)} all-gather(bf16[128,16]{0,1:T(8,128)(2,1)S(1)} %select_reduce_fusion), channel_id=1, replica_groups=mesh['rep'=8,'blk'=4] {'blk'}, dimensions={0}, use_global_device_ids=true | all-gather | bytes 20480 | tf_op jit(solution)/shard_map/all_gather | solution.py:153
  254.4 2.4 fusion.1
  256.8 2.0 copy.68
  258.8 80.8 %all-gather.12.cloned.1.call-done = bf16[4,1536,1536]{2,1,0:T(8,128)(2,1)} async-done(((bf16[4,192,1536]{2,1,0:T(8,128)(2,1)}), bf16[4,1536,1536]{2,1,0:T(8,128)(2,1)}) %all-gather.12.cloned.1.call-update) | async-done | bytes 18874384 | tf_op jit(solution)/shard_map/all_gather | solution.py:171
  339.6 13.8 %fusion.47 = f32[4,256,1536]{2,1,0:T(8,128)} fusion(bf16[4,256,1536]{2,1,0:T(8,128)(2,1)} %bitcast.80, bf16[4,1536,1536]{2,1,0:T(8,128)(2,1)} %all-gather.12.cloned.1.call-done), kind=kOutput, calls=%fused_computation.89 | convolution fusion | flops 4831838208 | bytes 28311552 | tf_op jit(solution)/shard_map/erd,edf->erf/dot_general | solution.py:168
  353.4 46.8 %all-gather.14.cloned.1.call-done = bf16[4,768,1536]{2,1,0:T(8,128)(2,1)} async-done(((bf16[4,96,1536]{2,1,0:T(8,128)(2,1)}), bf16[4,768,1536]{2,1,0:T(8,128)(2,1)}) %all-gather.14.cloned.1.call-update) | async-done | bytes 9437200 | tf_op jit(solution)/shard_map/all_gather | solution.py:179
  400.2 8.2 %convolution_convert_fusion = bf16[4,256,1536]{2,1,0:T(8,128)(2,1)S(1)} fusion(bf16[4,768,1536]{2,1,0:T(8,128)(2,1)} %all-gather.14.cloned.1.call-done, f32[4,256,1536]{2,1,0:T(8,128)} %fusion.47), kind=kOutput, calls=%fused_computation.2 | convolution fusion | flops 2419851264 | bytes 18874368 | tf_op jit(solution)/shard_map/erf,efd->erd/dot_general | solution.py:176
  408.4 1.8 fusion.4
  413.1 32.6 %reduce-scatter.2.cloned.1.call-done = bf16[128,1536]{1,0:T(8,128)(2,1)} async-done(((bf16[512,1536]{1,0:T(8,128)(2,1)}), bf16[128,1536]{1,0:T(8,128)(2,1)}) %reduce-scatter.2.cloned.1.call-update) | async-done | bytes 393232 | tf_op jit(solution)/shard_map/reduce_scatter | solution.py:185
  445.7 1.8 add_convert_fusion
  (89 shorter events, 20.4 us)
Async XLA Ops:
  7.2 101.2 %all-gather.6.cloned.1.call-start = ((), (), s32[]{:S(2)}) async-start(), calls=%async_computation.3 | async-start | bytes 6488064 | tf_op jit(solution)/shard_map/all_gather | solution.py:88
  8.9 165.5 %all-gather.8.cloned.1.call-start = ((), (), s32[]{:S(2)}) async-start(), calls=%async_computation.4 | async-start | bytes 4866048 | tf_op jit(solution)/shard_map/all_gather | solution.py:117
  14.8 6.5 %copy-start.12 = (s32[1,6]{1,0:T(1,128)S(1)}, s32[1,6]{1,0:T(1,128)}, u32[]{:S(2)}) copy-start(s32[1,6]{1,0:T(1,128)} %param.18) | copy-start | bytes 76
  14.8 7.4 %copy-start.2 = (bf16[128,1536]{1,0:T(8,128)(2,1)S(1)}, bf16[128,1536]{1,0:T(8,128)(2,1)}, u32[]{:S(2)}) copy-start(bf16[128,1536]{1,0:T(8,128)(2,1)} %param.11) | copy-start | bytes 1179652
  14.8 93.5 %copy-start.8 = (f32[1536]{0:T(1024)S(1)}, f32[1536]{0:T(1024)}, u32[]{:S(2)}) copy-start(f32[1536]{0:T(1024)} %param.16) | copy-start | bytes 18436
  14.8 164.7 %all-to-all-start = ((bf16[16,48,1536]{2,1,0:T(8,128)(2,1)}), bf16[16,48,1536]{2,1,0:T(8,128)(2,1)S(1)}, u32[]{:S(2)}, u32[]{:S(2)}) async-start(bf16[16,48,1536]{2,1,0:T(8,128)(2,1)} %convert_element_type.95), calls=%async_computation | async-start | bytes 4718592 | tf_op jit(solution)/shard_map/all_to_all | solution.py:144
  21.3 233.1 %all-gather.10.cloned.1.call-start = ((), (), s32[]{:S(2)}) async-start(), calls=%async_computation.5 | async-start | bytes 1966080 | tf_op jit(solution)/shard_map/all_gather | solution.py:152
  22.0 90.2 %copy-start.4 = (f32[128,64]{0,1:T(8,128)}, f32[128,64]{0,1:T(8,128)S(1)}, u32[]{:S(2)}) copy-start(f32[128,64]{0,1:T(8,128)S(1)} %get-tuple-element.10) | copy-start | bytes 98308
  22.0 90.2 %copy-start.5 = (f32[128,64]{0,1:T(8,128)}, f32[128,64]{0,1:T(8,128)S(1)}, u32[]{:S(2)}) copy-start(f32[128,64]{0,1:T(8,128)S(1)} %get-tuple-element.11) | copy-start | bytes 98308
  142.6 1.8 copy-start.7
  144.4 1.4 copy-start.6
  174.4 4.2 copy-start.9
  177.8 0.9 copy-start
  179.5 160.1 %all-gather.12.cloned.1.call-start = ((), (), s32[]{:S(2)}) async-start(), calls=%async_computation.6 | async-start | bytes 21233664 | tf_op jit(solution)/shard_map/all_gather | solution.py:171
  181.3 1.7 copy-start.3
  181.3 218.9 %all-gather.14.cloned.1.call-start = ((), (), s32[]{:S(2)}) async-start(), calls=%async_computation.7 | async-start | bytes 10616832 | tf_op jit(solution)/shard_map/all_gather | solution.py:179
  183.1 58.6 %copy-start.11 = (bf16[128,4]{0,1:T(4,128)(2,1)S(1)}, bf16[128,4]{0,1:T(4,128)(2,1)}, u32[]{:S(2)}) copy-start(bf16[128,4]{0,1:T(4,128)(2,1)} %param.21) | copy-start | bytes 3076
  183.1 58.6 %copy-start.10 = (s32[128,4]{0,1:T(4,128)S(1)}, s32[128,4]{0,1:T(4,128)}, u32[]{:S(2)}) copy-start(s32[128,4]{0,1:T(4,128)} %param.20) | copy-start | bytes 6148
  241.6 204.0 %reduce-scatter.2.cloned.1.call-start = ((), (), s32[]{:S(2)}) async-start(), calls=%async_computation.8 | async-start | bytes 1966080 | tf_op jit(solution)/shard_map/reduce_scatter | solution.py:185
  408.4 1.8 copy-start.13
  410.2 35.5 %copy-start.1 = (f32[128,1536]{1,0:T(8,128)S(1)}, f32[128,1536]{1,0:T(8,128)}, u32[]{:S(2)}) copy-start(f32[128,1536]{1,0:T(8,128)} %copy-done) | copy-start | bytes 2359300
Sparse Core Ops, SparseCore 0:
  11.4 96.8 all-gather.5
  111.2 63.1 all-gather.7
  179.7 61.0 all-gather.9
  242.5 97.1 all-gather.11
  341.4 58.8 all-gather.13
  410.4 35.2 reduce-scatter.1
where the time goes:
time: 455 us; the launch traced here: 454 us
  waiting for transfers between devices  273 us (60%)
  blocking collectives  86.6 us (19%)
  matrix products  36.2 us (8%)
  local copies, waits for them, and re-layouts  20.1 us (4%)
  other arithmetic  16.7 us (4%)
  between operations  15.1 us (3%)
  starting transfers between devices  6.66 us (1%)
    all_gather x1, waiting for transfers between devices, body(): lax.all_gather(attn_in.astype(jnp.bfloat16), ('rep', 'blk'), axis=0, tile...  85.2 us
    all_gather x1, waiting for transfers between devices, body(): lax.all_gather(owned_in, 'rep', axis=1, tiled=True)  80.8 us
    all_to_all x1, blocking collectives, body(): lax.all_to_all(expert_out.astype(jnp.bfloat16), 'blk', split_axis=0, conc...  57.3 us
    all_gather x1, waiting for transfers between devices, body(): lax.all_gather(owned_out, 'rep', axis=1, tiled=True)  46.8 us
    reduce_scatter x1, waiting for transfers between devices, body(): lax.psum_scatter(summed.reshape(count * lax.axis_size('blk'), D).astype(j...  32.6 us
    all_gather x1, waiting for transfers between devices, body(): lax.all_gather(attn_out.astype(jnp.bfloat16), ('rep', 'blk'), axis=0, til...  27.5 us
    all_gather x1, blocking collectives, body(): cache_all = lax.all_gather(cache_here, 'blk', axis=0, tiled=True)  17.2 us
    dot_general x1, matrix products, body(): jnp.einsum('erd,edf->erf', section, lax.all_gather(owned_in, 'rep', axis=...  13.8 us
  transfers between devices with their start and end apart: 7, of which 5 were waited for; matrix products, arithmetic and copies ran while one was open for 13% of the time, Pallas kernels for 0%

commit v1 on v0

v1 whole, which is shorter than its diff:
```python
import functools
import math

import jax
import jax.numpy as jnp
from jax import lax
from jax.experimental import pallas as pl
from jax.experimental.pallas import tpu as pltpu
from jax.sharding import PartitionSpec as P

D = 1536
FF = 768
QH = 12
KVH = 2
HD = 128
E = 16
PAGE = 128
QW = 1536
QKV = 2048
HALF = QKV // 2
COLS = 256
CHUNKS = 4
BF = jnp.bfloat16
F32 = jnp.float32
VMEM = 56 * 1024 * 1024


def rms_scale(values, gain):
    values = values.astype(F32)
    mean_sq = jnp.mean(values * values, axis=-1, keepdims=True)
    return values * lax.rsqrt(mean_sq + 1e-06) * gain


def rotation(position):
    half = HD // 2
    steps_all = jnp.arange(half, dtype=F32)
    frequency = jnp.exp(steps_all * (-2.0 * math.log(10000.0) / HD))
    angle = position[:, None] * frequency[None, :]
    cosine = jnp.cos(angle)
    sine = jnp.sin(angle)
    return (
        jnp.concatenate([cosine, cosine], axis=1),
        jnp.concatenate([-sine, sine], axis=1),
    )


def segment_begin(lengths, index):
    starts = jnp.cumsum(lengths) - lengths
    member = index[:, None] >= starts[None, :]
    return jnp.max(jnp.where(member, starts[None, :], 0), axis=1)


def project_kernel(pieces, rows, *refs):
    x_ref, cos_ref, sin_ref = refs[:3]
    weights = refs[3 : 3 + 2 * pieces]
    out_ref, held = refs[3 + 2 * pieces :]
    step = pl.program_id(0)

    @pl.when(step < HALF // COLS)
    def _():
        for p in range(pieces):
            held[p * rows : (p + 1) * rows, :] = weights[p][...]

    @pl.when(step >= HALF // COLS)
    def _():
        for p in range(pieces):
            held[p * rows : (p + 1) * rows, :] = weights[pieces + p][...]

    result = jnp.dot(x_ref[...], held[...], preferred_element_type=F32)

    @pl.when(step < (QW + KVH * HD) // COLS)
    def _():
        for h in range(COLS // HD):
            value = result[:, h * HD : (h + 1) * HD]
            turned = value * cos_ref[...] + pltpu.roll(value, HD // 2, 1) * sin_ref[...]
            out_ref[:, h * HD : (h + 1) * HD] = turned.astype(BF)

    @pl.when(step >= (QW + KVH * HD) // COLS)
    def _():
        out_ref[...] = result.astype(BF)


def project(x, cosine, sine, first, second):
    count = x.shape[0]
    pieces, rows = len(first), first[0].shape[0]
    steps = HALF // COLS
    whole = lambda j: (0, 0)
    return pl.pallas_call(
        functools.partial(project_kernel, pieces, rows),
        grid=(2 * steps,),
        in_specs=[
            pl.BlockSpec((count, D), whole),
            pl.BlockSpec((count, HD), whole),
            pl.BlockSpec((count, HD), whole),
        ]
        + [pl.BlockSpec((rows, COLS), lambda j: (0, jnp.minimum(j, steps - 1)))] * pieces
        + [pl.BlockSpec((rows, COLS), lambda j: (0, jnp.maximum(j - steps, 0)))] * pieces,
        out_specs=pl.BlockSpec((count, COLS), lambda j: (0, j)),
        out_shape=jax.ShapeDtypeStruct((count, QKV), BF),
        scratch_shapes=[pltpu.VMEM((D, COLS), BF)],
        compiler_params=pltpu.CompilerParams(vmem_limit_bytes=VMEM),
        cost_estimate=pl.CostEstimate(
            flops=2 * count * D * QKV, bytes_accessed=2 * D * QKV + 4 * count * D, transcendentals=0
        ),
        name="project",
    )(x, cosine, sine, *first, *second)


def attend_kernel(q_ref, k_ref, v_ref, begin_ref, index_ref, across_ref, out_ref):
    scores = lax.dot_general(
        q_ref[...], k_ref[...], (((1,), (1,)), ((), ())), preferred_element_type=F32
    ) * (1.0 / math.sqrt(HD))
    across = across_ref[...]
    allowed = (across >= begin_ref[...]) & (across <= index_ref[...])
    scores = jnp.where(allowed, scores, -1e30)
    highest = jnp.max(scores, axis=1, keepdims=True)
    weights = jnp.exp(scores - highest)
    total = jnp.sum(weights, axis=1, keepdims=True)
    probs = (weights / total).astype(BF)
    out_ref[...] = jnp.dot(probs, v_ref[...], preferred_element_type=F32).astype(BF)


def attend(qkv, begin, index):
    count = qkv.shape[0]
    per = QH // KVH
    column = pl.BlockSpec((count, 1), lambda h: (0, 0))
    return pl.pallas_call(
        attend_kernel,
        grid=(QH,),
        in_specs=[
            pl.BlockSpec((count, HD), lambda h: (0, h)),
            pl.BlockSpec((count, HD), lambda h: (0, QH + h // per)),
            pl.BlockSpec((count, HD), lambda h: (0, QH + KVH + h // per)),
            column,
            column,
            pl.BlockSpec((1, count), lambda h: (0, 0)),
        ],
        out_specs=pl.BlockSpec((count, HD), lambda h: (0, h)),
        out_shape=jax.ShapeDtypeStruct((count, QW), BF),
        compiler_params=pltpu.CompilerParams(vmem_limit_bytes=VMEM),
        cost_estimate=pl.CostEstimate(
            flops=4 * QH * count * count * HD,
            bytes_accessed=2 * count * (QKV + QW),
            transcendentals=QH * count * count,
        ),
        name="attend",
    )(qkv, qkv, qkv, begin[:, None], index[:, None], index[None, :])


def mix_kernel(pieces, rows, *refs):
    x_ref, tokens_ref = refs[:2]
    weights = refs[2 : 2 + pieces]
    out_ref, held = refs[2 + pieces :]
    for p in range(pieces):
        held[p * rows : (p + 1) * rows, :] = weights[p][...]
    out_ref[...] = tokens_ref[...].astype(F32) + jnp.dot(
        x_ref[...], held[...], preferred_element_type=F32
    )


def mix(x, tokens, weights):
    count = x.shape[0]
    pieces, rows = len(weights), weights[0].shape[0]
    return pl.pallas_call(
        functools.partial(mix_kernel, pieces, rows),
        grid=(D // COLS,),
        in_specs=[
            pl.BlockSpec((count, QW), lambda j: (0, 0)),
            pl.BlockSpec((count, COLS), lambda j: (0, j)),
        ]
        + [pl.BlockSpec((rows, COLS), lambda j: (0, j))] * pieces,
        out_specs=pl.BlockSpec((count, COLS), lambda j: (0, j)),
        out_shape=jax.ShapeDtypeStruct((count, D), F32),
        scratch_shapes=[pltpu.VMEM((QW, COLS), BF)],
        compiler_params=pltpu.CompilerParams(vmem_limit_bytes=VMEM),
        cost_estimate=pl.CostEstimate(
            flops=2 * count * D * QW, bytes_accessed=2 * D * QW + 8 * count * D, transcendentals=0
        ),
        name="mix",
    )(x, tokens, *weights)


def gate_up_kernel(pieces, rows, width, *refs):
    x_ref, gate_ref = refs[:2]
    weights = refs[2 : 2 + pieces]
    out_ref, held = refs[2 + pieces :]
    for p in range(pieces):
        held[p * rows : (p + 1) * rows, :] = weights[p][0]
    result = jnp.dot(x_ref[...], held[...], preferred_element_type=F32)
    activated = jnp.maximum(result[:, :width], 0.0) * result[:, width:]
    out_ref[0] = (activated * gate_ref[0]).astype(BF)


def gate_up(x, gate, weights):
    count = x.shape[0]
    pieces = len(weights)
    experts, rows, wide = weights[0].shape
    return pl.pallas_call(
        functools.partial(gate_up_kernel, pieces, rows, wide // 2),
        grid=(experts,),
        in_specs=[
            pl.BlockSpec((count, D), lambda e: (0, 0)),
            pl.BlockSpec((1, count, 1), lambda e: (e, 0, 0)),
        ]
        + [pl.BlockSpec((1, rows, wide), lambda e: (e, 0, 0))] * pieces,
        out_specs=pl.BlockSpec((1, count, wide // 2), lambda e: (e, 0, 0)),
        out_shape=jax.ShapeDtypeStruct((experts, count, wide // 2), BF),
        scratch_shapes=[pltpu.VMEM((D, wide), BF)],
        compiler_params=pltpu.CompilerParams(vmem_limit_bytes=VMEM),
        cost_estimate=pl.CostEstimate(
            flops=2 * experts * count * D * wide,
            bytes_accessed=2 * D * (experts * wide + count),
            transcendentals=0,
        ),
        name="gate_up",
    )(x, gate, *weights)


def along_blk(value, step):
    size = lax.axis_size("blk")
    return lax.ppermute(value, "blk", [(i, (i + step) % size) for i in range(size)])


def across_rep(value, mask):
    return lax.ppermute(value, "rep", [(i, i ^ mask) for i in range(lax.axis_size("rep"))])


def chip_gather(value, turn):
    bits = (lax.axis_size("rep") // 2).bit_length() - 1
    held = {0: value}
    for bit in [(i + turn) % bits for i in range(bits)]:
        held.update({k ^ (1 << bit): across_rep(v, 2 << bit) for k, v in sorted(held.items())})
    return [held[k] for k in sorted(held)]


def order_matrix(chip, core, place, rows, order):
    chips, cycle_size = lax.axis_size("rep") // 2, lax.axis_size("blk")
    sizes = {"chip": chips, "core": 2, "turn": cycle_size}
    spot = jnp.arange(D, dtype=jnp.int32)
    inner, rest, part = spot % rows, spot // rows, {}
    for name in reversed(order):
        part[name], rest = rest % sizes[name], rest // sizes[name]
    rep = (chip ^ part["chip"]) * 2 + (core ^ part["core"])
    blk = (place - part["turn"] + cycle_size) % cycle_size
    source = (rep * cycle_size + blk) * rows + inner
    return (spot[:, None] == source[None, :]).astype(BF)


def body(
    tokens,
    attn_in,
    attn_out,
    expert_in,
    expert_out,
    attn_gain,
    moe_gain,
    lengths,
    page_table,
    routes,
    gates,
):
    count = tokens.shape[0]
    reps, cycle_size = lax.axis_size("rep"), lax.axis_size("blk")
    rep, place = lax.axis_index("rep"), lax.axis_index("blk")
    chip, core = rep // 2, rep % 2
    group_rows = count * cycle_size
    shifts = range(1, cycle_size)
    half_experts = E // 2
    quarter = FF // cycle_size
    rows_in, rows_out = expert_in.shape[1], expert_out.shape[1]

    expert_ids = jnp.arange(E, dtype=jnp.int32)
    dense = jnp.sum(
        jnp.where(
            routes[:, :, None] == expert_ids[None, None, :],
            gates.astype(F32)[:, :, None],
            F32(0.0),
        ),
        axis=1,
    ).astype(BF)

    qkv_here, mix_here = attn_in.astype(BF), attn_out.astype(BF)
    qkv_line = jnp.concatenate([qkv_here] + [along_blk(qkv_here, s) for s in shifts], axis=0)
    mix_line = jnp.concatenate([mix_here] + [along_blk(mix_here, s) for s in shifts], axis=0)
    first_own = chip_gather(qkv_line[:, :HALF], 0)
    second_own = chip_gather(qkv_line[:, HALF:], 1)
    mix_own = chip_gather(mix_line, 1)
    first = first_own + [across_rep(v, 1) for v in first_own]
    second = second_own + [across_rep(v, 1) for v in second_own]
    mixing = mix_own + [across_rep(v, 1) for v in mix_own]

    sent = jnp.concatenate([tokens, jnp.pad(dense, ((0, 0), (0, 128 - E)))], axis=1)
    line = jnp.concatenate([sent] + [along_blk(sent, s) for s in shifts], axis=0)
    group, group_gates = line[:, :D], line[:, D : D + E]

    def split_cores(value):
        mine = lax.dynamic_slice_in_dim(value, core * half_experts, half_experts, 0)
        other = lax.dynamic_slice_in_dim(value, (1 - core) * half_experts, half_experts, 0)
        return jnp.stack([mine, across_rep(other, 1)], axis=1)

    down = split_cores(expert_out.astype(BF)).reshape(half_experts, 2 * rows_out, D)
    down_parts = [
        chip_gather(down[: half_experts // 2], 0),
        chip_gather(down[half_experts // 2 :], 1),
    ]
    down_all = jnp.concatenate(
        [
            jnp.stack([p.reshape(p.shape[0], 2, rows_out, D) for p in part], axis=1).reshape(
                -1, reps, rows_out, D
            )
            for part in down_parts
        ],
        axis=0,
    )
    down_all = jnp.take(down_all, jnp.arange(reps, dtype=jnp.int32) ^ rep, axis=1)
    down_all = down_all.reshape(half_experts * quarter, D)

    spot = jnp.arange(2 * FF, dtype=jnp.int32)
    inner = spot % rows_out
    from_rep = (spot // rows_out) % reps
    which = (spot // quarter) % 2
    from_blk = spot // (2 * quarter)
    column = which * FF + (from_rep * cycle_size + from_blk) * rows_out + inner
    shuffle = (spot[:, None] == column[None, :]).astype(BF)
    ordered = jnp.dot(
        expert_in.astype(BF).reshape(E * rows_in, 2 * FF), shuffle, preferred_element_type=F32
    )
    pairs = split_cores(ordered.astype(BF).reshape(E, rows_in, 2 * FF))
    per_chunk = half_experts // CHUNKS
    up_parts = []
    for n in range(CHUNKS):
        chunk = pairs[n * per_chunk : (n + 1) * per_chunk]
        cut = lambda s: lax.dynamic_slice_in_dim(
            chunk, ((place + s) % cycle_size) * 2 * quarter, 2 * quarter, 3
        )
        pieces = [cut(0)] + [along_blk(cut(s), s) for s in shifts]
        lined = jnp.stack(pieces, axis=1).reshape(per_chunk, cycle_size * 2 * rows_in, 2 * quarter)
        up_parts.append(chip_gather(lined, n))

    index = (
        ((place - jnp.arange(cycle_size, dtype=jnp.int32) + cycle_size) % cycle_size)[:, None] * count
        + jnp.arange(count, dtype=jnp.int32)[None, :]
    ).reshape(group_rows)
    begin = segment_begin(lengths[0], index)
    cosine, sine = rotation((index - begin).astype(F32))
    normed = rms_scale(group, attn_gain).astype(BF)
    order = order_matrix(chip, core, place, rows_in, ("core", "chip", "turn"))
    normed = jnp.dot(normed, order, preferred_element_type=F32).astype(BF)
    qkv = project(normed, cosine, sine, first, second)
    attended = attend(qkv, begin, index)
    attended = jnp.dot(attended, order, preferred_element_type=F32).astype(BF)
    hidden = mix(attended, group, mixing)

    page_count = count // PAGE
    targets = place * page_count + jnp.arange(page_count, dtype=jnp.int32)
    table = page_table[0]
    logical = jnp.sum(
        jnp.where(
            table[None, :] == targets[:, None],
            jnp.arange(table.shape[0], dtype=jnp.int32)[None, :],
            0,
        ),
        axis=1,
    )
    turned = (place - logical // page_count + cycle_size) % cycle_size
    first_row = turned * count + (logical % page_count) * PAGE
    cache = qkv[:, QW:]
    kv_pages = jnp.stack(
        [lax.dynamic_slice_in_dim(cache, first_row[i], PAGE, 0) for i in range(page_count)]
    )

    normed_two = rms_scale(hidden, moe_gain).astype(BF)
    both = jnp.concatenate([normed_two, across_rep(normed_two, 1)], axis=0)
    both_gates = jnp.concatenate([group_gates, across_rep(group_gates, 1)], axis=0)
    my_gates = lax.dynamic_slice_in_dim(both_gates, core * half_experts, half_experts, 1)
    my_gates = my_gates.astype(F32).T[:, :, None]
    order_two = order_matrix(chip, core, place, rows_in, ("chip", "turn", "core"))
    both = jnp.dot(both, order_two, preferred_element_type=F32).astype(BF)
    activated = jnp.concatenate(
        [
            gate_up(both, my_gates[n * per_chunk : (n + 1) * per_chunk], up_parts[n])
            for n in range(CHUNKS)
        ],
        axis=0,
    )
    activated = activated.transpose(1, 0, 2).reshape(2 * group_rows, half_experts * quarter)
    other = jnp.dot(activated[group_rows:], down_all, preferred_element_type=F32).astype(BF)
    mine = jnp.dot(activated[:group_rows], down_all, preferred_element_type=F32)
    summed = mine + across_rep(other, 1).astype(F32)
    total = hidden[:count] + summed[:count]
    for s in shifts:
        part = summed[s * count : (s + 1) * count].astype(BF)
        total = total + along_blk(part, -s).astype(F32)
    return (total.astype(BF), kv_pages)


def solution(mesh):
    in_specs = (
        P(("rep", "blk"), None),
        P(("rep", "blk"), None),
        P(("rep", "blk"), None),
        P(None, ("rep", "blk"), None),
        P(None, ("rep", "blk"), None),
        P(),
        P(),
        P("rep", None),
        P("rep", None),
        P(("rep", "blk"), None),
        P(("rep", "blk"), None),
    )
    out_specs = (P(("rep", "blk"), None), P(("rep", "blk"), None, None))
    return jax.shard_map(body, mesh=mesh, in_specs=in_specs, out_specs=out_specs, check_vma=False)
```

time: 455 us -> 415 us (0.912); the launches traced: 454 us -> 407 us
  waiting for transfers between devices: 273 us -> 138 us
  blocking collectives: 86.6 us -> 0 us
  starting transfers between devices: 6.66 us -> 80.1 us
  Pallas kernels: 0 us -> 64.6 us
  local copies, waits for them, and re-layouts: 20.1 us -> 45.5 us
  other arithmetic: 16.7 us -> 39.4 us
  between operations: 15.1 us -> 1.98 us
    all_gather x5 -> x0, waiting for transfers between devices: 240 us -> none  [the longest x1 85.2 us: body(): lax.all_gather(attn_in.astype(jnp.bfloat16), ('rep', 'blk'), axis=0, tile...]
    ppermute x0 -> x68, waiting for transfers between devices: none -> 138 us  [the longest x44 68.9 us: across_rep(): lax.ppermute(value, 'rep', [(i, i ^ mask) for i in range(lax.axis_size('r...]
    ppermute x0 -> x68, starting transfers between devices: none -> 80.1 us  [the longest x24 41 us: along_blk(): lax.ppermute(value, 'blk', [(i, (i + step) % size) for i in range(size)])]
    pallas_call x0 -> x7, Pallas kernels: none -> 64.6 us  [the longest x4 29.5 us: gate_up(): pl.pallas_call(functools.partial(gate_up_kernel, pieces, rows, wide // 2)...]
    all_to_all x1 -> x0, blocking collectives: 57.3 us -> none  [body(): lax.all_to_all(expert_out.astype(jnp.bfloat16), 'blk', split_axis=0, conc...]
    reduce_scatter x1 -> x0, waiting for transfers between devices: 32.6 us -> none  [body(): lax.psum_scatter(summed.reshape(count * lax.axis_size('blk'), D).astype(j...]
    all_gather x2 -> x0, blocking collectives: 29.2 us -> none  [the longest x1 17.2 us: body(): cache_all = lax.all_gather(cache_here, 'blk', axis=0, tiled=True)]
    slice x5 -> x15, local copies, waits for them, and re-layouts: 4.08 us -> 19.9 us  [the longest x2 6.25 us: body(): activated[group_rows:]]
  transfers between devices with their start and end apart: 7 -> 68, of which waited for: 5 -> 21; matrix products, arithmetic and copies ran while one was open for 13% -> 22% of each run, Pallas kernels for 0% -> 14%
where the time goes in v1:
time: 415 us; the launch traced here: 407 us
  waiting for transfers between devices  138 us (33%)
  starting transfers between devices  80.1 us (19%)
  Pallas kernels  64.6 us (16%)
  local copies, waits for them, and re-layouts  45.5 us (11%)
  other arithmetic  39.4 us (9%)
  matrix products  37.7 us (9%)
    ppermute x44, waiting for transfers between devices, across_rep(): lax.ppermute(value, 'rep', [(i, i ^ mask) for i in range(lax.axis_size('r...  68.9 us
    ppermute x24, waiting for transfers between devices, along_blk(): lax.ppermute(value, 'blk', [(i, (i + step) % size) for i in range(size)])  68.8 us
    ppermute x24, starting transfers between devices, along_blk(): lax.ppermute(value, 'blk', [(i, (i + step) % size) for i in range(size)])  41 us
    ppermute x44, starting transfers between devices, across_rep(): lax.ppermute(value, 'rep', [(i, i ^ mask) for i in range(lax.axis_size('r...  39.1 us
    pallas_call x4, Pallas kernels, gate_up(): pl.pallas_call(functools.partial(gate_up_kernel, pieces, rows, wide // 2)...  29.5 us
    pallas_call x1, Pallas kernels, attend(): pl.pallas_call(attend_kernel, grid=(QH,), in_specs=[pl.BlockSpec((count,...  15.8 us
    pallas_call x1, Pallas kernels, project(): pl.pallas_call(functools.partial(project_kernel, pieces, rows), grid=(2 *...  11 us
    dot_general x1, matrix products, body(): both = jnp.dot(both, order_two, preferred_element_type=F32).astype(BF)  8.46 us
  transfers between devices with their start and end apart: 68, of which 21 were waited for; matrix products, arithmetic and copies ran while one was open for 22% of the time, Pallas kernels for 14%

profile of v1, /device:TPU:0, one launch (start us, length us, event | category | flops | bytes accessed | tf_op | source)
XLA Modules:
  0.0 407.0 jit_solution(4172877459433756774)
XLA Ops:
  41.9 8.4 %collective-permute-done.21 = bf16[48,1536]{1,0:T(8,128)(2,1)} collective-permute-done((bf16[48,1536]{1,0:T(8,128)(2,1)S(1)}, bf16[48,1536]{1,0:T(8,128)(2,1)}, u32[]{:S(2)}, u32[]{:S(2)}) %collective-permute-start.21) | collective-permute-done | bytes 147488 | tf_op jit(solution)/shard_map/ppermute | solution.py:221
  50.3 9.3 %collective-permute-start.3 = (bf16[48,2048]{1,0:T(8,128)(2,1)}, bf16[48,2048]{1,0:T(8,128)(2,1)S(1)}, u32[]{:S(2)}, u32[]{:S(2)}) collective-permute-start(bf16[48,2048]{1,0:T(8,128)(2,1)} %convert_element_type.82), channel_id=1, source_target_pairs={{0,1},{1,2},{2,3},{3,0},{4,5},{5,6},{6,7},{7,4},{8,9},{9,10},{10,1... | collective-permute-start | bytes 589832 | tf_op jit(solution)/shard_map/ppermute | solution.py:221
  63.8 11.2 %collective-permute-done.4 = bf16[48,2048]{1,0:T(8,128)(2,1)S(1)} collective-permute-done((bf16[48,2048]{1,0:T(8,128)(2,1)}, bf16[48,2048]{1,0:T(8,128)(2,1)S(1)}, u32[]{:S(2)}, u32[]{:S(2)}) %collective-permute-start.4) | collective-permute-done | bytes 196640 | tf_op jit(solution)/shard_map/ppermute | solution.py:221
  103.6 9.7 %collective-permute-done.14.refs_13_ = bf16[192,1024]{1,0:T(8,128)(2,1)} collective-permute-done((bf16[192,1024]{1,0:T(8,128)(2,1)}, bf16[192,1024]{1,0:T(8,128)(2,1)}, u32[]{:S(2)}, u32[]{:S(2)}) %collective-permute-start.14) | collective-permute-done | bytes 393248 | tf_op jit(solution)/shard_map/ppermute | solution.py:225
  117.1 6.2 %collective-permute-done.8.refs_6_ = bf16[192,1024]{1,0:T(8,128)(2,1)S(1)} collective-permute-done((bf16[192,1024]{1,0:T(8,128)(2,1)}, bf16[192,1024]{1,0:T(8,128)(2,1)S(1)}, u32[]{:S(2)}, u32[]{:S(2)}) %collective-permute-start.8) | collective-permute-done | bytes 393248 | tf_op jit(solution)/shard_map/ppermute | solution.py:225
  132.1 6.1 %collective-permute-done.52 = bf16[2,2,48,384]{3,2,1,0:T(8,128)(2,1)S(1)} collective-permute-done((bf16[2,2,48,384]{3,2,1,0:T(8,128)(2,1)S(1)}, bf16[2,2,48,384]{3,2,1,0:T(8,128)(2,1)S(1)}, u32[]{:S(2)}, u32[]{:S(2)}) %collective-permute-start.52) | collective-permute-done | bytes 147488 | tf_op jit(solution)/shard_map/ppermute | solution.py:221
  148.3 8.9 %collective-permute-done.46 = bf16[2,2,48,384]{3,2,1,0:T(8,128)(2,1)S(1)} collective-permute-done((bf16[2,2,48,384]{3,2,1,0:T(8,128)(2,1)}, bf16[2,2,48,384]{3,2,1,0:T(8,128)(2,1)S(1)}, u32[]{:S(2)}, u32[]{:S(2)}) %collective-permute-start.46) | collective-permute-done | bytes 147488 | tf_op jit(solution)/shard_map/ppermute | solution.py:221
  162.1 7.8 %collective-permute-done.40 = bf16[2,2,48,384]{3,2,1,0:T(8,128)(2,1)S(1)} collective-permute-done((bf16[2,2,48,384]{3,2,1,0:T(8,128)(2,1)S(1)}, bf16[2,2,48,384]{3,2,1,0:T(8,128)(2,1)S(1)}, u32[]{:S(2)}, u32[]{:S(2)}) %collective-permute-start.40) | collective-permute-done | bytes 147488 | tf_op jit(solution)/shard_map/ppermute | solution.py:221
  184.3 11.0 %project.1.q_ref.k_ref.v_ref = bf16[512,2048]{1,0:T(8,128)(2,1)} custom-call(bf16[512,1536]{1,0:T(8,128)(2,1)} %fusion.16.refs_0_, f32[512,128]{1,0:T(8,128)} %get-tuple-element.45.refs_1_, f32[512,128]{1,0:T(8,128)} %get-tuple-element.46.refs_2_, bf16[192,1024]{1,0:T(8,128)(2,1)} %copy-done.16, bf16[192,1024]{1,0:T(8,128)(2,1)} %copy-done.32, ...), custom_call_target="tpu_custom_call" | custom-call | flops 3221225472 | bytes 9437184 | tf_op jit(solution)/shard_map/project/pallas_call | solution.py:88
  199.9 15.8 %attend.1 = bf16[512,1536]{1,0:T(8,128)(2,1)} custom-call(bf16[512,2048]{1,0:T(8,128)(2,1)} %project.1.q_ref.k_ref.v_ref, bf16[512,2048]{1,0:T(8,128)(2,1)} %project.1.q_ref.k_ref.v_ref, bf16[512,2048]{1,0:T(8,128)(2,1)} %project.1.q_ref.k_ref.v_ref, s32[512,1]{1,0:T(8,128)} %copy.141.begin_ref, s32[512,1]{1,0:T(8,128)} %copy.142.index_ref, s32[1,512]{1,0:T(1,128)} %bitcast.129), custom_call_target="tpu_custom_call" | custom-call | flops 1610612736 | bytes 3670016 | tf_op jit(solution)/shard_map/attend/pallas_call | solution.py:127
  227.3 8.3 %mix.1 = f32[512,1536]{1,0:T(8,128)} custom-call(bf16[512,1536]{1,0:T(8,128)(2,1)} %fusion.17.refs_0_, bf16[512,1536]{1,0:T(8,128)(2,1)} %slice.125.refs_1_, bf16[192,1536]{1,0:T(8,128)(2,1)} %pad_maximum_fusion.6.refs_2_, bf16[192,1536]{1,0:T(8,128)(2,1)} %copy-done.9, bf16[192,1536]{1,0:T(8,128)(2,1)} %collective-permute-done.24.refs_4_, ...), custom_call_target="tpu_custom_call" | custom-call | flops 2415919104 | bytes 11010048 | tf_op jit(solution)/shard_map/mix/pallas_call | solution.py:164
  241.4 8.5 %collective-permute-done.63 = bf16[4,48,1536]{2,1,0:T(8,128)(2,1)S(1)} collective-permute-done((bf16[4,48,1536]{2,1,0:T(8,128)(2,1)S(1)}, bf16[4,48,1536]{2,1,0:T(8,128)(2,1)S(1)}, u32[]{:S(2)}, u32[]{:S(2)}) %collective-permute-start.63) | collective-permute-done | bytes 589856 | tf_op jit(solution)/shard_map/ppermute | solution.py:225
  257.2 5.5 %gather_fusion = bf16[8,8,24,1536]{3,2,1,0:T(8,128)(2,1)} fusion(bf16[8,8,24,1536]{3,2,1,0:T(8,128)(2,1)} %pad_maximum_fusion, s32[1024]{0:T(1024)} %pad_clamp_fusion), kind=kCustom, calls=%fused_computation | custom fusion | bytes 9437216 | tf_op jit(solution)/shard_map/jit(_take)/gather | solution.py:315
  277.4 11.6 %collective-permute-done.43.refs_4_ = bf16[2,384,384]{2,1,0:T(8,128)(2,1)S(1)} collective-permute-done((bf16[2,384,384]{2,1,0:T(8,128)(2,1)}, bf16[2,384,384]{2,1,0:T(8,128)(2,1)S(1)}, u32[]{:S(2)}, u32[]{:S(2)}) %collective-permute-start.43) | collective-permute-done | bytes 589856 | tf_op jit(solution)/shard_map/ppermute | solution.py:225
  290.9 8.5 %fusion.8.refs_0_ = bf16[1024,1536]{1,0:T(8,128)(2,1)} fusion(s32[1536]{0:T(1024)S(1)} %copy-done.21, bf16[512,1536]{1,0:T(8,128)(2,1)} %collective-permute-done.30, bf16[512,1536]{1,0:T(8,128)(2,1)} %multiply_convert_fusion), kind=kOutput, calls=%fused_computation.17 | convolution fusion | flops 4842061824 | bytes 6297600 | tf_op jit(solution)/shard_map/dot_general | solution.py:378
  302.1 11.0 %collective-permute-done.56.refs_5_ = bf16[2,384,384]{2,1,0:T(8,128)(2,1)S(1)} collective-permute-done((bf16[2,384,384]{2,1,0:T(8,128)(2,1)}, bf16[2,384,384]{2,1,0:T(8,128)(2,1)S(1)}, u32[]{:S(2)}, u32[]{:S(2)}) %collective-permute-start.56) | collective-permute-done | bytes 589856 | tf_op jit(solution)/shard_map/ppermute | solution.py:225
  314.6 7.3 %gate_up.7 = bf16[2,1024,192]{2,1,0:T(8,128)(2,1)} custom-call(bf16[1024,1536]{1,0:T(8,128)(2,1)} %fusion.8.refs_0_, f32[2,1024,1]{2,1,0:T(8,128)} %copy.153.refs_1_, bf16[2,384,384]{2,1,0:T(8,128)(2,1)} %bitcast.37.refs_2_, bf16[2,384,384]{2,1,0:T(8,128)(2,1)} %collective-permute-done.54.refs_3_, bf16[2,384,384]{2,1,0:T(8,128)(2,1)} %collective-permute-done.55.refs_4_, ...), custom_call_target="tpu_custom_call" | custom-call | flops 2415919104 | bytes 5505024 | tf_op jit(solution)/shard_map/gate_up/pallas_call | solution.py:198
  322.8 7.3 %gate_up.6 = bf16[2,1024,192]{2,1,0:T(8,128)(2,1)} custom-call(bf16[1024,1536]{1,0:T(8,128)(2,1)} %fusion.8.refs_0_, f32[2,1024,1]{2,1,0:T(8,128)} %copy.150.refs_1_, bf16[2,384,384]{2,1,0:T(8,128)(2,1)} %bitcast.29.refs_2_, bf16[2,384,384]{2,1,0:T(8,128)(2,1)} %collective-permute-done.48.refs_3_, bf16[2,384,384]{2,1,0:T(8,128)(2,1)} %collective-permute-done.49.refs_4_, ...), custom_call_target="tpu_custom_call" | custom-call | flops 2415919104 | bytes 5505024 | tf_op jit(solution)/shard_map/gate_up/pallas_call | solution.py:198
  331.8 7.3 %gate_up.5 = bf16[2,1024,192]{2,1,0:T(8,128)(2,1)} custom-call(bf16[1024,1536]{1,0:T(8,128)(2,1)} %fusion.8.refs_0_, f32[2,1024,1]{2,1,0:T(8,128)} %copy.148.refs_1_, bf16[2,384,384]{2,1,0:T(8,128)(2,1)} %bitcast.114, bf16[2,384,384]{2,1,0:T(8,128)(2,1)} %copy-done.28, bf16[2,384,384]{2,1,0:T(8,128)(2,1)} %copy-done.27, bf16[2,384,384]{2,1,0:T(8,128)(2,1)} %copy-done.29), custom_call_target="tpu_custom_call" | custom-call | flops 2415919104 | bytes 5505024 | tf_op jit(solution)/shard_map/gate_up/pallas_call | solution.py:198
  339.2 7.5 %gate_up.4 = bf16[2,1024,192]{2,1,0:T(8,128)(2,1)} custom-call(bf16[1024,1536]{1,0:T(8,128)(2,1)} %fusion.8.refs_0_, f32[2,1024,1]{2,1,0:T(8,128)} %copy.146.refs_1_, bf16[2,384,384]{2,1,0:T(8,128)(2,1)} %bitcast.110, bf16[2,384,384]{2,1,0:T(8,128)(2,1)} %collective-permute-done.36.refs_3_, bf16[2,384,384]{2,1,0:T(8,128)(2,1)} %collective-permute-done.37.refs_4_, ...), custom_call_target="tpu_custom_call" | custom-call | flops 2415919104 | bytes 5505024 | tf_op jit(solution)/shard_map/gate_up/pallas_call | solution.py:198
  354.9 6.6 %convolution_convert_fusion = bf16[512,1536]{1,0:T(8,128)(2,1)} fusion(bf16[512,1536]{0,1:T(8,128)(2,1)} %bitcast.103, bf16[1536,1536]{1,0:T(8,128)(2,1)} %bitcast.88), kind=kOutput, calls=%fused_computation.30 | convolution fusion | flops 2416705536 | bytes 7864320 | tf_op jit(solution)/shard_map/dot_general | solution.py:387
  365.4 7.6 %fusion.90 = (bf16[512,1536]{1,0:T(8,128)(2,1)S(1)}, f32[512,1536]{1,0:T(8,128)}) fusion(bf16[512,1536]{1,0:T(8,128)(2,1)} %collective-permute-done.64, bf16[512,1536]{0,1:T(8,128)(2,1)} %bitcast.92, bf16[1536,1536]{1,0:T(8,128)(2,1)} %bitcast.89), kind=kOutput, calls=%fused_computation.225 | convolution fusion | flops 2418278400 | bytes 12582912 | tf_op jit(solution)/shard_map/dot_general | solution.py:388
  382.6 5.5 %collective-permute-done.67 = bf16[128,1536]{1,0:T(8,128)(2,1)S(1)} collective-permute-done((bf16[128,1536]{1,0:T(8,128)(2,1)}, bf16[128,1536]{1,0:T(8,128)(2,1)S(1)}, u32[]{:S(2)}, u32[]{:S(2)}) %collective-permute-start.67) | collective-permute-done | bytes 393248 | tf_op jit(solution)/shard_map/ppermute | solution.py:221
  388.1 16.5 %collective-permute-done.66 = bf16[128,1536]{1,0:T(8,128)(2,1)} collective-permute-done((bf16[128,1536]{1,0:T(8,128)(2,1)}, bf16[128,1536]{1,0:T(8,128)(2,1)}, u32[]{:S(2)}, u32[]{:S(2)}) %collective-permute-start.66) | collective-permute-done | bytes 393248 | tf_op jit(solution)/shard_map/ppermute | solution.py:221
  (302 shorter events, 191.4 us)
Async XLA Ops:
  3.9 74.4 %collective-permute-start.2 = (bf16[128,1664]{1,0:T(8,128)(2,1)}, bf16[128,1664]{1,0:T(8,128)(2,1)S(1)}, u32[]{:S(2)}, u32[]{:S(2)}) collective-permute-start(bf16[128,1664]{1,0:T(8,128)(2,1)} %pad_maximum_fusion.11), channel_id=1, source_target_pairs={{0,3},{1,0},{2,1},{3,2},{4,7},{5,4},{6,5},{7,6},{8,11},{9,8},{10,9... | collective-permute-start | bytes 1277960 | tf_op jit(solution)/shard_map/ppermute | solution.py:221
  9.0 70.9 %collective-permute-start.1 = (bf16[128,1664]{1,0:T(8,128)(2,1)}, bf16[128,1664]{1,0:T(8,128)(2,1)}, u32[]{:S(2)}, u32[]{:S(2)}) collective-permute-start(bf16[128,1664]{1,0:T(8,128)(2,1)} %pad_maximum_fusion.11), channel_id=1, source_target_pairs={{0,2},{1,3},{2,0},{3,1},{4,6},{5,7},{6,4},{7,5},{8,10},{9,11},{10,... | collective-permute-start | bytes 1277960 | tf_op jit(solution)/shard_map/ppermute | solution.py:221
  10.0 30.1 %collective-permute-start.22 = (bf16[48,1536]{1,0:T(8,128)(2,1)S(1)}, bf16[48,1536]{1,0:T(8,128)(2,1)}, u32[]{:S(2)}, u32[]{:S(2)}) collective-permute-start(bf16[48,1536]{1,0:T(8,128)(2,1)S(1)} %convert_element_type.84), channel_id=1, source_target_pairs={{0,3},{1,0},{2,1},{3,2},{4,7},{5,4},{6,5},{7,6},{8,11},{9,8},{10,9... | collective-permute-start | bytes 442376 | tf_op jit(solution)/shard_map/ppermute | solution.py:221
  10.5 39.8 %collective-permute-start.21 = (bf16[48,1536]{1,0:T(8,128)(2,1)S(1)}, bf16[48,1536]{1,0:T(8,128)(2,1)}, u32[]{:S(2)}, u32[]{:S(2)}) collective-permute-start(bf16[48,1536]{1,0:T(8,128)(2,1)S(1)} %convert_element_type.84), channel_id=1, source_target_pairs={{0,2},{1,3},{2,0},{3,1},{4,6},{5,7},{6,4},{7,5},{8,10},{9,11},{10,... | collective-permute-start | bytes 442376 | tf_op jit(solution)/shard_map/ppermute | solution.py:221
  13.0 37.3 %collective-permute-start.20 = (bf16[48,1536]{1,0:T(8,128)(2,1)S(1)}, bf16[48,1536]{1,0:T(8,128)(2,1)}, u32[]{:S(2)}, u32[]{:S(2)}) collective-permute-start(bf16[48,1536]{1,0:T(8,128)(2,1)S(1)} %convert_element_type.84), channel_id=1, source_target_pairs={{0,1},{1,2},{2,3},{3,0},{4,5},{5,6},{6,7},{7,4},{8,9},{9,10},{10,1... | collective-permute-start | bytes 442376 | tf_op jit(solution)/shard_map/ppermute | solution.py:221
  75.0 39.8 %collective-permute-start.32 = (bf16[8,48,1536]{2,1,0:T(8,128)(2,1)}, bf16[8,48,1536]{2,1,0:T(8,128)(2,1)S(1)}, u32[]{:S(2)}, u32[]{:S(2)}) collective-permute-start(bf16[8,48,1536]{2,1,0:T(8,128)(2,1)} %get-tuple-element.10), channel_id=1, source_target_pairs={{0,4},{4,0},{8,12},{12,8},{16,20},{20,16},{24,28},{28,24},{1,5},{5... | collective-permute-start | bytes 3538952 | tf_op jit(solution)/shard_map/ppermute | solution.py:225
  88.8 26.8 %collective-permute-start.57 = (bf16[8,24,1536]{2,1,0:T(8,128)(2,1)}, bf16[8,24,1536]{2,1,0:T(8,128)(2,1)}, u32[]{:S(2)}, u32[]{:S(2)}) collective-permute-start(bf16[8,24,1536]{2,1,0:T(8,128)(2,1)} %get-tuple-element.17), channel_id=1, source_target_pairs={{0,4},{4,0},{8,12},{12,8},{16,20},{20,16},{24,28},{28,24},{1,5},{5... | collective-permute-start | bytes 1769480 | tf_op jit(solution)/shard_map/ppermute | solution.py:225
  89.6 27.5 %collective-permute-start.24 = (bf16[192,1536]{1,0:T(8,128)(2,1)}, bf16[192,1536]{1,0:T(8,128)(2,1)}, u32[]{:S(2)}, u32[]{:S(2)}) collective-permute-start(bf16[192,1536]{1,0:T(8,128)(2,1)} %pad_maximum_fusion.6.refs_2_), channel_id=1, source_target_pairs={{0,16},{4,20},{8,24},{12,28},{16,0},{20,4},{24,8},{28,12},{1,17},{... | collective-permute-start | bytes 1769480 | tf_op jit(solution)/shard_map/ppermute | solution.py:225
  182.0 39.1 %collective-permute-start.62 = (bf16[4,48,1536]{2,1,0:T(8,128)(2,1)S(1)}, bf16[4,48,1536]{2,1,0:T(8,128)(2,1)S(1)}, u32[]{:S(2)}, u32[]{:S(2)}) collective-permute-start(bf16[4,48,1536]{2,1,0:T(8,128)(2,1)S(1)} %bitcast.99), channel_id=1, source_target_pairs={{0,16},{4,20},{8,24},{12,28},{16,0},{20,4},{24,8},{28,12},{1,17},{... | collective-permute-start | bytes 1769480 | tf_op jit(solution)/shard_map/ppermute | solution.py:225
  183.6 39.6 %collective-permute-start.58 = (bf16[4,48,1536]{2,1,0:T(8,128)(2,1)S(1)}, bf16[4,48,1536]{2,1,0:T(8,128)(2,1)S(1)}, u32[]{:S(2)}, u32[]{:S(2)}) collective-permute-start(bf16[4,48,1536]{2,1,0:T(8,128)(2,1)S(1)} %bitcast.96), channel_id=1, source_target_pairs={{0,8},{4,12},{8,0},{12,4},{16,24},{20,28},{24,16},{28,20},{1,9},{5... | collective-permute-start | bytes 1769480 | tf_op jit(solution)/shard_map/ppermute | solution.py:225
  195.3 29.4 %collective-permute-start.28 = (bf16[192,1536]{1,0:T(8,128)(2,1)}, bf16[192,1536]{1,0:T(8,128)(2,1)S(1)}, u32[]{:S(2)}, u32[]{:S(2)}) collective-permute-start(bf16[192,1536]{1,0:T(8,128)(2,1)} %collective-permute-done.24.refs_4_), channel_id=1, source_target_pairs={{0,4},{4,0},{8,12},{12,8},{16,20},{20,16},{24,28},{28,24},{1,5},{5... | collective-permute-start | bytes 1769480 | tf_op jit(solution)/shard_map/ppermute | solution.py:225
  195.4 29.3 %collective-permute-start.27 = (bf16[192,1536]{1,0:T(8,128)(2,1)S(1)}, bf16[192,1536]{1,0:T(8,128)(2,1)S(1)}, u32[]{:S(2)}, u32[]{:S(2)}) collective-permute-start(bf16[192,1536]{1,0:T(8,128)(2,1)S(1)} %collective-permute-done.23.refs_3_), channel_id=1, source_target_pairs={{0,4},{4,0},{8,12},{12,8},{16,20},{20,16},{24,28},{28,24},{1,5},{5... | collective-permute-start | bytes 1769480 | tf_op jit(solution)/shard_map/ppermute | solution.py:225
  223.2 27.2 %collective-permute-start.59 = (bf16[4,48,1536]{2,1,0:T(8,128)(2,1)S(1)}, bf16[4,48,1536]{2,1,0:T(8,128)(2,1)S(1)}, u32[]{:S(2)}, u32[]{:S(2)}) collective-permute-start(bf16[4,48,1536]{2,1,0:T(8,128)(2,1)S(1)} %bitcast.97), channel_id=1, source_target_pairs={{0,16},{4,20},{8,24},{12,28},{16,0},{20,4},{24,8},{28,12},{1,17},{... | collective-permute-start | bytes 1769480 | tf_op jit(solution)/shard_map/ppermute | solution.py:225
  224.8 27.8 %collective-permute-start.60 = (bf16[4,48,1536]{2,1,0:T(8,128)(2,1)S(1)}, bf16[4,48,1536]{2,1,0:T(8,128)(2,1)S(1)}, u32[]{:S(2)}, u32[]{:S(2)}) collective-permute-start(bf16[4,48,1536]{2,1,0:T(8,128)(2,1)S(1)} %collective-permute-done.58), channel_id=1, source_target_pairs={{0,16},{4,20},{8,24},{12,28},{16,0},{20,4},{24,8},{28,12},{1,17},{... | collective-permute-start | bytes 1769480 | tf_op jit(solution)/shard_map/ppermute | solution.py:225
  225.3 37.4 %collective-permute-start.54 = (bf16[2,384,384]{2,1,0:T(8,128)(2,1)}, bf16[2,384,384]{2,1,0:T(8,128)(2,1)}, u32[]{:S(2)}, u32[]{:S(2)}) collective-permute-start(bf16[2,384,384]{2,1,0:T(8,128)(2,1)} %bitcast.37.refs_2_), channel_id=1, source_target_pairs={{0,8},{4,12},{8,0},{12,4},{16,24},{20,28},{24,16},{28,20},{1,9},{5... | collective-permute-start | bytes 1769480 | tf_op jit(solution)/shard_map/ppermute | solution.py:225
  239.8 29.8 %collective-permute-start.55 = (bf16[2,384,384]{2,1,0:T(8,128)(2,1)}, bf16[2,384,384]{2,1,0:T(8,128)(2,1)}, u32[]{:S(2)}, u32[]{:S(2)}) collective-permute-start(bf16[2,384,384]{2,1,0:T(8,128)(2,1)} %bitcast.37.refs_2_), channel_id=1, source_target_pairs={{0,16},{4,20},{8,24},{12,28},{16,0},{20,4},{24,8},{28,12},{1,17},{... | collective-permute-start | bytes 1769480 | tf_op jit(solution)/shard_map/ppermute | solution.py:225
  249.9 40.6 %collective-permute-start.30 = (bf16[512,1536]{1,0:T(8,128)(2,1)}, bf16[512,1536]{1,0:T(8,128)(2,1)}, u32[]{:S(2)}, u32[]{:S(2)}) collective-permute-start(bf16[512,1536]{1,0:T(8,128)(2,1)} %multiply_convert_fusion), channel_id=1, source_target_pairs={{0,4},{4,0},{8,12},{12,8},{16,20},{20,16},{24,28},{28,24},{1,5},{5... | collective-permute-start | bytes 4718600 | tf_op jit(solution)/shard_map/ppermute | solution.py:225
  269.7 60.5 %collective-permute-start.42 = (bf16[2,384,384]{2,1,0:T(8,128)(2,1)S(1)}, bf16[2,384,384]{2,1,0:T(8,128)(2,1)S(1)}, u32[]{:S(2)}, u32[]{:S(2)}) collective-permute-start(bf16[2,384,384]{2,1,0:T(8,128)(2,1)S(1)} %bitcast.115), channel_id=1, source_target_pairs={{0,8},{4,12},{8,0},{12,4},{16,24},{20,28},{24,16},{28,20},{1,9},{5... | collective-permute-start | bytes 1769480 | tf_op jit(solution)/shard_map/ppermute | solution.py:225
  277.4 35.7 %collective-permute-start.56 = (bf16[2,384,384]{2,1,0:T(8,128)(2,1)}, bf16[2,384,384]{2,1,0:T(8,128)(2,1)S(1)}, u32[]{:S(2)}, u32[]{:S(2)}) collective-permute-start(bf16[2,384,384]{2,1,0:T(8,128)(2,1)} %collective-permute-done.55.refs_4_), channel_id=1, source_target_pairs={{0,8},{4,12},{8,0},{12,4},{16,24},{20,28},{24,16},{28,20},{1,9},{5... | collective-permute-start | bytes 1769480 | tf_op jit(solution)/shard_map/ppermute | solution.py:225
  289.0 33.0 %collective-permute-start.50 = (bf16[2,384,384]{2,1,0:T(8,128)(2,1)}, bf16[2,384,384]{2,1,0:T(8,128)(2,1)S(1)}, u32[]{:S(2)}, u32[]{:S(2)}) collective-permute-start(bf16[2,384,384]{2,1,0:T(8,128)(2,1)} %collective-permute-done.48.refs_3_), channel_id=1, source_target_pairs={{0,16},{4,20},{8,24},{12,28},{16,0},{20,4},{24,8},{28,12},{1,17},{... | collective-permute-start | bytes 1769480 | tf_op jit(solution)/shard_map/ppermute | solution.py:225
  290.5 39.6 %collective-permute-start.44 = (bf16[2,384,384]{2,1,0:T(8,128)(2,1)S(1)}, bf16[2,384,384]{2,1,0:T(8,128)(2,1)S(1)}, u32[]{:S(2)}, u32[]{:S(2)}) collective-permute-start(bf16[2,384,384]{2,1,0:T(8,128)(2,1)S(1)} %collective-permute-done.43.refs_4_), channel_id=1, source_target_pairs={{0,8},{4,12},{8,0},{12,4},{16,24},{20,28},{24,16},{28,20},{1,9},{5... | collective-permute-start | bytes 1769480 | tf_op jit(solution)/shard_map/ppermute | solution.py:225
  300.6 38.6 %collective-permute-start.37 = (bf16[2,384,384]{2,1,0:T(8,128)(2,1)S(1)}, bf16[2,384,384]{2,1,0:T(8,128)(2,1)}, u32[]{:S(2)}, u32[]{:S(2)}) collective-permute-start(bf16[2,384,384]{2,1,0:T(8,128)(2,1)S(1)} %bitcast.112), channel_id=1, source_target_pairs={{0,16},{4,20},{8,24},{12,28},{16,0},{20,4},{24,8},{28,12},{1,17},{... | collective-permute-start | bytes 1769480 | tf_op jit(solution)/shard_map/ppermute | solution.py:225
  377.2 27.5 %collective-permute-start.66 = (bf16[128,1536]{1,0:T(8,128)(2,1)}, bf16[128,1536]{1,0:T(8,128)(2,1)}, u32[]{:S(2)}, u32[]{:S(2)}) collective-permute-start(bf16[128,1536]{1,0:T(8,128)(2,1)} %get-tuple-element.13), channel_id=1, source_target_pairs={{0,2},{1,3},{2,0},{3,1},{4,6},{5,7},{6,4},{7,5},{8,10},{9,11},{10,... | collective-permute-start | bytes 1179656 | tf_op jit(solution)/shard_map/ppermute | solution.py:221
  377.2 27.5 %collective-permute-start.65 = (bf16[128,1536]{1,0:T(8,128)(2,1)}, bf16[128,1536]{1,0:T(8,128)(2,1)}, u32[]{:S(2)}, u32[]{:S(2)}) collective-permute-start(bf16[128,1536]{1,0:T(8,128)(2,1)} %get-tuple-element.11), channel_id=1, source_target_pairs={{0,3},{1,0},{2,1},{3,2},{4,7},{5,4},{6,5},{7,6},{8,11},{9,8},{10,9... | collective-permute-start | bytes 1179656 | tf_op jit(solution)/shard_map/ppermute | solution.py:221
  (93 other events, 1257.5 us)

commit v2 on v1

v2 whole, which is shorter than its diff:
```python
import functools
import math

import jax
import jax.numpy as jnp
from jax import lax
from jax.experimental import pallas as pl
from jax.experimental.pallas import tpu as pltpu
from jax.sharding import PartitionSpec as P

D = 1536
FF = 768
QH = 12
KVH = 2
HD = 128
E = 16
PAGE = 128
QW = 1536
QKV = 2048
WIDE = 512
ROWS = 256
PARTS = 2
CHUNKS = 2
BF = jnp.bfloat16
F32 = jnp.float32
VMEM = 56 * 1024 * 1024


def rms_scale(values, gain):
    values = values.astype(F32)
    mean_sq = jnp.mean(values * values, axis=-1, keepdims=True)
    return values * lax.rsqrt(mean_sq + 1e-06) * gain


def rotation(position):
    half = HD // 2
    steps_all = jnp.arange(half, dtype=F32)
    frequency = jnp.exp(steps_all * (-2.0 * math.log(10000.0) / HD))
    angle = position[:, None] * frequency[None, :]
    cosine = jnp.cos(angle)
    sine = jnp.sin(angle)
    return (
        jnp.concatenate([cosine, cosine], axis=1),
        jnp.concatenate([-sine, sine], axis=1),
    )


def segment_begin(lengths, index):
    starts = jnp.cumsum(lengths) - lengths
    member = index[:, None] >= starts[None, :]
    return jnp.max(jnp.where(member, starts[None, :], 0), axis=1)


def put(held, spots, first, block, value):
    rows = value.shape[0]
    if block % 16 != 0:
        held[pl.ds(first * block, rows), :] = value[...]
        return
    for k in range(rows // block):
        spot = pl.multiple_of(spots[first + k], block)
        held[pl.ds(spot, block), :] = value[k * block : (k + 1) * block, :]


def put_all(held, spots, block, pieces):
    first = 0
    for ref in pieces:
        for n in range(ref.shape[0]):
            put(held, spots, first, block, ref.at[n])
            first += ref.shape[1] // block


def project_kernel(pieces, block, spots, *refs):
    x_ref, cos_ref, sin_ref = refs[:3]
    out_ref, held = refs[3 + pieces :]
    step = pl.program_id(0)
    put_all(held, spots, block, refs[3 : 3 + pieces])
    result = jnp.dot(x_ref[...], held[...], preferred_element_type=F32)
    turning = (QW + KVH * HD) // HD
    for h in range(WIDE // HD):
        value = result[:, h * HD : (h + 1) * HD]
        turned = value * cos_ref[...] + pltpu.roll(value, HD // 2, 1) * sin_ref[...]
        value = jnp.where(step * (WIDE // HD) + h < turning, turned, value)
        out_ref[:, h * HD : (h + 1) * HD] = value.astype(BF)


def project(spots, block, x, cosine, sine, weights):
    count = x.shape[0]
    whole = lambda j, _: (0, 0)
    return pl.pallas_call(
        functools.partial(project_kernel, len(weights), block),
        grid_spec=pltpu.PrefetchScalarGridSpec(
            num_scalar_prefetch=1,
            grid=(QKV // WIDE,),
            in_specs=[
                pl.BlockSpec((count, D), whole),
                pl.BlockSpec((count, HD), whole),
                pl.BlockSpec((count, HD), whole),
            ]
            + [pl.BlockSpec(w.shape[:2] + (WIDE,), lambda j, _: (0, 0, j)) for w in weights],
            out_specs=pl.BlockSpec((count, WIDE), lambda j, _: (0, j)),
            scratch_shapes=[pltpu.VMEM((D, WIDE), BF)],
        ),
        out_shape=jax.ShapeDtypeStruct((count, QKV), BF),
        compiler_params=pltpu.CompilerParams(vmem_limit_bytes=VMEM),
        cost_estimate=pl.CostEstimate(
            flops=2 * count * D * QKV, bytes_accessed=2 * D * QKV + 4 * count * D, transcendentals=0
        ),
        name="project",
    )(spots, x, cosine, sine, *weights)


def attend_kernel(q_ref, k_ref, v_ref, begin_ref, across_ref, out_ref):
    count = q_ref.shape[0]
    for first in range(0, count, ROWS):
        rows, seen = slice(first, first + ROWS), first + ROWS
        scores = lax.dot_general(
            q_ref[rows, :], k_ref[:seen, :], (((1,), (1,)), ((), ())), preferred_element_type=F32
        ) * (1.0 / math.sqrt(HD))
        across = across_ref[:, :seen]
        mine = first + lax.broadcasted_iota(jnp.int32, (ROWS, 1), 0)
        allowed = (across >= begin_ref[rows, :]) & (across <= mine)
        scores = jnp.where(allowed, scores, -1e30)
        highest = jnp.max(scores, axis=1, keepdims=True)
        weights = jnp.exp(scores - highest)
        total = jnp.sum(weights, axis=1, keepdims=True)
        mixed = jnp.dot(weights.astype(BF), v_ref[:seen, :], preferred_element_type=F32)
        out_ref[rows, :] = (mixed / total).astype(BF)


def attend(qkv, begin, index):
    count = qkv.shape[0]
    per = QH // KVH
    column = pl.BlockSpec((count, 1), lambda h: (0, 0))
    return pl.pallas_call(
        attend_kernel,
        grid=(QH,),
        in_specs=[
            pl.BlockSpec((count, HD), lambda h: (0, h)),
            pl.BlockSpec((count, HD), lambda h: (0, QH + h // per)),
            pl.BlockSpec((count, HD), lambda h: (0, QH + KVH + h // per)),
            column,
            pl.BlockSpec((1, count), lambda h: (0, 0)),
        ],
        out_specs=pl.BlockSpec((count, HD), lambda h: (0, h)),
        out_shape=jax.ShapeDtypeStruct((count, QW), BF),
        compiler_params=pltpu.CompilerParams(vmem_limit_bytes=VMEM),
        cost_estimate=pl.CostEstimate(
            flops=4 * QH * count * count * HD,
            bytes_accessed=2 * count * (QKV + QW),
            transcendentals=QH * count * count,
        ),
        name="attend",
    )(qkv, qkv, qkv, begin[:, None], index[None, :])


def mix_kernel(pieces, block, spots, *refs):
    x_ref, tokens_ref = refs[:2]
    out_ref, held = refs[2 + pieces :]
    put_all(held, spots, block, refs[2 : 2 + pieces])
    out_ref[...] = tokens_ref[...].astype(F32) + jnp.dot(
        x_ref[...], held[...], preferred_element_type=F32
    )


def mix(spots, block, x, tokens, weights):
    count = x.shape[0]
    return pl.pallas_call(
        functools.partial(mix_kernel, len(weights), block),
        grid_spec=pltpu.PrefetchScalarGridSpec(
            num_scalar_prefetch=1,
            grid=(D // WIDE,),
            in_specs=[
                pl.BlockSpec((count, QW), lambda j, _: (0, 0)),
                pl.BlockSpec((count, WIDE), lambda j, _: (0, j)),
            ]
            + [pl.BlockSpec(w.shape[:2] + (WIDE,), lambda j, _: (0, 0, j)) for w in weights],
            out_specs=pl.BlockSpec((count, WIDE), lambda j, _: (0, j)),
            scratch_shapes=[pltpu.VMEM((QW, WIDE), BF)],
        ),
        out_shape=jax.ShapeDtypeStruct((count, D), F32),
        compiler_params=pltpu.CompilerParams(vmem_limit_bytes=VMEM),
        cost_estimate=pl.CostEstimate(
            flops=2 * count * D * QW, bytes_accessed=2 * D * QW + 8 * count * D, transcendentals=0
        ),
        name="mix",
    )(spots, x, tokens, *weights)


def norm_kernel(span, spots, x_ref, gain_ref, out_ref, held):
    value = x_ref[...]
    mean_sq = jnp.mean(value * value, axis=1, keepdims=True)
    held[...] = (value * lax.rsqrt(mean_sq + 1e-06) * gain_ref[...]).astype(BF)
    for k in range(D // span):
        spot = pl.multiple_of(spots[k], span) if span % 128 == 0 else k * span
        out_ref[:, k * span : (k + 1) * span] = held[:, pl.ds(spot, span)]


def norm_blocks(spots, span, x, gain):
    count = x.shape[0]
    out = pl.pallas_call(
        functools.partial(norm_kernel, span),
        grid_spec=pltpu.PrefetchScalarGridSpec(
            num_scalar_prefetch=1,
            grid=(count // 128,),
            in_specs=[
                pl.BlockSpec((128, D), lambda i, _: (i, 0)),
                pl.BlockSpec((1, D), lambda i, _: (0, 0)),
            ],
            out_specs=pl.BlockSpec((128, D), lambda i, _: (i, 0)),
            scratch_shapes=[pltpu.VMEM((128, D), BF)],
        ),
        out_shape=jax.ShapeDtypeStruct((count, D), BF),
        compiler_params=pltpu.CompilerParams(vmem_limit_bytes=VMEM),
        cost_estimate=pl.CostEstimate(
            flops=4 * count * D, bytes_accessed=6 * count * D, transcendentals=count
        ),
        name="norm",
    )(spots, x, gain[None, :])
    if span % 128 == 0:
        return out
    return jnp.concatenate(
        [lax.dynamic_slice_in_dim(out, spots[k], span, 1) for k in range(D // span)], axis=1
    )


def gate_up_kernel(orders, mine_ref, other_ref, gate_ref, *refs):
    weights, out_ref = refs[:-1], refs[-1]
    wide = weights[0].shape[1]
    width, span = wide // 4, D // len(orders[0])

    def one(x_ref):
        for p, order in enumerate(orders):
            some = len(order) // 2
            result = None
            for side in range(2):
                blocks = order[side * some : (side + 1) * some]
                if blocks == list(range(blocks[0], blocks[0] + some)):
                    x = x_ref[:, blocks[0] * span : (blocks[0] + some) * span]
                else:
                    x = jnp.concatenate(
                        [x_ref[:, k * span : (k + 1) * span] for k in blocks], axis=1
                    )
                term = jnp.dot(x, weights[2 * p + side][...], preferred_element_type=F32)
                result = term if result is None else result + term
            for e in range(2):
                n = 2 * p + e
                gate = result[:, 2 * e * width : (2 * e + 1) * width]
                up = result[:, (2 * e + 1) * width : (2 * e + 2) * width]
                activated = jnp.maximum(gate, 0.0) * up * gate_ref[:, n : n + 1]
                out_ref[:, n * width : (n + 1) * width] = activated.astype(BF)

    @pl.when(pl.program_id(0) == 0)
    def _():
        one(mine_ref)

    @pl.when(pl.program_id(0) == 1)
    def _():
        one(other_ref)


def gate_up(orders, mine, other, gate, weights):
    count, experts = mine.shape[0], gate.shape[1]
    deep, wide = weights[0].shape
    whole = pl.BlockSpec((deep, wide), lambda i: (0, 0))
    rows = pl.BlockSpec((count, D), lambda i: (0, 0))
    return pl.pallas_call(
        functools.partial(gate_up_kernel, orders),
        grid=(2,),
        in_specs=[rows, rows, pl.BlockSpec((count, experts), lambda i: (i, 0))]
        + [whole] * len(weights),
        out_specs=pl.BlockSpec((count, experts * wide // 4), lambda i: (i, 0)),
        out_shape=jax.ShapeDtypeStruct((2 * count, experts * wide // 4), BF),
        compiler_params=pltpu.CompilerParams(vmem_limit_bytes=VMEM),
        cost_estimate=pl.CostEstimate(
            flops=2 * experts * count * D * wide,
            bytes_accessed=D * (experts * wide + 4 * count),
            transcendentals=0,
        ),
        name="gate_up",
    )(mine, other, gate, *weights)


def down_kernel(parts, block, spots, *refs):
    acts, weights = refs[:parts], refs[parts:-4]
    mine_ref, other_ref, held, side = refs[-4:]
    deep = acts[0].shape[1]
    for n, act in enumerate(acts):
        side[:, n * deep : (n + 1) * deep] = act[...]
    span = held.shape[0] // E * 2
    experts = weights[0].shape[1]
    stacks = 2 if block % 16 == 0 else 1
    for n in range(0, len(weights), stacks):
        for e in range(experts):
            first = (n // stacks * experts + e) * span
            put_all(
                held.at[pl.ds(first, span)],
                spots.at[n // stacks],
                block,
                [w.at[:, e] for w in weights[n : n + stacks]],
            )
    half = side.shape[0] // 2
    total = jnp.dot(side[half:, :], held[...], preferred_element_type=F32)
    other_ref[...] = total.astype(other_ref.dtype)
    mine_ref[...] = jnp.dot(side[:half, :], held[...], preferred_element_type=F32)


def down_project(spots, block, acts, part, parts, weights):
    rows, deep = acts[0].shape
    total, wide = deep * len(acts), D // parts
    return pl.pallas_call(
        functools.partial(down_kernel, len(acts), block),
        grid_spec=pltpu.PrefetchScalarGridSpec(
            num_scalar_prefetch=1,
            grid=(1,),
            in_specs=[pl.BlockSpec((rows, deep), lambda j, _: (0, 0))] * len(acts)
            + [pl.BlockSpec(w.shape[:3] + (wide,), lambda j, _: (0, 0, 0, part)) for w in weights],
            out_specs=[pl.BlockSpec((rows // 2, wide), lambda j, _: (0, 0))] * 2,
            scratch_shapes=[pltpu.VMEM((total, wide), BF), pltpu.VMEM((rows, total), BF)],
        ),
        out_shape=[
            jax.ShapeDtypeStruct((rows // 2, wide), F32),
            jax.ShapeDtypeStruct((rows // 2, wide), BF),
        ],
        compiler_params=pltpu.CompilerParams(vmem_limit_bytes=VMEM),
        cost_estimate=pl.CostEstimate(
            flops=2 * rows * wide * total,
            bytes_accessed=2 * wide * total + 2 * rows * total + 3 * rows * wide,
            transcendentals=0,
        ),
        name="down",
    )(spots, *acts, *weights)


def along_blk(value, step):
    size = lax.axis_size("blk")
    return lax.ppermute(value, "blk", [(i, (i + step) % size) for i in range(size)])


def across_rep(value, mask):
    return lax.ppermute(value, "rep", [(i, i ^ mask) for i in range(lax.axis_size("rep"))])


def chip_bits():
    return (lax.axis_size("rep") // 2).bit_length() - 1


def chip_bits():
    return (lax.axis_size("rep") // 2).bit_length() - 1


def chip_start(value, turn):
    return value[None], across_rep(value[None], 2 << turn)


def chip_gather(held, came, turn, gate=()):
    bits = chip_bits()
    for n in range(1, bits):
        held = jnp.concatenate([held, came], axis=0)
        came = across_rep(after(held, gate), 2 << ((n + turn) % bits))
    return [held, came]


def chip_order(turn):
    bits = chip_bits()
    order = [0]
    for n in range(bits):
        order = order + [k ^ (1 << ((n + turn) % bits)) for k in order]
    return order


def after(value, other):
    if isinstance(other, tuple) and not other:
        return value
    return lax.optimization_barrier((value, other))[0]


def exchange_blk(value):
    return lax.all_to_all(value, "blk", 0, 0, tiled=True)


def gather_blk(value):
    size = lax.axis_size("blk")
    return exchange_blk(jnp.broadcast_to(value[None], (size,) + value.shape))


def body(
    tokens,
    attn_in,
    attn_out,
    expert_in,
    expert_out,
    attn_gain,
    moe_gain,
    lengths,
    page_table,
    routes,
    gates,
):
    count = tokens.shape[0]
    reps, cycle_size = lax.axis_size("rep"), lax.axis_size("blk")
    rep, place = lax.axis_index("rep"), lax.axis_index("blk")
    chip, core = rep // 2, rep % 2
    group_rows = count * cycle_size
    half_experts = E // 2
    quarter = FF // cycle_size
    rows_in, rows_out = expert_in.shape[1], expert_out.shape[1]

    def split_cores(value):
        half = value.shape[0] // 2
        mine = lax.dynamic_slice_in_dim(value, core * half, half, 0)
        other = lax.dynamic_slice_in_dim(value, (1 - core) * half, half, 0)
        came = across_rep(other, 1)
        return jnp.stack(
            [jnp.where(core == 0, mine, came), jnp.where(core == 0, came, mine)], axis=1
        )

    spot = jnp.arange(2 * FF, dtype=jnp.int32)
    inner = spot % rows_out
    from_rep = (spot // rows_out) % reps
    which = (spot // quarter) % 2
    from_blk = spot // (2 * quarter)
    column = which * FF + (from_rep * cycle_size + from_blk) * rows_out + inner
    shuffle = (spot[:, None] == column[None, :]).astype(BF)
    ordered = jnp.dot(
        expert_in.astype(BF).reshape(E * rows_in, 2 * FF), shuffle, preferred_element_type=F32
    )
    ordered = ordered.astype(BF).reshape(E // 2, 2, rows_in, 2 * FF)
    pairs = jnp.stack(
        [
            jnp.concatenate(
                [
                    lax.slice_in_dim(ordered[:, e], b * 2 * quarter, (b + 1) * 2 * quarter, axis=2)
                    for e in range(2)
                ],
                axis=2,
            )
            for b in range(cycle_size)
        ],
        axis=1,
    )
    pairs = split_cores(pairs)
    per_chunk = half_experts // 2 // CHUNKS

    down = split_cores(expert_out.astype(BF)).reshape(half_experts, 2 * rows_out, D)
    down_first = [chip_start(down[n * 4 : (n + 1) * 4], n % 2) for n in range(half_experts // 4)]

    attn_here = jnp.concatenate([attn_in.astype(BF), attn_out.astype(BF)], axis=1)
    attn_line = gather_blk(attn_here).reshape(cycle_size * rows_in, QKV + D)
    ready = after(attn_line, down_first)
    qkv_first = chip_start(ready[:, :QKV], 0)
    mix_first = chip_start(ready[:, QKV:], 1)
    down_parts = [chip_gather(*down_first[n], n % 2) for n in range(len(down_first))]

    gate = (qkv_first, mix_first, down_parts)
    qkv_own = chip_gather(*qkv_first, 0, gate)
    mix_own = chip_gather(*mix_first, 1, gate)
    qkv_weight = qkv_own + [across_rep(v, 1) for v in qkv_own]
    mix_weight = mix_own + [across_rep(v, 1) for v in mix_own]

    def line_up(n, earlier):
        chunk = pairs[n * per_chunk : (n + 1) * per_chunk].transpose(2, 0, 1, 3, 4)
        lined = exchange_blk(after(chunk, earlier)).transpose(1, 2, 0, 3, 4)
        return lined.reshape(per_chunk, 2 * cycle_size * rows_in, 4 * quarter)

    lines = [line_up(0, (attn_line,))]

    expert_ids = jnp.arange(E, dtype=jnp.int32)
    dense = jnp.sum(
        jnp.where(
            routes[:, :, None] == expert_ids[None, None, :],
            gates.astype(F32)[:, :, None],
            F32(0.0),
        ),
        axis=1,
    ).astype(BF)
    sent = jnp.concatenate([tokens, jnp.pad(dense, ((0, 0), (0, 128 - E)))], axis=1)
    line = gather_blk(after(sent, (lines[0],))).reshape(group_rows, -1)
    group, group_gates = line[:, :D], line[:, D : D + E]

    for n in range(1, CHUNKS):
        lines.append(line_up(n, (line, lines[-1])))

    index = jnp.arange(group_rows, dtype=jnp.int32)
    begin = segment_begin(lengths[0], index)
    cosine, sine = rotation((index - begin).astype(F32))
    block = cycle_size * rows_in

    def attn_spots(turn):
        from_chip = chip ^ jnp.array(chip_order(turn), jnp.int32)
        from_rep = from_chip[None, :] * 2 + (core ^ jnp.arange(2, dtype=jnp.int32))[:, None]
        return (from_rep * block).reshape(-1)

    normed = rms_scale(group, attn_gain).astype(BF)
    up_parts, steps, gate = [], [], ()
    for n in range(CHUNKS):
        lined = after(lines[n], gate)
        first = [chip_start(lined[k], k % 2) for k in range(per_chunk)]
        parts = [chip_gather(*first[k], k % 2) for k in range(per_chunk)]
        up_parts.append([p.reshape(-1, 4 * quarter) for part in parts for p in part])
        steps += [first, parts]
        gate = (parts,)
        if n == 0:
            x = after(normed, (first,))
            qkv = project(attn_spots(0), block, x, cosine, sine, qkv_weight)
            attended = attend(qkv, begin, index)
            gate = (qkv,)
    attended = after(attended, (steps[1],))
    hidden = mix(attn_spots(1), block, attended, group, mix_weight)

    page_count = count // PAGE
    targets = place * page_count + jnp.arange(page_count, dtype=jnp.int32)
    table = page_table[0]
    logical = jnp.sum(
        jnp.where(
            table[None, :] == targets[:, None],
            jnp.arange(table.shape[0], dtype=jnp.int32)[None, :],
            0,
        ),
        axis=1,
    )
    first_row = logical * PAGE
    cache = qkv[:, QW:]
    kv_pages = jnp.stack(
        [lax.dynamic_slice_in_dim(cache, first_row[i], PAGE, 0) for i in range(page_count)]
    )

    span = D // (reps // 2)
    up_spots = (chip ^ jnp.arange(reps // 2, dtype=jnp.int32)) * span
    normed_two = norm_blocks(up_spots, span, hidden, moe_gain)
    other_two = across_rep(normed_two, 1)
    both_gates = jnp.concatenate([group_gates, across_rep(group_gates, 1)], axis=0)
    my_gates = lax.dynamic_slice_in_dim(both_gates, core * half_experts, half_experts, 1).astype(F32)
    acts, orders = [], [chip_order(k % 2) for k in range(per_chunk)]
    for n in range(CHUNKS):
        experts = slice(n * 2 * per_chunk, (n + 1) * 2 * per_chunk)
        x = after(normed_two, (steps[2 * n + 2],)) if n + 1 < CHUNKS else normed_two
        acts.append(gate_up(orders, x, other_two, my_gates[:, experts], up_parts[n]))
    chips, chip_rows = reps // 2, 2 * rows_out
    whose = [chip ^ jnp.array(chip_order(n % 2), jnp.int32) for n in range(len(down_parts))]
    if chip_rows % 16 != 0:
        for n, part in enumerate(down_parts):
            part = jnp.take(jnp.concatenate(part, axis=0), jnp.argsort(whose[n]), axis=0)
            down_parts[n] = [part.transpose(1, 0, 2, 3).reshape(1, 4, chips * chip_rows, D)]
    down = [w for part in down_parts for w in part]
    down_spots = jnp.stack(whose) * chip_rows

    def at(array, shift):
        first = (place + shift) % cycle_size * count
        return lax.dynamic_slice_in_dim(array, first, count, 0).astype(F32)

    mixed, came = [], ()
    for n in range(PARTS):
        ready = after(acts, came)
        mine, other = down_project(down_spots, chip_rows, ready, n, PARTS, down)
        came = across_rep(other, 1)
        columns = slice(n * (D // PARTS), (n + 1) * (D // PARTS))
        total = at(hidden[:, columns], 0) + (at(mine, 0) + at(came, 0))
        for step in range(1, cycle_size):
            part = (at(mine, step) + at(came, step)).astype(BF)
            total = total + along_blk(part, step).astype(F32)
        mixed.append(total.astype(BF))
    return (jnp.concatenate(mixed, axis=1), kv_pages)


def solution(mesh):
    in_specs = (
        P(("rep", "blk"), None),
        P(("rep", "blk"), None),
        P(("rep", "blk"), None),
        P(None, ("rep", "blk"), None),
        P(None, ("rep", "blk"), None),
        P(),
        P(),
        P("rep", None),
        P("rep", None),
        P(("rep", "blk"), None),
        P(("rep", "blk"), None),
    )
    out_specs = (P(("rep", "blk"), None), P(("rep", "blk"), None, None))
    return jax.shard_map(body, mesh=mesh, in_specs=in_specs, out_specs=out_specs, check_vma=False)
```

time: 415 us -> 310 us (0.75); the launches traced: 407 us -> 309 us
  matrix products: 37.7 us -> 4.2 us
  starting transfers between devices: 80.1 us -> 47.4 us
  local copies, waits for them, and re-layouts: 45.5 us -> 20.7 us
  waiting for transfers between devices: 138 us -> 131 us
  other arithmetic: 39.4 us -> 33.7 us
  Pallas kernels: 64.6 us -> 69.9 us
    ppermute x24 -> x6, waiting for transfers between devices: 68.8 us -> 26.3 us  [along_blk(): lax.ppermute(value, 'blk', [(i, (i + step) % size) for i in range(size)])]
    dot_general x5 -> x0, matrix products: 32.4 us -> none  [the longest x1 8.46 us: body(): both = jnp.dot(both, order_two, preferred_element_type=F32).astype(BF)]
    ppermute x24 -> x6, starting transfers between devices: 41 us -> 8.82 us  [along_blk(): lax.ppermute(value, 'blk', [(i, (i + step) % size) for i in range(size)])]
    all_to_all x0 -> x4, waiting for transfers between devices: none -> 30.7 us  [exchange_blk(): return lax.all_to_all(value, 'blk', 0, 0, tiled=True)]
    ppermute x44 -> x26, starting transfers between devices: 39.1 us -> 20 us  [across_rep(): lax.ppermute(value, 'rep', [(i, i ^ mask) for i in range(lax.axis_size('r...]
    all_to_all x0 -> x4, starting transfers between devices: none -> 18.6 us  [exchange_blk(): return lax.all_to_all(value, 'blk', 0, 0, tiled=True)]
    slice x12 -> x7, local copies, waits for them, and re-layouts: 17.5 us -> 2.9 us  [the longest x2 1.2 us: body(): first = [chip_start(lined[k], k % 2) for k in range(per_chunk)]]
    pallas_call x6 -> x7, Pallas kernels: 48.8 us -> 57 us  [the longest x2 20.3 us: gate_up(): pl.pallas_call(functools.partial(gate_up_kernel, orders), grid=(2,), in_s...]
  transfers between devices with their start and end apart: 68 -> 36, of which waited for: 21 -> 12; matrix products, arithmetic and copies ran while one was open for 22% -> 16% of each run, Pallas kernels for 14% -> 15%
where the time goes in v2:
time: 310 us; the launch traced here: 309 us
  waiting for transfers between devices  131 us (42%)
  Pallas kernels  69.9 us (23%)
  starting transfers between devices  47.4 us (15%)
  other arithmetic  33.7 us (11%)
  local copies, waits for them, and re-layouts  20.7 us (7%)
  matrix products  4.2 us (1%)
    ppermute x26, waiting for transfers between devices, across_rep(): lax.ppermute(value, 'rep', [(i, i ^ mask) for i in range(lax.axis_size('r...  74 us
    all_to_all x4, waiting for transfers between devices, exchange_blk(): return lax.all_to_all(value, 'blk', 0, 0, tiled=True)  30.7 us
    ppermute x6, waiting for transfers between devices, along_blk(): lax.ppermute(value, 'blk', [(i, (i + step) % size) for i in range(size)])  26.3 us
    pallas_call x2, Pallas kernels, gate_up(): pl.pallas_call(functools.partial(gate_up_kernel, orders), grid=(2,), in_s...  20.3 us
    ppermute x26, starting transfers between devices, across_rep(): lax.ppermute(value, 'rep', [(i, i ^ mask) for i in range(lax.axis_size('r...  20 us
    all_to_all x4, starting transfers between devices, exchange_blk(): return lax.all_to_all(value, 'blk', 0, 0, tiled=True)  18.6 us
    pallas_call x2, Pallas kernels, down_project(): pl.pallas_call(functools.partial(down_kernel, len(acts), block), grid_spe...  14.6 us
    pallas_call x1, Pallas kernels, attend(): pl.pallas_call(attend_kernel, grid=(QH,), in_specs=[pl.BlockSpec((count,...  12.8 us
  transfers between devices with their start and end apart: 36, of which 12 were waited for; matrix products, arithmetic and copies ran while one was open for 16% of the time, Pallas kernels for 15%

profile of v2, /device:TPU:0, one launch (start us, length us, event | category | flops | bytes accessed | tf_op | source)
XLA Modules:
  0.0 308.7 jit_solution(3767147045433014424)
XLA Ops:
  3.9 6.4 %all-to-all-start = ((bf16[4,48,3584]{2,1,0:T(8,128)(2,1)}), bf16[4,48,3584]{2,1,0:T(8,128)(2,1)}, u32[]{:S(2)}, u32[]{:S(2)}) async-start(bf16[4,48,3584]{2,1,0:T(8,128)(2,1)} %broadcast_in_dim.41), calls=%async_computation | async-start | bytes 2752512 | tf_op jit(solution)/shard_map/all_to_all | solution.py:378
  14.0 4.2 %fusion.2 = bf16[1536,768]{0,1:T(8,128)(2,1)S(1)} fusion(bf16[768,1536]{1,0:T(8,128)(2,1)S(1)} %bitcast.76, s32[1536]{0:T(1024)S(1)} %fusion.23), kind=kOutput, calls=%fused_computation.5 | convolution fusion | flops 3627417600 | bytes 4724736 | tf_op jit(solution)/shard_map/dot_general | solution.py:424
  28.5 14.7 %all-to-all-done = bf16[4,48,3584]{2,1,0:T(8,128)(2,1)} async-done(((bf16[4,48,3584]{2,1,0:T(8,128)(2,1)}), bf16[4,48,3584]{2,1,0:T(8,128)(2,1)}, u32[]{:S(2)}, u32[]{:S(2)}) %all-to-all-start) | async-done | bytes 1376288 | tf_op jit(solution)/shard_map/all_to_all | solution.py:378
  43.2 3.7 %all-to-all-start.1 = ((bf16[4,2,2,48,768]{4,3,2,1,0:T(8,128)(2,1)}), bf16[4,2,2,48,768]{4,3,2,1,0:T(8,128)(2,1)S(1)}, u32[]{:S(2)}, u32[]{:S(2)}) async-start(bf16[4,2,2,48,768]{4,3,2,1,0:T(8,128)(2,1)} %get-tuple-element.18), calls=%async_computation.1 | async-start | bytes 2359296 | tf_op jit(solution)/shard_map/all_to_all | solution.py:378
  58.9 16.0 %all-to-all-done.1 = bf16[4,2,2,48,768]{4,3,2,1,0:T(8,128)(2,1)S(1)} async-done(((bf16[4,2,2,48,768]{4,3,2,1,0:T(8,128)(2,1)}), bf16[4,2,2,48,768]{4,3,2,1,0:T(8,128)(2,1)S(1)}, u32[]{:S(2)}, u32[]{:S(2)}) %all-to-all-start.1) | async-done | bytes 1179680 | tf_op jit(solution)/shard_map/all_to_all | solution.py:378
  76.3 3.6 %all-to-all-start.2 = ((bf16[4,128,1664]{2,1,0:T(8,128)(2,1)}), bf16[4,128,1664]{2,1,0:T(8,128)(2,1)S(1)}, u32[]{:S(2)}, u32[]{:S(2)}) async-start(bf16[4,128,1664]{2,1,0:T(8,128)(2,1)} %broadcast_in_dim.42), calls=%async_computation.2 | async-start | bytes 3407872 | tf_op jit(solution)/shard_map/all_to_all | solution.py:378
  79.9 16.9 %collective-permute-done.6 = bf16[1,192,2048]{2,1,0:T(8,128)(2,1)} collective-permute-done((bf16[1,192,2048]{2,1,0:T(8,128)(2,1)}, bf16[1,192,2048]{2,1,0:T(8,128)(2,1)}, u32[]{:S(2)}, u32[]{:S(2)}) %collective-permute-start.6) | collective-permute-done | bytes 786464 | tf_op jit(solution)/shard_map/ppermute | solution.py:340
  96.8 2.7 pad_maximum_fusion.1.refs_3_
  108.3 28.9 %collective-permute-done.10.refs_4_ = bf16[2,192,2048]{2,1,0:T(8,128)(2,1)} collective-permute-done((bf16[2,192,2048]{2,1,0:T(8,128)(2,1)}, bf16[2,192,2048]{2,1,0:T(8,128)(2,1)}, u32[]{:S(2)}, u32[]{:S(2)}) %collective-permute-start.10) | collective-permute-done | bytes 1572896 | tf_op jit(solution)/shard_map/ppermute | solution.py:340
  138.3 4.9 %all-to-all-start.3 = ((bf16[4,2,2,48,768]{4,3,2,1,0:T(8,128)(2,1)}), bf16[4,2,2,48,768]{4,3,2,1,0:T(8,128)(2,1)S(1)}, u32[]{:S(2)}, u32[]{:S(2)}) async-start(bf16[4,2,2,48,768]{4,3,2,1,0:T(8,128)(2,1)} %get-tuple-element.25), calls=%async_computation.3 | async-start | bytes 2359296 | tf_op jit(solution)/shard_map/all_to_all | solution.py:378
  155.0 9.2 %project.1.q_ref.k_ref.v_ref = bf16[512,2048]{1,0:T(8,128)(2,1)} custom-call(s32[8]{0:T(128)} %mul.146.spots, bf16[512,1536]{1,0:T(8,128)(2,1)} %fusion.5.refs_0_, f32[512,128]{1,0:T(8,128)} %get-tuple-element.80.refs_1_, f32[512,128]{1,0:T(8,128)} %get-tuple-element.81.refs_2_, bf16[2,192,2048]{2,1,0:T(8,128)(2,1)} %pad_maximum_fusion.1.refs_3_, ...), custom_call_target="tpu_custom_call" | custom-call | flops 3221225472 | bytes 9437184 | tf_op jit(solution)/shard_map/project/pallas_call | solution.py:89
  164.7 12.8 %attend.1.refs_0_ = bf16[512,1536]{1,0:T(8,128)(2,1)} custom-call(bf16[512,2048]{1,0:T(8,128)(2,1)} %project.1.q_ref.k_ref.v_ref, bf16[512,2048]{1,0:T(8,128)(2,1)} %project.1.q_ref.k_ref.v_ref, bf16[512,2048]{1,0:T(8,128)(2,1)} %project.1.q_ref.k_ref.v_ref, s32[512,1]{1,0:T(8,128)} %copy.66.begin_ref, s32[1,512]{1,0:T(1,128)} %iota.46.across_ref), custom_call_target="tpu_custom_call" | custom-call | flops 1610612736 | bytes 3670016 | tf_op jit(solution)/shard_map/attend/pallas_call | solution.py:134
  179.5 8.1 %mix.1.x_ref = f32[512,1536]{1,0:T(8,128)} custom-call(s32[8]{0:T(128)} %mul.143.spots, bf16[512,1536]{1,0:T(8,128)(2,1)} %attend.1.refs_0_, bf16[512,1536]{1,0:T(8,128)(2,1)} %slice.136.refs_1_, bf16[2,192,1536]{2,1,0:T(8,128)(2,1)} %pad_maximum_fusion.7.refs_2_, bf16[2,192,1536]{2,1,0:T(8,128)(2,1)} %collective-permute-done.15.refs_3_, ...), custom_call_target="tpu_custom_call" | custom-call | flops 2415919104 | bytes 11010048 | tf_op jit(solution)/shard_map/mix/pallas_call | solution.py:167
  187.6 5.0 %norm.1.mine_ref = bf16[512,1536]{1,0:T(8,128)(2,1)} custom-call(s32[4]{0:T(128)} %fusion.34.spots, f32[512,1536]{1,0:T(8,128)} %mix.1.x_ref, f32[1,1536]{1,0:T(1,128)} %broadcast_in_dim.48.gain_ref), custom_call_target="tpu_custom_call" | custom-call | flops 3145728 | bytes 4718592 | tf_op jit(solution)/shard_map/norm/pallas_call | solution.py:200
  195.9 12.8 %collective-permute-done.19 = bf16[1,384,768]{2,1,0:T(8,128)(2,1)S(1)} collective-permute-done((bf16[1,384,768]{2,1,0:T(8,128)(2,1)S(1)}, bf16[1,384,768]{2,1,0:T(8,128)(2,1)S(1)}, u32[]{:S(2)}, u32[]{:S(2)}) %collective-permute-start.19) | collective-permute-done | bytes 589856 | tf_op jit(solution)/shard_map/ppermute | solution.py:340
  214.1 10.2 %gate_up.2.refs_0_ = bf16[1024,768]{1,0:T(8,128)(2,1)} custom-call(bf16[512,1536]{1,0:T(8,128)(2,1)} %norm.1.mine_ref, bf16[512,1536]{1,0:T(8,128)(2,1)} %copy-done.14, f32[1024,4]{1,0:T(8,128)} %get-tuple-element.67.gate_ref, bf16[768,768]{1,0:T(8,128)(2,1)} %bitcast.82, bf16[768,768]{1,0:T(8,128)(2,1)} %bitcast.87, bf16[768,768]{1,0:T(8,128)(2,1)} %bitcast.83, ...), custom_call_target="tpu_custom_call" | custom-call | flops 4831838208 | bytes 7864320 | tf_op jit(solution)/shard_map/gate_up/pallas_call | solution.py:266
  224.3 9.3 %collective-permute-done.22 = bf16[2,384,768]{2,1,0:T(8,128)(2,1)} collective-permute-done((bf16[2,384,768]{2,1,0:T(8,128)(2,1)S(1)}, bf16[2,384,768]{2,1,0:T(8,128)(2,1)}, u32[]{:S(2)}, u32[]{:S(2)}) %collective-permute-start.22) | collective-permute-done | bytes 1179680 | tf_op jit(solution)/shard_map/ppermute | solution.py:340
  237.1 10.1 %gate_up.3.refs_1_ = bf16[1024,768]{1,0:T(8,128)(2,1)} custom-call(bf16[512,1536]{1,0:T(8,128)(2,1)} %norm.1.mine_ref, bf16[512,1536]{1,0:T(8,128)(2,1)} %copy-done.14, f32[1024,4]{1,0:T(8,128)} %get-tuple-element.66.gate_ref, bf16[768,768]{1,0:T(8,128)(2,1)} %bitcast.84, bf16[768,768]{1,0:T(8,128)(2,1)} %bitcast.39.refs_1_, bf16[768,768]{1,0:T(8,128)(2,1)} %bitcast.85, ...), custom_call_target="tpu_custom_call" | custom-call | flops 4831838208 | bytes 7864320 | tf_op jit(solution)/shard_map/gate_up/pallas_call | solution.py:266
  247.2 7.1 %down.2 = (f32[512,768]{1,0:T(8,128)}, bf16[512,768]{1,0:T(8,128)(2,1)}) custom-call(s32[2,4]{1,0:T(2,128)} %add_multiply_fusion.spots, bf16[1024,768]{1,0:T(8,128)(2,1)} %gate_up.2.refs_0_, bf16[1024,768]{1,0:T(8,128)(2,1)} %gate_up.3.refs_1_, bf16[2,4,48,1536]{3,2,1,0:T(8,128)(2,1)} %pad_maximum_fusion.3.refs_2_, ...), custom_call_target="tpu_custom_call" | custom-call | flops 2415919104 | bytes 7864320 | tf_op jit(solution)/shard_map/down/pallas_call | solution.py:310
  257.0 7.4 %down.3 = (f32[512,768]{1,0:T(8,128)}, bf16[512,768]{1,0:T(8,128)(2,1)}) custom-call(s32[2,4]{1,0:T(2,128)} %add_multiply_fusion.spots, bf16[1024,768]{1,0:T(8,128)(2,1)} %gate_up.2.refs_0_, bf16[1024,768]{1,0:T(8,128)(2,1)} %gate_up.3.refs_1_, bf16[2,4,48,1536]{3,2,1,0:T(8,128)(2,1)} %pad_maximum_fusion.3.refs_2_, ...), custom_call_target="tpu_custom_call" | custom-call | flops 2415919104 | bytes 7864320 | tf_op jit(solution)/shard_map/down/pallas_call | solution.py:310
  268.7 3.8 %collective-permute-start.27 = (bf16[128,768]{1,0:T(8,128)(2,1)S(1)}, bf16[128,768]{1,0:T(8,128)(2,1)S(1)}, u32[]{:S(2)}, u32[]{:S(2)}) collective-permute-start(bf16[128,768]{1,0:T(8,128)(2,1)S(1)} %get-tuple-element.39), channel_id=1, source_target_pairs={{0,3},{1,0},{2,1},{3,2},{4,7},{5,4},{6,5},{7,6},{8,11},{9,8},{10,9... | collective-permute-start | bytes 589832 | tf_op jit(solution)/shard_map/ppermute | solution.py:336
  275.5 2.7 collective-permute-start.31
  279.4 11.3 %collective-permute-done.26 = bf16[128,768]{1,0:T(8,128)(2,1)S(1)} collective-permute-done((bf16[128,768]{1,0:T(8,128)(2,1)S(1)}, bf16[128,768]{1,0:T(8,128)(2,1)S(1)}, u32[]{:S(2)}, u32[]{:S(2)}) %collective-permute-start.26) | collective-permute-done | bytes 196640 | tf_op jit(solution)/shard_map/ppermute | solution.py:336
  291.8 15.0 %collective-permute-done.30 = bf16[128,768]{1,0:T(8,128)(2,1)S(1)} collective-permute-done((bf16[128,768]{1,0:T(8,128)(2,1)S(1)}, bf16[128,768]{1,0:T(8,128)(2,1)S(1)}, u32[]{:S(2)}, u32[]{:S(2)}) %collective-permute-start.30) | collective-permute-done | bytes 196640 | tf_op jit(solution)/shard_map/ppermute | solution.py:336
  (171 shorter events, 80.1 us)
Async XLA Ops:
  3.9 39.3 %all-to-all-start = ((bf16[4,48,3584]{2,1,0:T(8,128)(2,1)}), bf16[4,48,3584]{2,1,0:T(8,128)(2,1)}, u32[]{:S(2)}, u32[]{:S(2)}) async-start(bf16[4,48,3584]{2,1,0:T(8,128)(2,1)} %broadcast_in_dim.41), calls=%async_computation | async-start | bytes 2752512 | tf_op jit(solution)/shard_map/all_to_all | solution.py:378
  22.2 24.8 %collective-permute-start.4 = (bf16[1,4,48,1536]{3,2,1,0:T(8,128)(2,1)S(1)}, bf16[1,4,48,1536]{3,2,1,0:T(8,128)(2,1)}, u32[]{:S(2)}, u32[]{:S(2)}) collective-permute-start(bf16[1,4,48,1536]{3,2,1,0:T(8,128)(2,1)S(1)} %bitcast.80), channel_id=1, source_target_pairs={{0,8},{4,12},{8,0},{12,4},{16,24},{20,28},{24,16},{28,20},{1,9},{5... | collective-permute-start | bytes 1769480 | tf_op jit(solution)/shard_map/ppermute | solution.py:340
  23.8 27.0 %collective-permute-start.5 = (bf16[1,4,48,1536]{3,2,1,0:T(8,128)(2,1)S(1)}, bf16[1,4,48,1536]{3,2,1,0:T(8,128)(2,1)}, u32[]{:S(2)}, u32[]{:S(2)}) collective-permute-start(bf16[1,4,48,1536]{3,2,1,0:T(8,128)(2,1)S(1)} %bitcast.78), channel_id=1, source_target_pairs={{0,16},{4,20},{8,24},{12,28},{16,0},{20,4},{24,8},{28,12},{1,17},{... | collective-permute-start | bytes 1769480 | tf_op jit(solution)/shard_map/ppermute | solution.py:340
  43.2 31.7 %all-to-all-start.1 = ((bf16[4,2,2,48,768]{4,3,2,1,0:T(8,128)(2,1)}), bf16[4,2,2,48,768]{4,3,2,1,0:T(8,128)(2,1)S(1)}, u32[]{:S(2)}, u32[]{:S(2)}) async-start(bf16[4,2,2,48,768]{4,3,2,1,0:T(8,128)(2,1)} %get-tuple-element.18), calls=%async_computation.1 | async-start | bytes 2359296 | tf_op jit(solution)/shard_map/all_to_all | solution.py:378
  49.2 50.2 %collective-permute-start.8 = (bf16[2,4,48,1536]{3,2,1,0:T(8,128)(2,1)}, bf16[2,4,48,1536]{3,2,1,0:T(8,128)(2,1)}, u32[]{:S(2)}, u32[]{:S(2)}) collective-permute-start(bf16[2,4,48,1536]{3,2,1,0:T(8,128)(2,1)} %pad_maximum_fusion.3.refs_2_), channel_id=1, source_target_pairs={{0,16},{4,20},{8,24},{12,28},{16,0},{20,4},{24,8},{28,12},{1,17},{... | collective-permute-start | bytes 3538952 | tf_op jit(solution)/shard_map/ppermute | solution.py:340
  53.0 46.5 %collective-permute-start.9 = (bf16[2,4,48,1536]{3,2,1,0:T(8,128)(2,1)}, bf16[2,4,48,1536]{3,2,1,0:T(8,128)(2,1)}, u32[]{:S(2)}, u32[]{:S(2)}) collective-permute-start(bf16[2,4,48,1536]{3,2,1,0:T(8,128)(2,1)} %pad_maximum_fusion.4.refs_4_), channel_id=1, source_target_pairs={{0,8},{4,12},{8,0},{12,4},{16,24},{20,28},{24,16},{28,20},{1,9},{5... | collective-permute-start | bytes 3538952 | tf_op jit(solution)/shard_map/ppermute | solution.py:340
  56.6 40.2 %collective-permute-start.6 = (bf16[1,192,2048]{2,1,0:T(8,128)(2,1)}, bf16[1,192,2048]{2,1,0:T(8,128)(2,1)}, u32[]{:S(2)}, u32[]{:S(2)}) collective-permute-start(bf16[1,192,2048]{2,1,0:T(8,128)(2,1)} %slice_bitcast_fusion.2), channel_id=1, source_target_pairs={{0,8},{4,12},{8,0},{12,4},{16,24},{20,28},{24,16},{28,20},{1,9},{5... | collective-permute-start | bytes 2359304 | tf_op jit(solution)/shard_map/ppermute | solution.py:340
  58.2 41.3 %collective-permute-start.7 = (bf16[1,192,1536]{2,1,0:T(8,128)(2,1)S(1)}, bf16[1,192,1536]{2,1,0:T(8,128)(2,1)}, u32[]{:S(2)}, u32[]{:S(2)}) collective-permute-start(bf16[1,192,1536]{2,1,0:T(8,128)(2,1)S(1)} %slice_bitcast_fusion.3), channel_id=1, source_target_pairs={{0,16},{4,20},{8,24},{12,28},{16,0},{20,4},{24,8},{28,12},{1,17},{... | collective-permute-start | bytes 1769480 | tf_op jit(solution)/shard_map/ppermute | solution.py:340
  76.3 62.0 %all-to-all-start.2 = ((bf16[4,128,1664]{2,1,0:T(8,128)(2,1)}), bf16[4,128,1664]{2,1,0:T(8,128)(2,1)S(1)}, u32[]{:S(2)}, u32[]{:S(2)}) async-start(bf16[4,128,1664]{2,1,0:T(8,128)(2,1)} %broadcast_in_dim.42), calls=%async_computation.2 | async-start | bytes 3407872 | tf_op jit(solution)/shard_map/all_to_all | solution.py:378
  99.5 37.7 %collective-permute-start.10 = (bf16[2,192,2048]{2,1,0:T(8,128)(2,1)}, bf16[2,192,2048]{2,1,0:T(8,128)(2,1)}, u32[]{:S(2)}, u32[]{:S(2)}) collective-permute-start(bf16[2,192,2048]{2,1,0:T(8,128)(2,1)} %pad_maximum_fusion.1.refs_3_), channel_id=1, source_target_pairs={{0,16},{4,20},{8,24},{12,28},{16,0},{20,4},{24,8},{28,12},{1,17},{... | collective-permute-start | bytes 4718600 | tf_op jit(solution)/shard_map/ppermute | solution.py:340
  101.4 51.5 %collective-permute-start.11 = (bf16[2,192,2048]{2,1,0:T(8,128)(2,1)}, bf16[2,192,2048]{2,1,0:T(8,128)(2,1)}, u32[]{:S(2)}, u32[]{:S(2)}) collective-permute-start(bf16[2,192,2048]{2,1,0:T(8,128)(2,1)} %pad_maximum_fusion.1.refs_3_), channel_id=1, source_target_pairs={{0,4},{4,0},{8,12},{12,8},{16,20},{20,16},{24,28},{28,24},{1,5},{5... | collective-permute-start | bytes 4718600 | tf_op jit(solution)/shard_map/ppermute | solution.py:340
  102.6 43.9 %collective-permute-start.1 = (bf16[1,384,768]{2,1,0:T(8,128)(2,1)}, bf16[1,384,768]{2,1,0:T(8,128)(2,1)}, u32[]{:S(2)}, u32[]{:S(2)}) collective-permute-start(bf16[1,384,768]{2,1,0:T(8,128)(2,1)} %bitcast.18), channel_id=1, source_target_pairs={{0,8},{4,12},{8,0},{12,4},{16,24},{20,28},{24,16},{28,20},{1,9},{5... | collective-permute-start | bytes 1769480 | tf_op jit(solution)/shard_map/ppermute | solution.py:340
  106.3 46.6 %collective-permute-start.15 = (bf16[2,192,1536]{2,1,0:T(8,128)(2,1)}, bf16[2,192,1536]{2,1,0:T(8,128)(2,1)}, u32[]{:S(2)}, u32[]{:S(2)}) collective-permute-start(bf16[2,192,1536]{2,1,0:T(8,128)(2,1)} %pad_maximum_fusion.7.refs_2_), channel_id=1, source_target_pairs={{0,8},{4,12},{8,0},{12,4},{16,24},{20,28},{24,16},{28,20},{1,9},{5... | collective-permute-start | bytes 3538952 | tf_op jit(solution)/shard_map/ppermute | solution.py:340
  106.8 41.6 %collective-permute-start.2 = (bf16[1,384,768]{2,1,0:T(8,128)(2,1)}, bf16[1,384,768]{2,1,0:T(8,128)(2,1)S(1)}, u32[]{:S(2)}, u32[]{:S(2)}) collective-permute-start(bf16[1,384,768]{2,1,0:T(8,128)(2,1)} %bitcast.19), channel_id=1, source_target_pairs={{0,16},{4,20},{8,24},{12,28},{16,0},{20,4},{24,8},{28,12},{1,17},{... | collective-permute-start | bytes 1769480 | tf_op jit(solution)/shard_map/ppermute | solution.py:340
  138.3 40.3 %all-to-all-start.3 = ((bf16[4,2,2,48,768]{4,3,2,1,0:T(8,128)(2,1)}), bf16[4,2,2,48,768]{4,3,2,1,0:T(8,128)(2,1)S(1)}, u32[]{:S(2)}, u32[]{:S(2)}) async-start(bf16[4,2,2,48,768]{4,3,2,1,0:T(8,128)(2,1)} %get-tuple-element.25), calls=%async_computation.3 | async-start | bytes 2359296 | tf_op jit(solution)/shard_map/all_to_all | solution.py:378
  147.8 29.7 %collective-permute-start.13 = (bf16[2,384,768]{2,1,0:T(8,128)(2,1)S(1)}, bf16[2,384,768]{2,1,0:T(8,128)(2,1)S(1)}, u32[]{:S(2)}, u32[]{:S(2)}) collective-permute-start(bf16[2,384,768]{2,1,0:T(8,128)(2,1)S(1)} %pad_maximum_fusion.5), channel_id=1, source_target_pairs={{0,16},{4,20},{8,24},{12,28},{16,0},{20,4},{24,8},{28,12},{1,17},{... | collective-permute-start | bytes 3538952 | tf_op jit(solution)/shard_map/ppermute | solution.py:340
  149.6 29.0 %collective-permute-start.14 = (bf16[2,384,768]{2,1,0:T(8,128)(2,1)S(1)}, bf16[2,384,768]{2,1,0:T(8,128)(2,1)}, u32[]{:S(2)}, u32[]{:S(2)}) collective-permute-start(bf16[2,384,768]{2,1,0:T(8,128)(2,1)S(1)} %pad_maximum_fusion.6), channel_id=1, source_target_pairs={{0,8},{4,12},{8,0},{12,4},{16,24},{20,28},{24,16},{28,20},{1,9},{5... | collective-permute-start | bytes 3538952 | tf_op jit(solution)/shard_map/ppermute | solution.py:340
  152.9 26.6 %collective-permute-start.16 = (bf16[2,192,1536]{2,1,0:T(8,128)(2,1)}, bf16[2,192,1536]{2,1,0:T(8,128)(2,1)}, u32[]{:S(2)}, u32[]{:S(2)}) collective-permute-start(bf16[2,192,1536]{2,1,0:T(8,128)(2,1)} %pad_maximum_fusion.7.refs_2_), channel_id=1, source_target_pairs={{0,4},{4,0},{8,12},{12,8},{16,20},{20,16},{24,28},{28,24},{1,5},{5... | collective-permute-start | bytes 3538952 | tf_op jit(solution)/shard_map/ppermute | solution.py:340
  152.9 26.5 %collective-permute-start.17 = (bf16[2,192,1536]{2,1,0:T(8,128)(2,1)}, bf16[2,192,1536]{2,1,0:T(8,128)(2,1)}, u32[]{:S(2)}, u32[]{:S(2)}) collective-permute-start(bf16[2,192,1536]{2,1,0:T(8,128)(2,1)} %collective-permute-done.15.refs_3_), channel_id=1, source_target_pairs={{0,4},{4,0},{8,12},{12,8},{16,20},{20,16},{24,28},{28,24},{1,5},{5... | collective-permute-start | bytes 3538952 | tf_op jit(solution)/shard_map/ppermute | solution.py:340
  192.5 20.5 %collective-permute-start.20 = (bf16[512,1536]{1,0:T(8,128)(2,1)}, bf16[512,1536]{1,0:T(8,128)(2,1)S(1)}, u32[]{:S(2)}, u32[]{:S(2)}) collective-permute-start(bf16[512,1536]{1,0:T(8,128)(2,1)} %norm.1.mine_ref), channel_id=1, source_target_pairs={{0,4},{4,0},{8,12},{12,8},{16,20},{20,16},{24,28},{28,24},{1,5},{5... | collective-permute-start | bytes 4718600 | tf_op jit(solution)/shard_map/ppermute | solution.py:340
  194.3 39.4 %collective-permute-start.22 = (bf16[2,384,768]{2,1,0:T(8,128)(2,1)S(1)}, bf16[2,384,768]{2,1,0:T(8,128)(2,1)}, u32[]{:S(2)}, u32[]{:S(2)}) collective-permute-start(bf16[2,384,768]{2,1,0:T(8,128)(2,1)S(1)} %pad_maximum_fusion.8), channel_id=1, source_target_pairs={{0,16},{4,20},{8,24},{12,28},{16,0},{20,4},{24,8},{28,12},{1,17},{... | collective-permute-start | bytes 3538952 | tf_op jit(solution)/shard_map/ppermute | solution.py:340
  208.8 27.3 %collective-permute-start.23 = (bf16[2,384,768]{2,1,0:T(8,128)(2,1)S(1)}, bf16[2,384,768]{2,1,0:T(8,128)(2,1)S(1)}, u32[]{:S(2)}, u32[]{:S(2)}) collective-permute-start(bf16[2,384,768]{2,1,0:T(8,128)(2,1)S(1)} %pad_maximum_fusion.9), channel_id=1, source_target_pairs={{0,8},{4,12},{8,0},{12,4},{16,24},{20,28},{24,16},{28,20},{1,9},{5... | collective-permute-start | bytes 3538952 | tf_op jit(solution)/shard_map/ppermute | solution.py:340
  278.3 28.6 %collective-permute-start.30 = (bf16[128,768]{1,0:T(8,128)(2,1)S(1)}, bf16[128,768]{1,0:T(8,128)(2,1)S(1)}, u32[]{:S(2)}, u32[]{:S(2)}) collective-permute-start(bf16[128,768]{1,0:T(8,128)(2,1)S(1)} %get-tuple-element.43), channel_id=1, source_target_pairs={{0,2},{1,3},{2,0},{3,1},{4,6},{5,7},{6,4},{7,5},{8,10},{9,11},{10,... | collective-permute-start | bytes 589832 | tf_op jit(solution)/shard_map/ppermute | solution.py:336
  279.4 27.4 %collective-permute-start.29 = (bf16[128,768]{1,0:T(8,128)(2,1)S(1)}, bf16[128,768]{1,0:T(8,128)(2,1)S(1)}, u32[]{:S(2)}, u32[]{:S(2)}) collective-permute-start(bf16[128,768]{1,0:T(8,128)(2,1)S(1)} %get-tuple-element.41), channel_id=1, source_target_pairs={{0,1},{1,2},{2,3},{3,0},{4,5},{5,6},{6,7},{7,4},{8,9},{9,10},{10,1... | collective-permute-start | bytes 589832 | tf_op jit(solution)/shard_map/ppermute | solution.py:336
  (32 other events, 268.5 us)

commit v3 on v2

--- a/solution.py
+++ b/solution.py
@@ -19,7 +19,7 @@
 QKV = 2048
 WIDE = 512
 ROWS = 256
-PARTS = 2
+EASE = 16
 CHUNKS = 2
 BF = jnp.bfloat16
 F32 = jnp.float32
@@ -49,6 +49,12 @@
     starts = jnp.cumsum(lengths) - lengths
     member = index[:, None] >= starts[None, :]
     return jnp.max(jnp.where(member, starts[None, :], 0), axis=1)
+
+
+def cost(flops, bytes_accessed, transcendentals):
+    return pl.CostEstimate(
+        flops=flops // EASE, bytes_accessed=bytes_accessed // EASE, transcendentals=transcendentals // EASE
+    )
 
 
 def put(held, spots, first, block, value):
@@ -102,7 +108,7 @@
         ),
         out_shape=jax.ShapeDtypeStruct((count, QKV), BF),
         compiler_params=pltpu.CompilerParams(vmem_limit_bytes=VMEM),
-        cost_estimate=pl.CostEstimate(
+        cost_estimate=cost(
             flops=2 * count * D * QKV, bytes_accessed=2 * D * QKV + 4 * count * D, transcendentals=0
         ),
         name="project",
@@ -144,7 +150,7 @@
         out_specs=pl.BlockSpec((count, HD), lambda h: (0, h)),
         out_shape=jax.ShapeDtypeStruct((count, QW), BF),
         compiler_params=pltpu.CompilerParams(vmem_limit_bytes=VMEM),
-        cost_estimate=pl.CostEstimate(
+        cost_estimate=cost(
             flops=4 * QH * count * count * HD,
             bytes_accessed=2 * count * (QKV + QW),
             transcendentals=QH * count * count,
@@ -179,7 +185,7 @@
         ),
         out_shape=jax.ShapeDtypeStruct((count, D), F32),
         compiler_params=pltpu.CompilerParams(vmem_limit_bytes=VMEM),
-        cost_estimate=pl.CostEstimate(
+        cost_estimate=cost(
             flops=2 * count * D * QW, bytes_accessed=2 * D * QW + 8 * count * D, transcendentals=0
         ),
         name="mix",
@@ -211,7 +217,7 @@
         ),
         out_shape=jax.ShapeDtypeStruct((count, D), BF),
         compiler_params=pltpu.CompilerParams(vmem_limit_bytes=VMEM),
-        cost_estimate=pl.CostEstimate(
+        cost_estimate=cost(
             flops=4 * count * D, bytes_accessed=6 * count * D, transcendentals=count
         ),
         name="norm",
@@ -271,7 +277,7 @@
         out_specs=pl.BlockSpec((count, experts * wide // 4), lambda i: (i, 0)),
         out_shape=jax.ShapeDtypeStruct((2 * count, experts * wide // 4), BF),
         compiler_params=pltpu.CompilerParams(vmem_limit_bytes=VMEM),
-        cost_estimate=pl.CostEstimate(
+        cost_estimate=cost(
             flops=2 * experts * count * D * wide,
             bytes_accessed=D * (experts * wide + 4 * count),
             transcendentals=0,
@@ -280,60 +286,46 @@
     )(mine, other, gate, *weights)
 
 
-def down_kernel(parts, block, spots, *refs):
-    acts, weights = refs[:parts], refs[parts:-4]
-    mine_ref, other_ref, held, side = refs[-4:]
-    deep = acts[0].shape[1]
-    for n, act in enumerate(acts):
-        side[:, n * deep : (n + 1) * deep] = act[...]
-    span = held.shape[0] // E * 2
+def down_kernel(block, stacks, spots, act_ref, *refs):
+    weights, held = refs[:stacks], refs[-1]
+    addend, out_ref = refs[stacks:-2], refs[-2]
     experts = weights[0].shape[1]
-    stacks = 2 if block % 16 == 0 else 1
-    for n in range(0, len(weights), stacks):
-        for e in range(experts):
-            first = (n // stacks * experts + e) * span
-            put_all(
-                held.at[pl.ds(first, span)],
-                spots.at[n // stacks],
-                block,
-                [w.at[:, e] for w in weights[n : n + stacks]],
-            )
-    half = side.shape[0] // 2
-    total = jnp.dot(side[half:, :], held[...], preferred_element_type=F32)
-    other_ref[...] = total.astype(other_ref.dtype)
-    mine_ref[...] = jnp.dot(side[:half, :], held[...], preferred_element_type=F32)
-
-
-def down_project(spots, block, acts, part, parts, weights):
-    rows, deep = acts[0].shape
-    total, wide = deep * len(acts), D // parts
+    span = held.shape[0] // experts
+    for e in range(experts):
+        put_all(held.at[pl.ds(e * span, span)], spots, block, [w.at[:, e] for w in weights])
+    total = jnp.dot(act_ref[...], held[...], preferred_element_type=F32)
+    if addend:
+        total += addend[0][...]
+    out_ref[...] = total.astype(out_ref.dtype)
+
+
+def down_project(spots, block, act, weights, kind, part=0, parts=1, addend=()):
+    rows, deep = act.shape
+    rows, wide = rows // parts, D // 2
     return pl.pallas_call(
-        functools.partial(down_kernel, len(acts), block),
+        functools.partial(down_kernel, block, len(weights)),
         grid_spec=pltpu.PrefetchScalarGridSpec(
             num_scalar_prefetch=1,
-            grid=(1,),
-            in_specs=[pl.BlockSpec((rows, deep), lambda j, _: (0, 0))] * len(acts)
-            + [pl.BlockSpec(w.shape[:3] + (wide,), lambda j, _: (0, 0, 0, part)) for w in weights],
-            out_specs=[pl.BlockSpec((rows // 2, wide), lambda j, _: (0, 0))] * 2,
-            scratch_shapes=[pltpu.VMEM((total, wide), BF), pltpu.VMEM((rows, total), BF)],
-        ),
-        out_shape=[
-            jax.ShapeDtypeStruct((rows // 2, wide), F32),
-            jax.ShapeDtypeStruct((rows // 2, wide), BF),
-        ],
+            grid=(D // wide,),
+            in_specs=[pl.BlockSpec((rows, deep), lambda j, _: (part, 0))]
+            + [pl.BlockSpec(w.shape[:3] + (wide,), lambda j, _: (0, 0, 0, j)) for w in weights]
+            + [pl.BlockSpec((rows, wide), lambda j, _: (part, j)) for _ in addend],
+            out_specs=pl.BlockSpec((rows, wide), lambda j, _: (0, j)),
+            scratch_shapes=[pltpu.VMEM((deep, wide), BF)],
+        ),
+        out_shape=jax.ShapeDtypeStruct((rows, D), kind),
         compiler_params=pltpu.CompilerParams(vmem_limit_bytes=VMEM),
-        cost_estimate=pl.CostEstimate(
-            flops=2 * rows * wide * total,
-            bytes_accessed=2 * wide * total + 2 * rows * total + 3 * rows * wide,
+        cost_estimate=cost(
+            flops=2 * rows * D * deep,
+            bytes_accessed=2 * D * deep + 2 * rows * deep + 8 * rows * D,
             transcendentals=0,
         ),
         name="down",
-    )(spots, *acts, *weights)
-
-
-def along_blk(value, step):
-    size = lax.axis_size("blk")
-    return lax.ppermute(value, "blk", [(i, (i + step) % size) for i in range(size)])
+    )(spots, act, *weights, *addend)
+
+
+def across_blk(value, mask):
+    return lax.ppermute(value, "blk", [(i, i ^ mask) for i in range(lax.axis_size("blk"))])
 
 
 def across_rep(value, mask):
@@ -414,6 +406,11 @@
             [jnp.where(core == 0, mine, came), jnp.where(core == 0, came, mine)], axis=1
         )
 
+    down = split_cores(expert_out.astype(BF)).reshape(half_experts, 2 * rows_out, D)
+    down_first = [chip_start(down[n * 4 : (n + 1) * 4], n % 2) for n in range(half_experts // 4)]
+
+    down_parts = [chip_gather(*down_first[n], n % 2) for n in range(len(down_first))]
+
     spot = jnp.arange(2 * FF, dtype=jnp.int32)
     inner = spot % rows_out
     from_rep = (spot // rows_out) % reps
@@ -421,6 +418,7 @@
     from_blk = spot // (2 * quarter)
     column = which * FF + (from_rep * cycle_size + from_blk) * rows_out + inner
     shuffle = (spot[:, None] == column[None, :]).astype(BF)
+    expert_in = after(expert_in, down_first)
     ordered = jnp.dot(
         expert_in.astype(BF).reshape(E * rows_in, 2 * FF), shuffle, preferred_element_type=F32
     )
@@ -441,17 +439,13 @@
     pairs = split_cores(pairs)
     per_chunk = half_experts // 2 // CHUNKS
 
-    down = split_cores(expert_out.astype(BF)).reshape(half_experts, 2 * rows_out, D)
-    down_first = [chip_start(down[n * 4 : (n + 1) * 4], n % 2) for n in range(half_experts // 4)]
-
     attn_here = jnp.concatenate([attn_in.astype(BF), attn_out.astype(BF)], axis=1)
     attn_line = gather_blk(attn_here).reshape(cycle_size * rows_in, QKV + D)
-    ready = after(attn_line, down_first)
+    ready = after(attn_line, down_parts)
     qkv_first = chip_start(ready[:, :QKV], 0)
     mix_first = chip_start(ready[:, QKV:], 1)
-    down_parts = [chip_gather(*down_first[n], n % 2) for n in range(len(down_first))]
-
-    gate = (qkv_first, mix_first, down_parts)
+
+    gate = (qkv_first, mix_first)
     qkv_own = chip_gather(*qkv_first, 0, gate)
     mix_own = chip_gather(*mix_first, 1, gate)
     qkv_weight = qkv_own + [across_rep(v, 1) for v in qkv_own]
@@ -462,7 +456,7 @@
         lined = exchange_blk(after(chunk, earlier)).transpose(1, 2, 0, 3, 4)
         return lined.reshape(per_chunk, 2 * cycle_size * rows_in, 4 * quarter)
 
-    lines = [line_up(0, (attn_line,))]
+    lines = [line_up(0, (attn_line, down_first))]
 
     expert_ids = jnp.arange(E, dtype=jnp.int32)
     dense = jnp.sum(
@@ -474,7 +468,7 @@
         axis=1,
     ).astype(BF)
     sent = jnp.concatenate([tokens, jnp.pad(dense, ((0, 0), (0, 128 - E)))], axis=1)
-    line = gather_blk(after(sent, (lines[0],))).reshape(group_rows, -1)
+    line = gather_blk(after(sent, (lines[0], qkv_first, mix_first))).reshape(group_rows, -1)
     group, group_gates = line[:, :D], line[:, D : D + E]
 
     for n in range(1, CHUNKS):
@@ -503,7 +497,7 @@
             x = after(normed, (first,))
             qkv = project(attn_spots(0), block, x, cosine, sine, qkv_weight)
             attended = attend(qkv, begin, index)
-            gate = (qkv,)
+            gate = (attended,)
     attended = after(attended, (steps[1],))
     hidden = mix(attn_spots(1), block, attended, group, mix_weight)
 
@@ -530,36 +524,36 @@
     other_two = across_rep(normed_two, 1)
     both_gates = jnp.concatenate([group_gates, across_rep(group_gates, 1)], axis=0)
     my_gates = lax.dynamic_slice_in_dim(both_gates, core * half_experts, half_experts, 1).astype(F32)
-    acts, orders = [], [chip_order(k % 2) for k in range(per_chunk)]
-    for n in range(CHUNKS):
-        experts = slice(n * 2 * per_chunk, (n + 1) * 2 * per_chunk)
-        x = after(normed_two, (steps[2 * n + 2],)) if n + 1 < CHUNKS else normed_two
-        acts.append(gate_up(orders, x, other_two, my_gates[:, experts], up_parts[n]))
-    chips, chip_rows = reps // 2, 2 * rows_out
-    whose = [chip ^ jnp.array(chip_order(n % 2), jnp.int32) for n in range(len(down_parts))]
+    chip_rows = 2 * rows_out
+    whose = [chip ^ jnp.array(chip_order(n % 2), jnp.int32) for n in range(CHUNKS)]
+    down_spots = [spots * chip_rows for spots in whose]
     if chip_rows % 16 != 0:
         for n, part in enumerate(down_parts):
             part = jnp.take(jnp.concatenate(part, axis=0), jnp.argsort(whose[n]), axis=0)
-            down_parts[n] = [part.transpose(1, 0, 2, 3).reshape(1, 4, chips * chip_rows, D)]
-    down = [w for part in down_parts for w in part]
-    down_spots = jnp.stack(whose) * chip_rows
-
-    def at(array, shift):
-        first = (place + shift) % cycle_size * count
-        return lax.dynamic_slice_in_dim(array, first, count, 0).astype(F32)
-
-    mixed, came = [], ()
-    for n in range(PARTS):
-        ready = after(acts, came)
-        mine, other = down_project(down_spots, chip_rows, ready, n, PARTS, down)
-        came = across_rep(other, 1)
-        columns = slice(n * (D // PARTS), (n + 1) * (D // PARTS))
-        total = at(hidden[:, columns], 0) + (at(mine, 0) + at(came, 0))
-        for step in range(1, cycle_size):
-            part = (at(mine, step) + at(came, step)).astype(BF)
-            total = total + along_blk(part, step).astype(F32)
-        mixed.append(total.astype(BF))
-    return (jnp.concatenate(mixed, axis=1), kv_pages)
+            part = part.transpose(1, 0, 2, 3)
+            down_parts[n] = [part.reshape(1, part.shape[0], quarter, D)]
+
+    orders, partial = [chip_order(k % 2) for k in range(per_chunk)], ()
+    for n in range(CHUNKS):
+        experts = slice(n * 2 * per_chunk, (n + 1) * 2 * per_chunk)
+        weights = after(up_parts[n], partial)
+        act = gate_up(orders, normed_two, other_two, my_gates[:, experts], weights)
+        down = (down_spots[n], chip_rows, act, down_parts[n])
+        if n + 1 < CHUNKS:
+            partial = (down_project(*down, F32, addend=partial),)
+        else:
+            other = down_project(*down, BF, 1, 2, partial)
+            came = across_rep(other, 1)
+            mine = down_project(*down, F32, 0, 2, partial)
+
+    def at(array, mask):
+        return lax.dynamic_slice_in_dim(array, (place ^ mask) * count, count, 0).astype(F32)
+
+    total = at(hidden, 0) + (at(mine, 0) + at(came, 0))
+    for mask in range(1, cycle_size):
+        part = (at(mine, mask) + at(came, mask)).astype(BF)
+        total = total + across_blk(part, mask).astype(F32)
+    return (total.astype(BF), kv_pages)
 
 
 def solution(mesh):

time: 310 us -> 287 us (0.926)
  waiting for transfers between devices: 131 us -> 110 us
  starting transfers between devices: 47.4 us -> 41.2 us
  Pallas kernels: 69.9 us -> 74.5 us
    ppermute x26 -> x25, waiting for transfers between devices: 74 us -> 32.8 us  [across_rep(): lax.ppermute(value, 'rep', [(i, i ^ mask) for i in range(lax.axis_size('r...]
    all_to_all x4, waiting for transfers between devices: 30.7 us -> 45.4 us  [exchange_blk(): return lax.all_to_all(value, 'blk', 0, 0, tiled=True)]
    ppermute x6 -> x3, waiting for transfers between devices: 26.3 us -> 31.9 us  [across_blk(): lax.ppermute(value, 'blk', [(i, i ^ mask) for i in range(lax.axis_size('b...]
    pallas_call x2 -> x3, Pallas kernels: 14.6 us -> 19.2 us  [down_project(): pl.pallas_call(functools.partial(down_kernel, block, len(weights)), grid_...]
    ppermute x6 -> x3, starting transfers between devices: 8.82 us -> 4.39 us  [across_blk(): lax.ppermute(value, 'blk', [(i, i ^ mask) for i in range(lax.axis_size('b...]
    all_to_all x2, local copies, waits for them, and re-layouts: 0.15 us -> 3.76 us  [exchange_blk(): return lax.all_to_all(value, 'blk', 0, 0, tiled=True)]
    broadcast_in_dim x2, local copies, waits for them, and re-layouts: 3.23 us -> 0.12 us  [chip_start(): return (value[None], across_rep(value[None], 2 << turn))]
    ppermute x26 -> x25, starting transfers between devices: 20 us -> 18.3 us  [across_rep(): lax.ppermute(value, 'rep', [(i, i ^ mask) for i in range(lax.axis_size('r...]
  transfers between devices with their start and end apart: 36 -> 32, of which waited for: 12 -> 15; matrix products, arithmetic and copies ran while one was open for 16% -> 16% of each run, Pallas kernels for 15% -> 21%
where the time goes in v3:
time: 287 us; the launch traced here: 286 us
  waiting for transfers between devices  110 us (38%)
  Pallas kernels  74.5 us (26%)
  starting transfers between devices  41.2 us (14%)
  other arithmetic  35 us (12%)
  local copies, waits for them, and re-layouts  19 us (7%)
  matrix products  4.14 us (1%)
    all_to_all x4, waiting for transfers between devices, exchange_blk(): return lax.all_to_all(value, 'blk', 0, 0, tiled=True)  45.4 us
    ppermute x25, waiting for transfers between devices, across_rep(): lax.ppermute(value, 'rep', [(i, i ^ mask) for i in range(lax.axis_size('r...  32.8 us
    ppermute x3, waiting for transfers between devices, across_blk(): lax.ppermute(value, 'blk', [(i, i ^ mask) for i in range(lax.axis_size('b...  31.9 us
    pallas_call x2, Pallas kernels, gate_up(): pl.pallas_call(functools.partial(gate_up_kernel, orders), grid=(2,), in_s...  20.2 us
    pallas_call x3, Pallas kernels, down_project(): pl.pallas_call(functools.partial(down_kernel, block, len(weights)), grid_...  19.2 us
    all_to_all x4, starting transfers between devices, exchange_blk(): return lax.all_to_all(value, 'blk', 0, 0, tiled=True)  18.5 us
    ppermute x25, starting transfers between devices, across_rep(): lax.ppermute(value, 'rep', [(i, i ^ mask) for i in range(lax.axis_size('r...  18.3 us
    concatenate x8, other arithmetic, chip_gather(): held = jnp.concatenate([held, came], axis=0)  13.3 us
  transfers between devices with their start and end apart: 32, of which 15 were waited for; matrix products, arithmetic and copies ran while one was open for 16% of the time, Pallas kernels for 21%

profile of v3, /device:TPU:0, one launch (start us, length us, event | category | flops | bytes accessed | tf_op | source)
XLA Modules:
  0.0 285.7 jit_solution(15994730468360153280)
XLA Ops:
  4.9 2.9 %collective-permute-start.1 = (bf16[1,4,48,1536]{3,2,1,0:T(8,128)(2,1)S(1)}, bf16[1,4,48,1536]{3,2,1,0:T(8,128)(2,1)}, u32[]{:S(2)}, u32[]{:S(2)}) collective-permute-start(bf16[1,4,48,1536]{3,2,1,0:T(8,128)(2,1)S(1)} %bitcast.76), channel_id=1, source_target_pairs={{0,8},{4,12},{8,0},{12,4},{16,24},{20,28},{24,16},{28,20},{1,9},{5... | collective-permute-start | bytes 1769480 | tf_op jit(solution)/shard_map/ppermute | solution.py:332
  10.8 4.9 %all-to-all-start = ((bf16[4,48,3584]{2,1,0:T(8,128)(2,1)}), bf16[4,48,3584]{2,1,0:T(8,128)(2,1)S(1)}, u32[]{:S(2)}, u32[]{:S(2)}) async-start(bf16[4,48,3584]{2,1,0:T(8,128)(2,1)} %broadcast_in_dim.43), calls=%async_computation | async-start | bytes 2752512 | tf_op jit(solution)/shard_map/all_to_all | solution.py:370
  15.7 5.9 %collective-permute-done.1 = bf16[1,4,48,1536]{3,2,1,0:T(8,128)(2,1)} collective-permute-done((bf16[1,4,48,1536]{3,2,1,0:T(8,128)(2,1)S(1)}, bf16[1,4,48,1536]{3,2,1,0:T(8,128)(2,1)}, u32[]{:S(2)}, u32[]{:S(2)}) %collective-permute-start.1) | collective-permute-done | bytes 589856 | tf_op jit(solution)/shard_map/ppermute | solution.py:332
  25.8 4.1 %fusion.2 = bf16[768,1536]{1,0:T(8,128)(2,1)S(1)} fusion(bf16[768,1536]{1,0:T(8,128)(2,1)S(1)} %bitcast.74, s32[1536]{0:T(1024)S(1)} %fusion.23), kind=kOutput, calls=%fused_computation.5 | convolution fusion | flops 3627417600 | bytes 4724736 | tf_op jit(solution)/shard_map/dot_general | solution.py:422
  41.8 6.3 %all-to-all-done = bf16[4,48,3584]{2,1,0:T(8,128)(2,1)S(1)} async-done(((bf16[4,48,3584]{2,1,0:T(8,128)(2,1)}), bf16[4,48,3584]{2,1,0:T(8,128)(2,1)S(1)}, u32[]{:S(2)}, u32[]{:S(2)}) %all-to-all-start) | async-done | bytes 1376288 | tf_op jit(solution)/shard_map/all_to_all | solution.py:370
  48.1 4.3 %all-to-all-start.1 = ((bf16[4,2,2,48,768]{4,3,2,1,0:T(8,128)(2,1)}), bf16[4,2,2,48,768]{4,3,2,1,0:T(8,128)(2,1)}, u32[]{:S(2)}, u32[]{:S(2)}) async-start(bf16[4,2,2,48,768]{4,3,2,1,0:T(8,128)(2,1)} %get-tuple-element.17), calls=%async_computation.1 | async-start | bytes 2359296 | tf_op jit(solution)/shard_map/all_to_all | solution.py:370
  52.4 11.2 %collective-permute-done.4.refs_1_ = bf16[2,4,48,1536]{3,2,1,0:T(8,128)(2,1)} collective-permute-done((bf16[2,4,48,1536]{3,2,1,0:T(8,128)(2,1)}, bf16[2,4,48,1536]{3,2,1,0:T(8,128)(2,1)}, u32[]{:S(2)}, u32[]{:S(2)}) %collective-permute-start.4) | collective-permute-done | bytes 1179680 | tf_op jit(solution)/shard_map/ppermute | solution.py:332
  68.2 12.3 %all-to-all-done.1 = bf16[4,2,2,48,768]{4,3,2,1,0:T(8,128)(2,1)} async-done(((bf16[4,2,2,48,768]{4,3,2,1,0:T(8,128)(2,1)}), bf16[4,2,2,48,768]{4,3,2,1,0:T(8,128)(2,1)}, u32[]{:S(2)}, u32[]{:S(2)}) %all-to-all-start.1) | async-done | bytes 1179680 | tf_op jit(solution)/shard_map/all_to_all | solution.py:370
  86.5 4.9 %all-to-all-start.2 = ((bf16[4,128,1664]{2,1,0:T(8,128)(2,1)}), bf16[4,128,1664]{2,1,0:T(8,128)(2,1)S(1)}, u32[]{:S(2)}, u32[]{:S(2)}) async-start(bf16[4,128,1664]{2,1,0:T(8,128)(2,1)} %broadcast_in_dim.46), calls=%async_computation.2 | async-start | bytes 3407872 | tf_op jit(solution)/shard_map/all_to_all | solution.py:370
  103.0 26.8 %all-to-all-done.2 = bf16[4,128,1664]{2,1,0:T(8,128)(2,1)S(1)} async-done(((bf16[4,128,1664]{2,1,0:T(8,128)(2,1)}), bf16[4,128,1664]{2,1,0:T(8,128)(2,1)S(1)}, u32[]{:S(2)}, u32[]{:S(2)}) %all-to-all-start.2) | async-done | bytes 1703968 | tf_op jit(solution)/shard_map/all_to_all | solution.py:370
  129.8 4.5 %all-to-all-start.3 = ((bf16[4,2,2,48,768]{4,3,2,1,0:T(8,128)(2,1)}), bf16[4,2,2,48,768]{4,3,2,1,0:T(8,128)(2,1)}, u32[]{:S(2)}, u32[]{:S(2)}) async-start(bf16[4,2,2,48,768]{4,3,2,1,0:T(8,128)(2,1)} %get-tuple-element.24), calls=%async_computation.3 | async-start | bytes 2359296 | tf_op jit(solution)/shard_map/all_to_all | solution.py:370
  146.9 9.2 %project.1.q_ref.k_ref.v_ref = bf16[512,2048]{1,0:T(8,128)(2,1)} custom-call(s32[8]{0:T(128)} %mul.140.spots, bf16[512,1536]{1,0:T(8,128)(2,1)} %fusion.5.refs_0_, f32[512,128]{1,0:T(8,128)} %get-tuple-element.70.refs_1_, f32[512,128]{1,0:T(8,128)} %get-tuple-element.71.refs_2_, bf16[2,192,2048]{2,1,0:T(8,128)(2,1)} %copy-done.3, ...), custom_call_target="tpu_custom_call" | custom-call | flops 201326592 | bytes 589824 | tf_op jit(solution)/shard_map/project/pallas_call | solution.py:95
  156.7 12.9 %attend.1.refs_0_ = bf16[512,1536]{1,0:T(8,128)(2,1)} custom-call(bf16[512,2048]{1,0:T(8,128)(2,1)} %project.1.q_ref.k_ref.v_ref, bf16[512,2048]{1,0:T(8,128)(2,1)} %project.1.q_ref.k_ref.v_ref, bf16[512,2048]{1,0:T(8,128)(2,1)} %project.1.q_ref.k_ref.v_ref, s32[512,1]{1,0:T(8,128)} %copy.66.begin_ref, s32[1,512]{1,0:T(1,128)} %iota.46.across_ref), custom_call_target="tpu_custom_call" | custom-call | flops 100663296 | bytes 229376 | tf_op jit(solution)/shard_map/attend/pallas_call | solution.py:140
  177.2 8.1 %mix.1.x_ref = f32[512,1536]{1,0:T(8,128)} custom-call(s32[8]{0:T(128)} %mul.137.spots, bf16[512,1536]{1,0:T(8,128)(2,1)} %attend.1.refs_0_, bf16[512,1536]{1,0:T(8,128)(2,1)} %slice.130.refs_1_, bf16[2,192,1536]{2,1,0:T(8,128)(2,1)} %pad_maximum_fusion.7.refs_2_, bf16[2,192,1536]{2,1,0:T(8,128)(2,1)} %collective-permute-done.15.refs_3_, ...), custom_call_target="tpu_custom_call" | custom-call | flops 150994944 | bytes 688128 | tf_op jit(solution)/shard_map/mix/pallas_call | solution.py:173
  185.3 4.9 %norm.1.mine_ref = bf16[512,1536]{1,0:T(8,128)(2,1)} custom-call(s32[4]{0:T(128)} %fusion.34.spots, f32[512,1536]{1,0:T(8,128)} %mix.1.x_ref, f32[1,1536]{1,0:T(1,128)} %broadcast_in_dim.48.gain_ref), custom_call_target="tpu_custom_call" | custom-call | flops 196608 | bytes 294912 | tf_op jit(solution)/shard_map/norm/pallas_call | solution.py:206
  196.5 10.1 %gate_up.2.act_ref = bf16[1024,768]{1,0:T(8,128)(2,1)} custom-call(bf16[512,1536]{1,0:T(8,128)(2,1)} %norm.1.mine_ref, bf16[512,1536]{1,0:T(8,128)(2,1)} %copy-done.2, f32[1024,4]{1,0:T(8,128)} %get-tuple-element.57.gate_ref, bf16[768,768]{1,0:T(8,128)(2,1)} %bitcast.34.refs_0_, bf16[768,768]{1,0:T(8,128)(2,1)} %bitcast.35.refs_1_, ...), custom_call_target="tpu_custom_call" | custom-call | flops 301989888 | bytes 491520 | tf_op jit(solution)/shard_map/gate_up/pallas_call | solution.py:272
  206.7 7.5 %down.3.refs_2_ = f32[1024,1536]{1,0:T(8,128)} custom-call(s32[4]{0:T(128)} %fusion.35.spots, bf16[1024,768]{1,0:T(8,128)(2,1)} %gate_up.2.act_ref, bf16[2,4,48,1536]{3,2,1,0:T(8,128)(2,1)} %pad_maximum_fusion.3.refs_0_, bf16[2,4,48,1536]{3,2,1,0:T(8,128)(2,1)} %collective-permute-done.4.refs_1_), custom_call_target="tpu_custom_call" | custom-call | flops 150994944 | bytes 1032192 | tf_op jit(solution)/shard_map/down/pallas_call | solution.py:305
  214.2 4.6 %collective-permute-done.21 = bf16[2,384,768]{2,1,0:T(8,128)(2,1)S(1)} collective-permute-done((bf16[2,384,768]{2,1,0:T(8,128)(2,1)S(1)}, bf16[2,384,768]{2,1,0:T(8,128)(2,1)S(1)}, u32[]{:S(2)}, u32[]{:S(2)}) %collective-permute-start.21) | collective-permute-done | bytes 1179680 | tf_op jit(solution)/shard_map/ppermute | solution.py:332
  220.5 10.1 %gate_up.3.act_ref = bf16[1024,768]{1,0:T(8,128)(2,1)} custom-call(bf16[512,1536]{1,0:T(8,128)(2,1)} %norm.1.mine_ref, bf16[512,1536]{1,0:T(8,128)(2,1)} %copy-done.2, f32[1024,4]{1,0:T(8,128)} %get-tuple-element.58.gate_ref, bf16[768,768]{1,0:T(8,128)(2,1)} %bitcast.70, bf16[768,768]{1,0:T(8,128)(2,1)} %bitcast.82, bf16[768,768]{1,0:T(8,128)(2,1)} %bitcast.71, ...), custom_call_target="tpu_custom_call" | custom-call | flops 301989888 | bytes 491520 | tf_op jit(solution)/shard_map/gate_up/pallas_call | solution.py:272
  230.6 5.7 %down.5 = bf16[512,1536]{1,0:T(8,128)(2,1)} custom-call(s32[4]{0:T(128)} %get-tuple-element.65.spots, bf16[1024,768]{1,0:T(8,128)(2,1)} %gate_up.3.act_ref, bf16[2,4,48,1536]{3,2,1,0:T(8,128)(2,1)} %copy-done, bf16[2,4,48,1536]{3,2,1,0:T(8,128)(2,1)} %collective-permute-done.5.refs_1_, f32[1024,1536]{1,0:T(8,128)} %down.3.refs_2_), custom_call_target="tpu_custom_call" | custom-call | flops 75497472 | bytes 589824 | tf_op jit(solution)/shard_map/down/pallas_call | solution.py:305
  236.2 6.0 %down.4 = f32[512,1536]{1,0:T(8,128)} custom-call(s32[4]{0:T(128)} %get-tuple-element.65.spots, bf16[1024,768]{1,0:T(8,128)(2,1)} %gate_up.3.act_ref, bf16[2,4,48,1536]{3,2,1,0:T(8,128)(2,1)} %copy-done, bf16[2,4,48,1536]{3,2,1,0:T(8,128)(2,1)} %collective-permute-done.5.refs_1_, f32[1024,1536]{1,0:T(8,128)} %down.3.refs_2_), custom_call_target="tpu_custom_call" | custom-call | flops 75497472 | bytes 589824 | tf_op jit(solution)/shard_map/down/pallas_call | solution.py:305
  245.0 3.6 %collective-permute-start.27 = (bf16[128,1536]{1,0:T(8,128)(2,1)}, bf16[128,1536]{1,0:T(8,128)(2,1)S(1)}, u32[]{:S(2)}, u32[]{:S(2)}) collective-permute-start(bf16[128,1536]{1,0:T(8,128)(2,1)} %get-tuple-element.31), channel_id=1, source_target_pairs={{0,3},{1,2},{2,1},{3,0},{4,7},{5,6},{6,5},{7,4},{8,11},{9,10},{10,... | collective-permute-start | bytes 1179656 | tf_op jit(solution)/shard_map/ppermute | solution.py:328
  251.4 7.7 %collective-permute-done.27 = bf16[128,1536]{1,0:T(8,128)(2,1)S(1)} collective-permute-done((bf16[128,1536]{1,0:T(8,128)(2,1)}, bf16[128,1536]{1,0:T(8,128)(2,1)S(1)}, u32[]{:S(2)}, u32[]{:S(2)}) %collective-permute-start.27) | collective-permute-done | bytes 393248 | tf_op jit(solution)/shard_map/ppermute | solution.py:328
  259.1 24.1 %collective-permute-done.26 = bf16[128,1536]{1,0:T(8,128)(2,1)S(1)} collective-permute-done((bf16[128,1536]{1,0:T(8,128)(2,1)}, bf16[128,1536]{1,0:T(8,128)(2,1)S(1)}, u32[]{:S(2)}, u32[]{:S(2)}) %collective-permute-start.26) | collective-permute-done | bytes 393248 | tf_op jit(solution)/shard_map/ppermute | solution.py:328
  (168 shorter events, 81.3 us)
Async XLA Ops:
  4.9 16.7 %collective-permute-start.1 = (bf16[1,4,48,1536]{3,2,1,0:T(8,128)(2,1)S(1)}, bf16[1,4,48,1536]{3,2,1,0:T(8,128)(2,1)}, u32[]{:S(2)}, u32[]{:S(2)}) collective-permute-start(bf16[1,4,48,1536]{3,2,1,0:T(8,128)(2,1)S(1)} %bitcast.76), channel_id=1, source_target_pairs={{0,8},{4,12},{8,0},{12,4},{16,24},{20,28},{24,16},{28,20},{1,9},{5... | collective-permute-start | bytes 1769480 | tf_op jit(solution)/shard_map/ppermute | solution.py:332
  10.8 37.4 %all-to-all-start = ((bf16[4,48,3584]{2,1,0:T(8,128)(2,1)}), bf16[4,48,3584]{2,1,0:T(8,128)(2,1)S(1)}, u32[]{:S(2)}, u32[]{:S(2)}) async-start(bf16[4,48,3584]{2,1,0:T(8,128)(2,1)} %broadcast_in_dim.43), calls=%async_computation | async-start | bytes 2752512 | tf_op jit(solution)/shard_map/all_to_all | solution.py:370
  35.0 28.7 %collective-permute-start.4 = (bf16[2,4,48,1536]{3,2,1,0:T(8,128)(2,1)}, bf16[2,4,48,1536]{3,2,1,0:T(8,128)(2,1)}, u32[]{:S(2)}, u32[]{:S(2)}) collective-permute-start(bf16[2,4,48,1536]{3,2,1,0:T(8,128)(2,1)} %pad_maximum_fusion.3.refs_0_), channel_id=1, source_target_pairs={{0,16},{4,20},{8,24},{12,28},{16,0},{20,4},{24,8},{28,12},{1,17},{... | collective-permute-start | bytes 3538952 | tf_op jit(solution)/shard_map/ppermute | solution.py:332
  37.7 28.3 %collective-permute-start.5 = (bf16[2,4,48,1536]{3,2,1,0:T(8,128)(2,1)S(1)}, bf16[2,4,48,1536]{3,2,1,0:T(8,128)(2,1)}, u32[]{:S(2)}, u32[]{:S(2)}) collective-permute-start(bf16[2,4,48,1536]{3,2,1,0:T(8,128)(2,1)S(1)} %pad_maximum_fusion.4.refs_0_), channel_id=1, source_target_pairs={{0,8},{4,12},{8,0},{12,4},{16,24},{20,28},{24,16},{28,20},{1,9},{5... | collective-permute-start | bytes 3538952 | tf_op jit(solution)/shard_map/ppermute | solution.py:332
  48.1 32.4 %all-to-all-start.1 = ((bf16[4,2,2,48,768]{4,3,2,1,0:T(8,128)(2,1)}), bf16[4,2,2,48,768]{4,3,2,1,0:T(8,128)(2,1)}, u32[]{:S(2)}, u32[]{:S(2)}) async-start(bf16[4,2,2,48,768]{4,3,2,1,0:T(8,128)(2,1)} %get-tuple-element.17), calls=%async_computation.1 | async-start | bytes 2359296 | tf_op jit(solution)/shard_map/all_to_all | solution.py:370
  66.1 18.9 %collective-permute-start.6 = (bf16[1,192,2048]{2,1,0:T(8,128)(2,1)S(1)}, bf16[1,192,2048]{2,1,0:T(8,128)(2,1)S(1)}, u32[]{:S(2)}, u32[]{:S(2)}) collective-permute-start(bf16[1,192,2048]{2,1,0:T(8,128)(2,1)S(1)} %slice_bitcast_fusion.2), channel_id=1, source_target_pairs={{0,8},{4,12},{8,0},{12,4},{16,24},{20,28},{24,16},{28,20},{1,9},{5... | collective-permute-start | bytes 2359304 | tf_op jit(solution)/shard_map/ppermute | solution.py:332
  66.7 16.2 %collective-permute-start.7 = (bf16[1,192,1536]{2,1,0:T(8,128)(2,1)S(1)}, bf16[1,192,1536]{2,1,0:T(8,128)(2,1)S(1)}, u32[]{:S(2)}, u32[]{:S(2)}) collective-permute-start(bf16[1,192,1536]{2,1,0:T(8,128)(2,1)S(1)} %slice_bitcast_fusion.3), channel_id=1, source_target_pairs={{0,16},{4,20},{8,24},{12,28},{16,0},{20,4},{24,8},{28,12},{1,17},{... | collective-permute-start | bytes 1769480 | tf_op jit(solution)/shard_map/ppermute | solution.py:332
  86.5 43.3 %all-to-all-start.2 = ((bf16[4,128,1664]{2,1,0:T(8,128)(2,1)}), bf16[4,128,1664]{2,1,0:T(8,128)(2,1)S(1)}, u32[]{:S(2)}, u32[]{:S(2)}) async-start(bf16[4,128,1664]{2,1,0:T(8,128)(2,1)} %broadcast_in_dim.46), calls=%async_computation.2 | async-start | bytes 3407872 | tf_op jit(solution)/shard_map/all_to_all | solution.py:370
  93.1 41.2 %collective-permute-start.10 = (bf16[2,192,2048]{2,1,0:T(8,128)(2,1)S(1)}, bf16[2,192,2048]{2,1,0:T(8,128)(2,1)}, u32[]{:S(2)}, u32[]{:S(2)}) collective-permute-start(bf16[2,192,2048]{2,1,0:T(8,128)(2,1)S(1)} %pad_maximum_fusion.1.refs_3_), channel_id=1, source_target_pairs={{0,16},{4,20},{8,24},{12,28},{16,0},{20,4},{24,8},{28,12},{1,17},{... | collective-permute-start | bytes 4718600 | tf_op jit(solution)/shard_map/ppermute | solution.py:332
  96.2 40.1 %collective-permute-start.15 = (bf16[2,192,1536]{2,1,0:T(8,128)(2,1)}, bf16[2,192,1536]{2,1,0:T(8,128)(2,1)}, u32[]{:S(2)}, u32[]{:S(2)}) collective-permute-start(bf16[2,192,1536]{2,1,0:T(8,128)(2,1)} %pad_maximum_fusion.7.refs_2_), channel_id=1, source_target_pairs={{0,8},{4,12},{8,0},{12,4},{16,24},{20,28},{24,16},{28,20},{1,9},{5... | collective-permute-start | bytes 3538952 | tf_op jit(solution)/shard_map/ppermute | solution.py:332
  97.3 46.1 %collective-permute-start.11 = (bf16[2,192,2048]{2,1,0:T(8,128)(2,1)S(1)}, bf16[2,192,2048]{2,1,0:T(8,128)(2,1)}, u32[]{:S(2)}, u32[]{:S(2)}) collective-permute-start(bf16[2,192,2048]{2,1,0:T(8,128)(2,1)S(1)} %pad_maximum_fusion.1.refs_3_), channel_id=1, source_target_pairs={{0,4},{4,0},{8,12},{12,8},{16,20},{20,16},{24,28},{28,24},{1,5},{5... | collective-permute-start | bytes 4718600 | tf_op jit(solution)/shard_map/ppermute | solution.py:332
  98.5 38.4 %collective-permute-start.8 = (bf16[1,384,768]{2,1,0:T(8,128)(2,1)}, bf16[1,384,768]{2,1,0:T(8,128)(2,1)}, u32[]{:S(2)}, u32[]{:S(2)}) collective-permute-start(bf16[1,384,768]{2,1,0:T(8,128)(2,1)} %bitcast.22), channel_id=1, source_target_pairs={{0,8},{4,12},{8,0},{12,4},{16,24},{20,28},{24,16},{28,20},{1,9},{5... | collective-permute-start | bytes 1769480 | tf_op jit(solution)/shard_map/ppermute | solution.py:332
  101.5 38.9 %collective-permute-start.9 = (bf16[1,384,768]{2,1,0:T(8,128)(2,1)}, bf16[1,384,768]{2,1,0:T(8,128)(2,1)}, u32[]{:S(2)}, u32[]{:S(2)}) collective-permute-start(bf16[1,384,768]{2,1,0:T(8,128)(2,1)} %bitcast.80), channel_id=1, source_target_pairs={{0,16},{4,20},{8,24},{12,28},{16,0},{20,4},{24,8},{28,12},{1,17},{... | collective-permute-start | bytes 1769480 | tf_op jit(solution)/shard_map/ppermute | solution.py:332
  129.8 39.8 %all-to-all-start.3 = ((bf16[4,2,2,48,768]{4,3,2,1,0:T(8,128)(2,1)}), bf16[4,2,2,48,768]{4,3,2,1,0:T(8,128)(2,1)}, u32[]{:S(2)}, u32[]{:S(2)}) async-start(bf16[4,2,2,48,768]{4,3,2,1,0:T(8,128)(2,1)} %get-tuple-element.24), calls=%async_computation.3 | async-start | bytes 2359296 | tf_op jit(solution)/shard_map/all_to_all | solution.py:370
  136.3 40.8 %collective-permute-start.16 = (bf16[2,192,1536]{2,1,0:T(8,128)(2,1)}, bf16[2,192,1536]{2,1,0:T(8,128)(2,1)}, u32[]{:S(2)}, u32[]{:S(2)}) collective-permute-start(bf16[2,192,1536]{2,1,0:T(8,128)(2,1)} %pad_maximum_fusion.7.refs_2_), channel_id=1, source_target_pairs={{0,4},{4,0},{8,12},{12,8},{16,20},{20,16},{24,28},{28,24},{1,5},{5... | collective-permute-start | bytes 3538952 | tf_op jit(solution)/shard_map/ppermute | solution.py:332
  136.8 40.3 %collective-permute-start.17 = (bf16[2,192,1536]{2,1,0:T(8,128)(2,1)}, bf16[2,192,1536]{2,1,0:T(8,128)(2,1)}, u32[]{:S(2)}, u32[]{:S(2)}) collective-permute-start(bf16[2,192,1536]{2,1,0:T(8,128)(2,1)} %collective-permute-done.15.refs_3_), channel_id=1, source_target_pairs={{0,4},{4,0},{8,12},{12,8},{16,20},{20,16},{24,28},{28,24},{1,5},{5... | collective-permute-start | bytes 3538952 | tf_op jit(solution)/shard_map/ppermute | solution.py:332
  140.4 32.2 %collective-permute-start.13 = (bf16[2,384,768]{2,1,0:T(8,128)(2,1)}, bf16[2,384,768]{2,1,0:T(8,128)(2,1)}, u32[]{:S(2)}, u32[]{:S(2)}) collective-permute-start(bf16[2,384,768]{2,1,0:T(8,128)(2,1)} %pad_maximum_fusion.5), channel_id=1, source_target_pairs={{0,16},{4,20},{8,24},{12,28},{16,0},{20,4},{24,8},{28,12},{1,17},{... | collective-permute-start | bytes 3538952 | tf_op jit(solution)/shard_map/ppermute | solution.py:332
  143.5 33.7 %collective-permute-start.14 = (bf16[2,384,768]{2,1,0:T(8,128)(2,1)}, bf16[2,384,768]{2,1,0:T(8,128)(2,1)}, u32[]{:S(2)}, u32[]{:S(2)}) collective-permute-start(bf16[2,384,768]{2,1,0:T(8,128)(2,1)} %pad_maximum_fusion.6), channel_id=1, source_target_pairs={{0,8},{4,12},{8,0},{12,4},{16,24},{20,28},{24,16},{28,20},{1,9},{5... | collective-permute-start | bytes 3538952 | tf_op jit(solution)/shard_map/ppermute | solution.py:332
  171.0 19.2 %collective-permute-start.20 = (bf16[1,384,768]{2,1,0:T(8,128)(2,1)S(1)}, bf16[1,384,768]{2,1,0:T(8,128)(2,1)S(1)}, u32[]{:S(2)}, u32[]{:S(2)}) collective-permute-start(bf16[1,384,768]{2,1,0:T(8,128)(2,1)S(1)} %get-tuple-element.42), channel_id=1, source_target_pairs={{0,8},{4,12},{8,0},{12,4},{16,24},{20,28},{24,16},{28,20},{1,9},{5... | collective-permute-start | bytes 1769480 | tf_op jit(solution)/shard_map/ppermute | solution.py:332
  172.6 18.3 %collective-permute-start.22 = (bf16[1,384,768]{2,1,0:T(8,128)(2,1)S(1)}, bf16[1,384,768]{2,1,0:T(8,128)(2,1)}, u32[]{:S(2)}, u32[]{:S(2)}) collective-permute-start(bf16[1,384,768]{2,1,0:T(8,128)(2,1)S(1)} %get-tuple-element.41), channel_id=1, source_target_pairs={{0,16},{4,20},{8,24},{12,28},{16,0},{20,4},{24,8},{28,12},{1,17},{... | collective-permute-start | bytes 1769480 | tf_op jit(solution)/shard_map/ppermute | solution.py:332
  190.3 28.4 %collective-permute-start.21 = (bf16[2,384,768]{2,1,0:T(8,128)(2,1)S(1)}, bf16[2,384,768]{2,1,0:T(8,128)(2,1)S(1)}, u32[]{:S(2)}, u32[]{:S(2)}) collective-permute-start(bf16[2,384,768]{2,1,0:T(8,128)(2,1)S(1)} %pad_maximum_fusion.8), channel_id=1, source_target_pairs={{0,16},{4,20},{8,24},{12,28},{16,0},{20,4},{24,8},{28,12},{1,17},{... | collective-permute-start | bytes 3538952 | tf_op jit(solution)/shard_map/ppermute | solution.py:332
  192.1 28.4 %collective-permute-start.23 = (bf16[2,384,768]{2,1,0:T(8,128)(2,1)S(1)}, bf16[2,384,768]{2,1,0:T(8,128)(2,1)}, u32[]{:S(2)}, u32[]{:S(2)}) collective-permute-start(bf16[2,384,768]{2,1,0:T(8,128)(2,1)S(1)} %pad_maximum_fusion.9), channel_id=1, source_target_pairs={{0,8},{4,12},{8,0},{12,4},{16,24},{20,28},{24,16},{28,20},{1,9},{5... | collective-permute-start | bytes 3538952 | tf_op jit(solution)/shard_map/ppermute | solution.py:332
  248.6 34.7 %collective-permute-start.26 = (bf16[128,1536]{1,0:T(8,128)(2,1)}, bf16[128,1536]{1,0:T(8,128)(2,1)S(1)}, u32[]{:S(2)}, u32[]{:S(2)}) collective-permute-start(bf16[128,1536]{1,0:T(8,128)(2,1)} %get-tuple-element.32), channel_id=1, source_target_pairs={{0,2},{1,3},{2,0},{3,1},{4,6},{5,7},{6,4},{7,5},{8,10},{9,11},{10,... | collective-permute-start | bytes 1179656 | tf_op jit(solution)/shard_map/ppermute | solution.py:328
  248.6 34.7 %collective-permute-start.25 = (bf16[128,1536]{1,0:T(8,128)(2,1)}, bf16[128,1536]{1,0:T(8,128)(2,1)S(1)}, u32[]{:S(2)}, u32[]{:S(2)}) collective-permute-start(bf16[128,1536]{1,0:T(8,128)(2,1)} %get-tuple-element.30), channel_id=1, source_target_pairs={{0,1},{1,0},{2,3},{3,2},{4,5},{5,4},{6,7},{7,6},{8,9},{9,8},{10,11... | collective-permute-start | bytes 1179656 | tf_op jit(solution)/shard_map/ppermute | solution.py:328
  (32 other events, 192.0 us)

commit v4 on v3

--- a/solution.py
+++ b/solution.py
@@ -159,74 +159,60 @@
     )(qkv, qkv, qkv, begin[:, None], index[None, :])
 
 
-def mix_kernel(pieces, block, spots, *refs):
-    x_ref, tokens_ref = refs[:2]
-    out_ref, held = refs[2 + pieces :]
-    put_all(held, spots, block, refs[2 : 2 + pieces])
-    out_ref[...] = tokens_ref[...].astype(F32) + jnp.dot(
+def mix_kernel(pieces, block, span, spots, up_spots, x_ref, tokens_ref, gain_ref, *refs):
+    hidden_ref, normed_ref, held, row = refs[pieces:]
+    step, wide = pl.program_id(0), held.shape[1]
+    put_all(held, spots, block, refs[:pieces])
+    columns = pl.ds(pl.multiple_of(step * wide, wide), wide)
+    hidden_ref[:, columns] = tokens_ref[...].astype(F32) + jnp.dot(
         x_ref[...], held[...], preferred_element_type=F32
     )
 
-
-def mix(spots, block, x, tokens, weights):
-    count = x.shape[0]
-    return pl.pallas_call(
-        functools.partial(mix_kernel, len(weights), block),
+    @pl.when(step == D // wide - 1)
+    def _():
+        for first in range(0, hidden_ref.shape[0], 128):
+            rows = slice(first, first + 128)
+            value = hidden_ref[rows, :]
+            mean_sq = jnp.mean(value * value, axis=1, keepdims=True)
+            row[...] = (value * lax.rsqrt(mean_sq + 1e-06) * gain_ref[...]).astype(BF)
+            for k in range(D // span):
+                spot = pl.multiple_of(up_spots[k], span) if span % 128 == 0 else k * span
+                normed_ref[rows, k * span : (k + 1) * span] = row[:, pl.ds(spot, span)]
+
+
+def mix(spots, block, up_spots, span, x, tokens, weights, gain):
+    count, wide = x.shape[0], D // 2
+    whole = lambda j, *_: (0, 0)
+    hidden, normed = pl.pallas_call(
+        functools.partial(mix_kernel, len(weights), block, span),
         grid_spec=pltpu.PrefetchScalarGridSpec(
-            num_scalar_prefetch=1,
-            grid=(D // WIDE,),
+            num_scalar_prefetch=2,
+            grid=(D // wide,),
             in_specs=[
-                pl.BlockSpec((count, QW), lambda j, _: (0, 0)),
-                pl.BlockSpec((count, WIDE), lambda j, _: (0, j)),
+                pl.BlockSpec((count, QW), whole),
+                pl.BlockSpec((count, wide), lambda j, *_: (0, j)),
+                pl.BlockSpec((1, D), whole),
             ]
-            + [pl.BlockSpec(w.shape[:2] + (WIDE,), lambda j, _: (0, 0, j)) for w in weights],
-            out_specs=pl.BlockSpec((count, WIDE), lambda j, _: (0, j)),
-            scratch_shapes=[pltpu.VMEM((QW, WIDE), BF)],
-        ),
-        out_shape=jax.ShapeDtypeStruct((count, D), F32),
+            + [pl.BlockSpec(w.shape[:2] + (wide,), lambda j, *_: (0, 0, j)) for w in weights],
+            out_specs=[pl.BlockSpec((count, D), whole)] * 2,
+            scratch_shapes=[pltpu.VMEM((QW, wide), BF), pltpu.VMEM((128, D), BF)],
+        ),
+        out_shape=[
+            jax.ShapeDtypeStruct((count, D), F32),
+            jax.ShapeDtypeStruct((count, D), BF),
+        ],
         compiler_params=pltpu.CompilerParams(vmem_limit_bytes=VMEM),
         cost_estimate=cost(
-            flops=2 * count * D * QW, bytes_accessed=2 * D * QW + 8 * count * D, transcendentals=0
+            flops=2 * count * D * QW, bytes_accessed=2 * D * QW + 10 * count * D, transcendentals=0
         ),
         name="mix",
-    )(spots, x, tokens, *weights)
-
-
-def norm_kernel(span, spots, x_ref, gain_ref, out_ref, held):
-    value = x_ref[...]
-    mean_sq = jnp.mean(value * value, axis=1, keepdims=True)
-    held[...] = (value * lax.rsqrt(mean_sq + 1e-06) * gain_ref[...]).astype(BF)
-    for k in range(D // span):
-        spot = pl.multiple_of(spots[k], span) if span % 128 == 0 else k * span
-        out_ref[:, k * span : (k + 1) * span] = held[:, pl.ds(spot, span)]
-
-
-def norm_blocks(spots, span, x, gain):
-    count = x.shape[0]
-    out = pl.pallas_call(
-        functools.partial(norm_kernel, span),
-        grid_spec=pltpu.PrefetchScalarGridSpec(
-            num_scalar_prefetch=1,
-            grid=(count // 128,),
-            in_specs=[
-                pl.BlockSpec((128, D), lambda i, _: (i, 0)),
-                pl.BlockSpec((1, D), lambda i, _: (0, 0)),
-            ],
-            out_specs=pl.BlockSpec((128, D), lambda i, _: (i, 0)),
-            scratch_shapes=[pltpu.VMEM((128, D), BF)],
-        ),
-        out_shape=jax.ShapeDtypeStruct((count, D), BF),
-        compiler_params=pltpu.CompilerParams(vmem_limit_bytes=VMEM),
-        cost_estimate=cost(
-            flops=4 * count * D, bytes_accessed=6 * count * D, transcendentals=count
-        ),
-        name="norm",
-    )(spots, x, gain[None, :])
-    if span % 128 == 0:
-        return out
-    return jnp.concatenate(
-        [lax.dynamic_slice_in_dim(out, spots[k], span, 1) for k in range(D // span)], axis=1
-    )
+    )(spots, up_spots, x, tokens, gain[None, :], *weights)
+    if span % 128 != 0:
+        normed = jnp.concatenate(
+            [lax.dynamic_slice_in_dim(normed, up_spots[k], span, 1) for k in range(D // span)],
+            axis=1,
+        )
+    return hidden, normed
 
 
 def gate_up_kernel(orders, mine_ref, other_ref, gate_ref, *refs):
@@ -499,7 +485,11 @@
             attended = attend(qkv, begin, index)
             gate = (attended,)
     attended = after(attended, (steps[1],))
-    hidden = mix(attn_spots(1), block, attended, group, mix_weight)
+    span = D // (reps // 2)
+    up_spots = (chip ^ jnp.arange(reps // 2, dtype=jnp.int32)) * span
+    hidden, normed_two = mix(
+        attn_spots(1), block, up_spots, span, attended, group, mix_weight, moe_gain
+    )
 
     page_count = count // PAGE
     targets = place * page_count + jnp.arange(page_count, dtype=jnp.int32)
@@ -518,9 +508,6 @@
         [lax.dynamic_slice_in_dim(cache, first_row[i], PAGE, 0) for i in range(page_count)]
     )
 
-    span = D // (reps // 2)
-    up_spots = (chip ^ jnp.arange(reps // 2, dtype=jnp.int32)) * span
-    normed_two = norm_blocks(up_spots, span, hidden, moe_gain)
     other_two = across_rep(normed_two, 1)
     both_gates = jnp.concatenate([group_gates, across_rep(group_gates, 1)], axis=0)
     my_gates = lax.dynamic_slice_in_dim(both_gates, core * half_experts, half_experts, 1).astype(F32)

time: 287 us -> 283 us (0.986)
  Pallas kernels: 74.5 us -> 70.8 us
    pallas_call x2 -> x1, Pallas kernels: 13 us -> 9.37 us  [mix(): pl.pallas_call(functools.partial(mix_kernel, len(weights), block, span),...]
  transfers between devices with their start and end apart: 32 -> 32, of which waited for: 15 -> 15; matrix products, arithmetic and copies ran while one was open for 16% -> 16% of each run, Pallas kernels for 21% -> 19%
where the time goes in v4:
time: 283 us; the launch traced here: 282 us
  waiting for transfers between devices  110 us (39%)
  Pallas kernels  70.8 us (25%)
  starting transfers between devices  41.7 us (15%)
  other arithmetic  34.9 us (12%)
  local copies, waits for them, and re-layouts  18.9 us (7%)
  matrix products  4.14 us (1%)
    all_to_all x4, waiting for transfers between devices, exchange_blk(): return lax.all_to_all(value, 'blk', 0, 0, tiled=True)  45.4 us
    ppermute x25, waiting for transfers between devices, across_rep(): lax.ppermute(value, 'rep', [(i, i ^ mask) for i in range(lax.axis_size('r...  32.5 us
    ppermute x3, waiting for transfers between devices, across_blk(): lax.ppermute(value, 'blk', [(i, i ^ mask) for i in range(lax.axis_size('b...  31.8 us
    pallas_call x2, Pallas kernels, gate_up(): pl.pallas_call(functools.partial(gate_up_kernel, orders), grid=(2,), in_s...  20.2 us
    pallas_call x3, Pallas kernels, down_project(): pl.pallas_call(functools.partial(down_kernel, block, len(weights)), grid_...  19.2 us
    ppermute x25, starting transfers between devices, across_rep(): lax.ppermute(value, 'rep', [(i, i ^ mask) for i in range(lax.axis_size('r...  18.8 us
    all_to_all x4, starting transfers between devices, exchange_blk(): return lax.all_to_all(value, 'blk', 0, 0, tiled=True)  18.5 us
    concatenate x8, other arithmetic, chip_gather(): held = jnp.concatenate([held, came], axis=0)  13.2 us
  transfers between devices with their start and end apart: 32, of which 15 were waited for; matrix products, arithmetic and copies ran while one was open for 16% of the time, Pallas kernels for 19%

profile of v4, /device:TPU:0, one launch (start us, length us, event | category | flops | bytes accessed | tf_op | source)
XLA Modules:
  0.0 281.9 jit_solution(6293627378940965247)
XLA Ops:
  4.9 2.9 %collective-permute-start.1 = (bf16[1,4,48,1536]{3,2,1,0:T(8,128)(2,1)S(1)}, bf16[1,4,48,1536]{3,2,1,0:T(8,128)(2,1)}, u32[]{:S(2)}, u32[]{:S(2)}) collective-permute-start(bf16[1,4,48,1536]{3,2,1,0:T(8,128)(2,1)S(1)} %bitcast.76), channel_id=1, source_target_pairs={{0,8},{4,12},{8,0},{12,4},{16,24},{20,28},{24,16},{28,20},{1,9},{5... | collective-permute-start | bytes 1769480 | tf_op jit(solution)/shard_map/ppermute | solution.py:318
  10.8 4.9 %all-to-all-start = ((bf16[4,48,3584]{2,1,0:T(8,128)(2,1)}), bf16[4,48,3584]{2,1,0:T(8,128)(2,1)S(1)}, u32[]{:S(2)}, u32[]{:S(2)}) async-start(bf16[4,48,3584]{2,1,0:T(8,128)(2,1)} %broadcast_in_dim.43), calls=%async_computation | async-start | bytes 2752512 | tf_op jit(solution)/shard_map/all_to_all | solution.py:356
  15.7 5.9 %collective-permute-done.1 = bf16[1,4,48,1536]{3,2,1,0:T(8,128)(2,1)} collective-permute-done((bf16[1,4,48,1536]{3,2,1,0:T(8,128)(2,1)S(1)}, bf16[1,4,48,1536]{3,2,1,0:T(8,128)(2,1)}, u32[]{:S(2)}, u32[]{:S(2)}) %collective-permute-start.1) | collective-permute-done | bytes 589856 | tf_op jit(solution)/shard_map/ppermute | solution.py:318
  25.8 4.1 %fusion.2 = bf16[768,1536]{1,0:T(8,128)(2,1)S(1)} fusion(bf16[768,1536]{1,0:T(8,128)(2,1)S(1)} %bitcast.74, s32[1536]{0:T(1024)S(1)} %fusion.23), kind=kOutput, calls=%fused_computation.5 | convolution fusion | flops 3627417600 | bytes 4724736 | tf_op jit(solution)/shard_map/dot_general | solution.py:408
  41.8 6.3 %all-to-all-done = bf16[4,48,3584]{2,1,0:T(8,128)(2,1)S(1)} async-done(((bf16[4,48,3584]{2,1,0:T(8,128)(2,1)}), bf16[4,48,3584]{2,1,0:T(8,128)(2,1)S(1)}, u32[]{:S(2)}, u32[]{:S(2)}) %all-to-all-start) | async-done | bytes 1376288 | tf_op jit(solution)/shard_map/all_to_all | solution.py:356
  48.1 4.3 %all-to-all-start.1 = ((bf16[4,2,2,48,768]{4,3,2,1,0:T(8,128)(2,1)}), bf16[4,2,2,48,768]{4,3,2,1,0:T(8,128)(2,1)}, u32[]{:S(2)}, u32[]{:S(2)}) async-start(bf16[4,2,2,48,768]{4,3,2,1,0:T(8,128)(2,1)} %get-tuple-element.19), calls=%async_computation.1 | async-start | bytes 2359296 | tf_op jit(solution)/shard_map/all_to_all | solution.py:356
  52.4 11.3 %collective-permute-done.4.refs_1_ = bf16[2,4,48,1536]{3,2,1,0:T(8,128)(2,1)} collective-permute-done((bf16[2,4,48,1536]{3,2,1,0:T(8,128)(2,1)}, bf16[2,4,48,1536]{3,2,1,0:T(8,128)(2,1)}, u32[]{:S(2)}, u32[]{:S(2)}) %collective-permute-start.4) | collective-permute-done | bytes 1179680 | tf_op jit(solution)/shard_map/ppermute | solution.py:318
  68.3 12.2 %all-to-all-done.1 = bf16[4,2,2,48,768]{4,3,2,1,0:T(8,128)(2,1)} async-done(((bf16[4,2,2,48,768]{4,3,2,1,0:T(8,128)(2,1)}), bf16[4,2,2,48,768]{4,3,2,1,0:T(8,128)(2,1)}, u32[]{:S(2)}, u32[]{:S(2)}) %all-to-all-start.1) | async-done | bytes 1179680 | tf_op jit(solution)/shard_map/all_to_all | solution.py:356
  86.5 4.9 %all-to-all-start.2 = ((bf16[4,128,1664]{2,1,0:T(8,128)(2,1)}), bf16[4,128,1664]{2,1,0:T(8,128)(2,1)S(1)}, u32[]{:S(2)}, u32[]{:S(2)}) async-start(bf16[4,128,1664]{2,1,0:T(8,128)(2,1)} %broadcast_in_dim.46), calls=%async_computation.2 | async-start | bytes 3407872 | tf_op jit(solution)/shard_map/all_to_all | solution.py:356
  102.9 26.8 %all-to-all-done.2 = bf16[4,128,1664]{2,1,0:T(8,128)(2,1)S(1)} async-done(((bf16[4,128,1664]{2,1,0:T(8,128)(2,1)}), bf16[4,128,1664]{2,1,0:T(8,128)(2,1)S(1)}, u32[]{:S(2)}, u32[]{:S(2)}) %all-to-all-start.2) | async-done | bytes 1703968 | tf_op jit(solution)/shard_map/all_to_all | solution.py:356
  129.8 4.5 %all-to-all-start.3 = ((bf16[4,2,2,48,768]{4,3,2,1,0:T(8,128)(2,1)}), bf16[4,2,2,48,768]{4,3,2,1,0:T(8,128)(2,1)}, u32[]{:S(2)}, u32[]{:S(2)}) async-start(bf16[4,2,2,48,768]{4,3,2,1,0:T(8,128)(2,1)} %get-tuple-element.28), calls=%async_computation.3 | async-start | bytes 2359296 | tf_op jit(solution)/shard_map/all_to_all | solution.py:356
  146.9 9.1 %project.1.q_ref.k_ref.v_ref = bf16[512,2048]{1,0:T(8,128)(2,1)} custom-call(s32[8]{0:T(128)} %mul.141.spots, bf16[512,1536]{1,0:T(8,128)(2,1)} %fusion.5.refs_0_, f32[512,128]{1,0:T(8,128)} %get-tuple-element.74.refs_1_, f32[512,128]{1,0:T(8,128)} %get-tuple-element.75.refs_2_, bf16[2,192,2048]{2,1,0:T(8,128)(2,1)} %copy-done.3, ...), custom_call_target="tpu_custom_call" | custom-call | flops 201326592 | bytes 589824 | tf_op jit(solution)/shard_map/project/pallas_call | solution.py:95
  156.6 12.8 %attend.1.x_ref = bf16[512,1536]{1,0:T(8,128)(2,1)} custom-call(bf16[512,2048]{1,0:T(8,128)(2,1)} %project.1.q_ref.k_ref.v_ref, bf16[512,2048]{1,0:T(8,128)(2,1)} %project.1.q_ref.k_ref.v_ref, bf16[512,2048]{1,0:T(8,128)(2,1)} %project.1.q_ref.k_ref.v_ref, s32[512,1]{1,0:T(8,128)} %copy.66.begin_ref, s32[1,512]{1,0:T(1,128)} %iota.47.across_ref), custom_call_target="tpu_custom_call" | custom-call | flops 100663296 | bytes 229376 | tf_op jit(solution)/shard_map/attend/pallas_call | solution.py:140
  177.1 9.4 %mix.1 = (f32[512,1536]{1,0:T(8,128)}, bf16[512,1536]{1,0:T(8,128)(2,1)}) custom-call(s32[8]{0:T(128)} %mul.137.spots, s32[4]{0:T(128)} %fusion.36.up_spots, bf16[512,1536]{1,0:T(8,128)(2,1)} %attend.1.x_ref, bf16[512,1536]{1,0:T(8,128)(2,1)} %slice.130.tokens_ref, f32[1,1536]{1,0:T(1,128)} %broadcast_in_dim.48.gain_ref, ...), custom_call_target="tpu_custom_call" | custom-call | flops 150994944 | bytes 786432 | tf_op jit(solution)/shard_map/mix/pallas_call | solution.py:186
  193.3 10.1 %gate_up.2.act_ref = bf16[1024,768]{1,0:T(8,128)(2,1)} custom-call(bf16[512,1536]{1,0:T(8,128)(2,1)} %get-tuple-element.27.mine_ref, bf16[512,1536]{1,0:T(8,128)(2,1)} %copy-done.2, f32[1024,4]{1,0:T(8,128)} %get-tuple-element.61.gate_ref, bf16[768,768]{1,0:T(8,128)(2,1)} %bitcast.34.refs_0_, bf16[768,768]{1,0:T(8,128)(2,1)} %bitcast.35.refs_1_, ...), custom_call_target="tpu_custom_call" | custom-call | flops 301989888 | bytes 491520 | tf_op jit(solution)/shard_map/gate_up/pallas_call | solution.py:258
  203.4 7.5 %down.3.refs_2_ = f32[1024,1536]{1,0:T(8,128)} custom-call(s32[4]{0:T(128)} %fusion.34.spots, bf16[1024,768]{1,0:T(8,128)(2,1)} %gate_up.2.act_ref, bf16[2,4,48,1536]{3,2,1,0:T(8,128)(2,1)} %pad_maximum_fusion.3.refs_0_, bf16[2,4,48,1536]{3,2,1,0:T(8,128)(2,1)} %collective-permute-done.4.refs_1_), custom_call_target="tpu_custom_call" | custom-call | flops 150994944 | bytes 1032192 | tf_op jit(solution)/shard_map/down/pallas_call | solution.py:291
  210.9 4.1 %collective-permute-done.21 = bf16[2,384,768]{2,1,0:T(8,128)(2,1)S(1)} collective-permute-done((bf16[2,384,768]{2,1,0:T(8,128)(2,1)S(1)}, bf16[2,384,768]{2,1,0:T(8,128)(2,1)S(1)}, u32[]{:S(2)}, u32[]{:S(2)}) %collective-permute-start.21) | collective-permute-done | bytes 1179680 | tf_op jit(solution)/shard_map/ppermute | solution.py:318
  216.7 10.1 %gate_up.3.act_ref = bf16[1024,768]{1,0:T(8,128)(2,1)} custom-call(bf16[512,1536]{1,0:T(8,128)(2,1)} %get-tuple-element.27.mine_ref, bf16[512,1536]{1,0:T(8,128)(2,1)} %copy-done.2, f32[1024,4]{1,0:T(8,128)} %get-tuple-element.62.gate_ref, bf16[768,768]{1,0:T(8,128)(2,1)} %bitcast.70, bf16[768,768]{1,0:T(8,128)(2,1)} %bitcast.82, bf16[768,768]{1,0:T(8,128)(2,1)} %bitcast.71, ...), custom_call_target="tpu_custom_call" | custom-call | flops 301989888 | bytes 491520 | tf_op jit(solution)/shard_map/gate_up/pallas_call | solution.py:258
  226.8 5.7 %down.5 = bf16[512,1536]{1,0:T(8,128)(2,1)} custom-call(s32[4]{0:T(128)} %get-tuple-element.69.spots, bf16[1024,768]{1,0:T(8,128)(2,1)} %gate_up.3.act_ref, bf16[2,4,48,1536]{3,2,1,0:T(8,128)(2,1)} %copy-done, bf16[2,4,48,1536]{3,2,1,0:T(8,128)(2,1)} %collective-permute-done.5.refs_1_, f32[1024,1536]{1,0:T(8,128)} %down.3.refs_2_), custom_call_target="tpu_custom_call" | custom-call | flops 75497472 | bytes 589824 | tf_op jit(solution)/shard_map/down/pallas_call | solution.py:291
  232.5 6.0 %down.4 = f32[512,1536]{1,0:T(8,128)} custom-call(s32[4]{0:T(128)} %get-tuple-element.69.spots, bf16[1024,768]{1,0:T(8,128)(2,1)} %gate_up.3.act_ref, bf16[2,4,48,1536]{3,2,1,0:T(8,128)(2,1)} %copy-done, bf16[2,4,48,1536]{3,2,1,0:T(8,128)(2,1)} %collective-permute-done.5.refs_1_, f32[1024,1536]{1,0:T(8,128)} %down.3.refs_2_), custom_call_target="tpu_custom_call" | custom-call | flops 75497472 | bytes 589824 | tf_op jit(solution)/shard_map/down/pallas_call | solution.py:291
  238.5 2.8 add_convert_fusion.3
  241.3 3.5 %collective-permute-start.27 = (bf16[128,1536]{1,0:T(8,128)(2,1)}, bf16[128,1536]{1,0:T(8,128)(2,1)S(1)}, u32[]{:S(2)}, u32[]{:S(2)}) collective-permute-start(bf16[128,1536]{1,0:T(8,128)(2,1)} %get-tuple-element.35), channel_id=1, source_target_pairs={{0,3},{1,2},{2,1},{3,0},{4,7},{5,6},{6,5},{7,4},{8,11},{9,10},{10,... | collective-permute-start | bytes 1179656 | tf_op jit(solution)/shard_map/ppermute | solution.py:314
  247.7 7.7 %collective-permute-done.27 = bf16[128,1536]{1,0:T(8,128)(2,1)S(1)} collective-permute-done((bf16[128,1536]{1,0:T(8,128)(2,1)}, bf16[128,1536]{1,0:T(8,128)(2,1)S(1)}, u32[]{:S(2)}, u32[]{:S(2)}) %collective-permute-start.27) | collective-permute-done | bytes 393248 | tf_op jit(solution)/shard_map/ppermute | solution.py:314
  255.4 24.1 %collective-permute-done.26 = bf16[128,1536]{1,0:T(8,128)(2,1)S(1)} collective-permute-done((bf16[128,1536]{1,0:T(8,128)(2,1)}, bf16[128,1536]{1,0:T(8,128)(2,1)S(1)}, u32[]{:S(2)}, u32[]{:S(2)}) %collective-permute-start.26) | collective-permute-done | bytes 393248 | tf_op jit(solution)/shard_map/ppermute | solution.py:314
  (167 shorter events, 79.0 us)
Async XLA Ops:
  4.9 16.7 %collective-permute-start.1 = (bf16[1,4,48,1536]{3,2,1,0:T(8,128)(2,1)S(1)}, bf16[1,4,48,1536]{3,2,1,0:T(8,128)(2,1)}, u32[]{:S(2)}, u32[]{:S(2)}) collective-permute-start(bf16[1,4,48,1536]{3,2,1,0:T(8,128)(2,1)S(1)} %bitcast.76), channel_id=1, source_target_pairs={{0,8},{4,12},{8,0},{12,4},{16,24},{20,28},{24,16},{28,20},{1,9},{5... | collective-permute-start | bytes 1769480 | tf_op jit(solution)/shard_map/ppermute | solution.py:318
  7.9 15.3 %collective-permute-start.2 = (bf16[1,4,48,1536]{3,2,1,0:T(8,128)(2,1)S(1)}, bf16[1,4,48,1536]{3,2,1,0:T(8,128)(2,1)}, u32[]{:S(2)}, u32[]{:S(2)}) collective-permute-start(bf16[1,4,48,1536]{3,2,1,0:T(8,128)(2,1)S(1)} %bitcast.78), channel_id=1, source_target_pairs={{0,16},{4,20},{8,24},{12,28},{16,0},{20,4},{24,8},{28,12},{1,17},{... | collective-permute-start | bytes 1769480 | tf_op jit(solution)/shard_map/ppermute | solution.py:318
  10.8 37.4 %all-to-all-start = ((bf16[4,48,3584]{2,1,0:T(8,128)(2,1)}), bf16[4,48,3584]{2,1,0:T(8,128)(2,1)S(1)}, u32[]{:S(2)}, u32[]{:S(2)}) async-start(bf16[4,48,3584]{2,1,0:T(8,128)(2,1)} %broadcast_in_dim.43), calls=%async_computation | async-start | bytes 2752512 | tf_op jit(solution)/shard_map/all_to_all | solution.py:356
  35.0 28.7 %collective-permute-start.4 = (bf16[2,4,48,1536]{3,2,1,0:T(8,128)(2,1)}, bf16[2,4,48,1536]{3,2,1,0:T(8,128)(2,1)}, u32[]{:S(2)}, u32[]{:S(2)}) collective-permute-start(bf16[2,4,48,1536]{3,2,1,0:T(8,128)(2,1)} %pad_maximum_fusion.3.refs_0_), channel_id=1, source_target_pairs={{0,16},{4,20},{8,24},{12,28},{16,0},{20,4},{24,8},{28,12},{1,17},{... | collective-permute-start | bytes 3538952 | tf_op jit(solution)/shard_map/ppermute | solution.py:318
  37.7 28.3 %collective-permute-start.5 = (bf16[2,4,48,1536]{3,2,1,0:T(8,128)(2,1)S(1)}, bf16[2,4,48,1536]{3,2,1,0:T(8,128)(2,1)}, u32[]{:S(2)}, u32[]{:S(2)}) collective-permute-start(bf16[2,4,48,1536]{3,2,1,0:T(8,128)(2,1)S(1)} %pad_maximum_fusion.4.refs_0_), channel_id=1, source_target_pairs={{0,8},{4,12},{8,0},{12,4},{16,24},{20,28},{24,16},{28,20},{1,9},{5... | collective-permute-start | bytes 3538952 | tf_op jit(solution)/shard_map/ppermute | solution.py:318
  48.1 32.4 %all-to-all-start.1 = ((bf16[4,2,2,48,768]{4,3,2,1,0:T(8,128)(2,1)}), bf16[4,2,2,48,768]{4,3,2,1,0:T(8,128)(2,1)}, u32[]{:S(2)}, u32[]{:S(2)}) async-start(bf16[4,2,2,48,768]{4,3,2,1,0:T(8,128)(2,1)} %get-tuple-element.19), calls=%async_computation.1 | async-start | bytes 2359296 | tf_op jit(solution)/shard_map/all_to_all | solution.py:356
  66.1 18.9 %collective-permute-start.6 = (bf16[1,192,2048]{2,1,0:T(8,128)(2,1)S(1)}, bf16[1,192,2048]{2,1,0:T(8,128)(2,1)S(1)}, u32[]{:S(2)}, u32[]{:S(2)}) collective-permute-start(bf16[1,192,2048]{2,1,0:T(8,128)(2,1)S(1)} %slice_bitcast_fusion.2), channel_id=1, source_target_pairs={{0,8},{4,12},{8,0},{12,4},{16,24},{20,28},{24,16},{28,20},{1,9},{5... | collective-permute-start | bytes 2359304 | tf_op jit(solution)/shard_map/ppermute | solution.py:318
  66.7 16.1 %collective-permute-start.7 = (bf16[1,192,1536]{2,1,0:T(8,128)(2,1)S(1)}, bf16[1,192,1536]{2,1,0:T(8,128)(2,1)S(1)}, u32[]{:S(2)}, u32[]{:S(2)}) collective-permute-start(bf16[1,192,1536]{2,1,0:T(8,128)(2,1)S(1)} %slice_bitcast_fusion.3), channel_id=1, source_target_pairs={{0,16},{4,20},{8,24},{12,28},{16,0},{20,4},{24,8},{28,12},{1,17},{... | collective-permute-start | bytes 1769480 | tf_op jit(solution)/shard_map/ppermute | solution.py:318
  86.5 43.3 %all-to-all-start.2 = ((bf16[4,128,1664]{2,1,0:T(8,128)(2,1)}), bf16[4,128,1664]{2,1,0:T(8,128)(2,1)S(1)}, u32[]{:S(2)}, u32[]{:S(2)}) async-start(bf16[4,128,1664]{2,1,0:T(8,128)(2,1)} %broadcast_in_dim.46), calls=%async_computation.2 | async-start | bytes 3407872 | tf_op jit(solution)/shard_map/all_to_all | solution.py:356
  93.1 41.2 %collective-permute-start.10 = (bf16[2,192,2048]{2,1,0:T(8,128)(2,1)S(1)}, bf16[2,192,2048]{2,1,0:T(8,128)(2,1)}, u32[]{:S(2)}, u32[]{:S(2)}) collective-permute-start(bf16[2,192,2048]{2,1,0:T(8,128)(2,1)S(1)} %pad_maximum_fusion.1.refs_3_), channel_id=1, source_target_pairs={{0,16},{4,20},{8,24},{12,28},{16,0},{20,4},{24,8},{28,12},{1,17},{... | collective-permute-start | bytes 4718600 | tf_op jit(solution)/shard_map/ppermute | solution.py:318
  96.2 40.1 %collective-permute-start.15 = (bf16[2,192,1536]{2,1,0:T(8,128)(2,1)}, bf16[2,192,1536]{2,1,0:T(8,128)(2,1)}, u32[]{:S(2)}, u32[]{:S(2)}) collective-permute-start(bf16[2,192,1536]{2,1,0:T(8,128)(2,1)} %pad_maximum_fusion.7.refs_0_), channel_id=1, source_target_pairs={{0,8},{4,12},{8,0},{12,4},{16,24},{20,28},{24,16},{28,20},{1,9},{5... | collective-permute-start | bytes 3538952 | tf_op jit(solution)/shard_map/ppermute | solution.py:318
  97.3 46.2 %collective-permute-start.11 = (bf16[2,192,2048]{2,1,0:T(8,128)(2,1)S(1)}, bf16[2,192,2048]{2,1,0:T(8,128)(2,1)}, u32[]{:S(2)}, u32[]{:S(2)}) collective-permute-start(bf16[2,192,2048]{2,1,0:T(8,128)(2,1)S(1)} %pad_maximum_fusion.1.refs_3_), channel_id=1, source_target_pairs={{0,4},{4,0},{8,12},{12,8},{16,20},{20,16},{24,28},{28,24},{1,5},{5... | collective-permute-start | bytes 4718600 | tf_op jit(solution)/shard_map/ppermute | solution.py:318
  98.4 38.5 %collective-permute-start.8 = (bf16[1,384,768]{2,1,0:T(8,128)(2,1)}, bf16[1,384,768]{2,1,0:T(8,128)(2,1)}, u32[]{:S(2)}, u32[]{:S(2)}) collective-permute-start(bf16[1,384,768]{2,1,0:T(8,128)(2,1)} %bitcast.22), channel_id=1, source_target_pairs={{0,8},{4,12},{8,0},{12,4},{16,24},{20,28},{24,16},{28,20},{1,9},{5... | collective-permute-start | bytes 1769480 | tf_op jit(solution)/shard_map/ppermute | solution.py:318
  101.4 39.0 %collective-permute-start.9 = (bf16[1,384,768]{2,1,0:T(8,128)(2,1)}, bf16[1,384,768]{2,1,0:T(8,128)(2,1)}, u32[]{:S(2)}, u32[]{:S(2)}) collective-permute-start(bf16[1,384,768]{2,1,0:T(8,128)(2,1)} %bitcast.80), channel_id=1, source_target_pairs={{0,16},{4,20},{8,24},{12,28},{16,0},{20,4},{24,8},{28,12},{1,17},{... | collective-permute-start | bytes 1769480 | tf_op jit(solution)/shard_map/ppermute | solution.py:318
  129.8 39.7 %all-to-all-start.3 = ((bf16[4,2,2,48,768]{4,3,2,1,0:T(8,128)(2,1)}), bf16[4,2,2,48,768]{4,3,2,1,0:T(8,128)(2,1)}, u32[]{:S(2)}, u32[]{:S(2)}) async-start(bf16[4,2,2,48,768]{4,3,2,1,0:T(8,128)(2,1)} %get-tuple-element.28), calls=%async_computation.3 | async-start | bytes 2359296 | tf_op jit(solution)/shard_map/all_to_all | solution.py:356
  136.3 40.7 %collective-permute-start.16 = (bf16[2,192,1536]{2,1,0:T(8,128)(2,1)}, bf16[2,192,1536]{2,1,0:T(8,128)(2,1)}, u32[]{:S(2)}, u32[]{:S(2)}) collective-permute-start(bf16[2,192,1536]{2,1,0:T(8,128)(2,1)} %pad_maximum_fusion.7.refs_0_), channel_id=1, source_target_pairs={{0,4},{4,0},{8,12},{12,8},{16,20},{20,16},{24,28},{28,24},{1,5},{5... | collective-permute-start | bytes 3538952 | tf_op jit(solution)/shard_map/ppermute | solution.py:318
  136.8 40.2 %collective-permute-start.17 = (bf16[2,192,1536]{2,1,0:T(8,128)(2,1)}, bf16[2,192,1536]{2,1,0:T(8,128)(2,1)}, u32[]{:S(2)}, u32[]{:S(2)}) collective-permute-start(bf16[2,192,1536]{2,1,0:T(8,128)(2,1)} %collective-permute-done.15.refs_1_), channel_id=1, source_target_pairs={{0,4},{4,0},{8,12},{12,8},{16,20},{20,16},{24,28},{28,24},{1,5},{5... | collective-permute-start | bytes 3538952 | tf_op jit(solution)/shard_map/ppermute | solution.py:318
  140.4 32.1 %collective-permute-start.13 = (bf16[2,384,768]{2,1,0:T(8,128)(2,1)}, bf16[2,384,768]{2,1,0:T(8,128)(2,1)}, u32[]{:S(2)}, u32[]{:S(2)}) collective-permute-start(bf16[2,384,768]{2,1,0:T(8,128)(2,1)} %pad_maximum_fusion.5), channel_id=1, source_target_pairs={{0,16},{4,20},{8,24},{12,28},{16,0},{20,4},{24,8},{28,12},{1,17},{... | collective-permute-start | bytes 3538952 | tf_op jit(solution)/shard_map/ppermute | solution.py:318
  143.5 33.6 %collective-permute-start.14 = (bf16[2,384,768]{2,1,0:T(8,128)(2,1)}, bf16[2,384,768]{2,1,0:T(8,128)(2,1)}, u32[]{:S(2)}, u32[]{:S(2)}) collective-permute-start(bf16[2,384,768]{2,1,0:T(8,128)(2,1)} %pad_maximum_fusion.6), channel_id=1, source_target_pairs={{0,8},{4,12},{8,0},{12,4},{16,24},{20,28},{24,16},{28,20},{1,9},{5... | collective-permute-start | bytes 3538952 | tf_op jit(solution)/shard_map/ppermute | solution.py:318
  170.9 15.5 %collective-permute-start.20 = (bf16[1,384,768]{2,1,0:T(8,128)(2,1)S(1)}, bf16[1,384,768]{2,1,0:T(8,128)(2,1)S(1)}, u32[]{:S(2)}, u32[]{:S(2)}) collective-permute-start(bf16[1,384,768]{2,1,0:T(8,128)(2,1)S(1)} %get-tuple-element.46), channel_id=1, source_target_pairs={{0,8},{4,12},{8,0},{12,4},{16,24},{20,28},{24,16},{28,20},{1,9},{5... | collective-permute-start | bytes 1769480 | tf_op jit(solution)/shard_map/ppermute | solution.py:318
  186.6 28.4 %collective-permute-start.21 = (bf16[2,384,768]{2,1,0:T(8,128)(2,1)S(1)}, bf16[2,384,768]{2,1,0:T(8,128)(2,1)S(1)}, u32[]{:S(2)}, u32[]{:S(2)}) collective-permute-start(bf16[2,384,768]{2,1,0:T(8,128)(2,1)S(1)} %pad_maximum_fusion.8), channel_id=1, source_target_pairs={{0,16},{4,20},{8,24},{12,28},{16,0},{20,4},{24,8},{28,12},{1,17},{... | collective-permute-start | bytes 3538952 | tf_op jit(solution)/shard_map/ppermute | solution.py:318
  188.3 28.4 %collective-permute-start.23 = (bf16[2,384,768]{2,1,0:T(8,128)(2,1)S(1)}, bf16[2,384,768]{2,1,0:T(8,128)(2,1)}, u32[]{:S(2)}, u32[]{:S(2)}) collective-permute-start(bf16[2,384,768]{2,1,0:T(8,128)(2,1)S(1)} %pad_maximum_fusion.9), channel_id=1, source_target_pairs={{0,8},{4,12},{8,0},{12,4},{16,24},{20,28},{24,16},{28,20},{1,9},{5... | collective-permute-start | bytes 3538952 | tf_op jit(solution)/shard_map/ppermute | solution.py:318
  244.9 34.7 %collective-permute-start.26 = (bf16[128,1536]{1,0:T(8,128)(2,1)}, bf16[128,1536]{1,0:T(8,128)(2,1)S(1)}, u32[]{:S(2)}, u32[]{:S(2)}) collective-permute-start(bf16[128,1536]{1,0:T(8,128)(2,1)} %get-tuple-element.36), channel_id=1, source_target_pairs={{0,2},{1,3},{2,0},{3,1},{4,6},{5,7},{6,4},{7,5},{8,10},{9,11},{10,... | collective-permute-start | bytes 1179656 | tf_op jit(solution)/shard_map/ppermute | solution.py:314
  244.9 34.7 %collective-permute-start.25 = (bf16[128,1536]{1,0:T(8,128)(2,1)}, bf16[128,1536]{1,0:T(8,128)(2,1)S(1)}, u32[]{:S(2)}, u32[]{:S(2)}) collective-permute-start(bf16[128,1536]{1,0:T(8,128)(2,1)} %get-tuple-element.34), channel_id=1, source_target_pairs={{0,1},{1,0},{2,3},{3,2},{4,5},{5,4},{6,7},{7,6},{8,9},{9,8},{10,11... | collective-permute-start | bytes 1179656 | tf_op jit(solution)/shard_map/ppermute | solution.py:314
  (32 other events, 192.2 us)

commit v5 on v4

--- a/solution.py
+++ b/solution.py
@@ -17,7 +17,7 @@
 PAGE = 128
 QW = 1536
 QKV = 2048
-WIDE = 512
+WIDE = 1024
 ROWS = 256
 EASE = 16
 CHUNKS = 2
@@ -117,10 +117,11 @@
 
 def attend_kernel(q_ref, k_ref, v_ref, begin_ref, across_ref, out_ref):
     count = q_ref.shape[0]
-    for first in range(0, count, ROWS):
+    for first, h in [(f, h) for f in range(0, count, ROWS) for h in range(2)]:
         rows, seen = slice(first, first + ROWS), first + ROWS
+        head = slice(h * HD, (h + 1) * HD)
         scores = lax.dot_general(
-            q_ref[rows, :], k_ref[:seen, :], (((1,), (1,)), ((), ())), preferred_element_type=F32
+            q_ref[rows, head], k_ref[:seen, :], (((1,), (1,)), ((), ())), preferred_element_type=F32
         ) * (1.0 / math.sqrt(HD))
         across = across_ref[:, :seen]
         mine = first + lax.broadcasted_iota(jnp.int32, (ROWS, 1), 0)
@@ -130,7 +131,7 @@
         weights = jnp.exp(scores - highest)
         total = jnp.sum(weights, axis=1, keepdims=True)
         mixed = jnp.dot(weights.astype(BF), v_ref[:seen, :], preferred_element_type=F32)
-        out_ref[rows, :] = (mixed / total).astype(BF)
+        out_ref[rows, head] = (mixed / total).astype(BF)
 
 
 def attend(qkv, begin, index):
@@ -139,15 +140,15 @@
     column = pl.BlockSpec((count, 1), lambda h: (0, 0))
     return pl.pallas_call(
         attend_kernel,
-        grid=(QH,),
+        grid=(QH // 2,),
         in_specs=[
-            pl.BlockSpec((count, HD), lambda h: (0, h)),
-            pl.BlockSpec((count, HD), lambda h: (0, QH + h // per)),
-            pl.BlockSpec((count, HD), lambda h: (0, QH + KVH + h // per)),
+            pl.BlockSpec((count, 2 * HD), lambda h: (0, h)),
+            pl.BlockSpec((count, HD), lambda h: (0, QH + 2 * h // per)),
+            pl.BlockSpec((count, HD), lambda h: (0, QH + KVH + 2 * h // per)),
             column,
             pl.BlockSpec((1, count), lambda h: (0, 0)),
         ],
-        out_specs=pl.BlockSpec((count, HD), lambda h: (0, h)),
+        out_specs=pl.BlockSpec((count, 2 * HD), lambda h: (0, h)),
         out_shape=jax.ShapeDtypeStruct((count, QW), BF),
         compiler_params=pltpu.CompilerParams(vmem_limit_bytes=VMEM),
         cost_estimate=cost(

time: 283 us -> 281 us (level)
  no operation moved by 1% of the time
where the time goes in v5:
time: 281 us; the launch traced here: 280 us
  waiting for transfers between devices  110 us (39%)
  Pallas kernels  69 us (25%)
  starting transfers between devices  41.7 us (15%)
  other arithmetic  34.9 us (12%)
  local copies, waits for them, and re-layouts  18.9 us (7%)
  matrix products  4.14 us (1%)
    all_to_all x4, waiting for transfers between devices, exchange_blk(): return lax.all_to_all(value, 'blk', 0, 0, tiled=True)  45.4 us
    ppermute x25, waiting for transfers between devices, across_rep(): lax.ppermute(value, 'rep', [(i, i ^ mask) for i in range(lax.axis_size('r...  32.7 us
    ppermute x3, waiting for transfers between devices, across_blk(): lax.ppermute(value, 'blk', [(i, i ^ mask) for i in range(lax.axis_size('b...  31.8 us
    pallas_call x2, Pallas kernels, gate_up(): pl.pallas_call(functools.partial(gate_up_kernel, orders), grid=(2,), in_s...  20.2 us
    pallas_call x3, Pallas kernels, down_project(): pl.pallas_call(functools.partial(down_kernel, block, len(weights)), grid_...  19 us
    ppermute x25, starting transfers between devices, across_rep(): lax.ppermute(value, 'rep', [(i, i ^ mask) for i in range(lax.axis_size('r...  18.8 us
    all_to_all x4, starting transfers between devices, exchange_blk(): return lax.all_to_all(value, 'blk', 0, 0, tiled=True)  18.5 us
    concatenate x8, other arithmetic, chip_gather(): held = jnp.concatenate([held, came], axis=0)  13.2 us
  transfers between devices with their start and end apart: 32, of which 15 were waited for; matrix products, arithmetic and copies ran while one was open for 16% of the time, Pallas kernels for 19%

profile of v5, /device:TPU:0, one launch (start us, length us, event | category | flops | bytes accessed | tf_op | source)
XLA Modules:
  0.0 280.4 jit_solution(5285610562377729010)
XLA Ops:
  4.9 2.9 %collective-permute-start.1 = (bf16[1,4,48,1536]{3,2,1,0:T(8,128)(2,1)S(1)}, bf16[1,4,48,1536]{3,2,1,0:T(8,128)(2,1)}, u32[]{:S(2)}, u32[]{:S(2)}) collective-permute-start(bf16[1,4,48,1536]{3,2,1,0:T(8,128)(2,1)S(1)} %bitcast.76), channel_id=1, source_target_pairs={{0,8},{4,12},{8,0},{12,4},{16,24},{20,28},{24,16},{28,20},{1,9},{5... | collective-permute-start | bytes 1769480 | tf_op jit(solution)/shard_map/ppermute | solution.py:319
  10.8 4.9 %all-to-all-start = ((bf16[4,48,3584]{2,1,0:T(8,128)(2,1)}), bf16[4,48,3584]{2,1,0:T(8,128)(2,1)S(1)}, u32[]{:S(2)}, u32[]{:S(2)}) async-start(bf16[4,48,3584]{2,1,0:T(8,128)(2,1)} %broadcast_in_dim.43), calls=%async_computation | async-start | bytes 2752512 | tf_op jit(solution)/shard_map/all_to_all | solution.py:357
  15.7 5.9 %collective-permute-done.1 = bf16[1,4,48,1536]{3,2,1,0:T(8,128)(2,1)} collective-permute-done((bf16[1,4,48,1536]{3,2,1,0:T(8,128)(2,1)S(1)}, bf16[1,4,48,1536]{3,2,1,0:T(8,128)(2,1)}, u32[]{:S(2)}, u32[]{:S(2)}) %collective-permute-start.1) | collective-permute-done | bytes 589856 | tf_op jit(solution)/shard_map/ppermute | solution.py:319
  25.8 4.1 %fusion.2 = bf16[768,1536]{1,0:T(8,128)(2,1)S(1)} fusion(bf16[768,1536]{1,0:T(8,128)(2,1)S(1)} %bitcast.74, s32[1536]{0:T(1024)S(1)} %fusion.23), kind=kOutput, calls=%fused_computation.5 | convolution fusion | flops 3627417600 | bytes 4724736 | tf_op jit(solution)/shard_map/dot_general | solution.py:409
  41.8 6.3 %all-to-all-done = bf16[4,48,3584]{2,1,0:T(8,128)(2,1)S(1)} async-done(((bf16[4,48,3584]{2,1,0:T(8,128)(2,1)}), bf16[4,48,3584]{2,1,0:T(8,128)(2,1)S(1)}, u32[]{:S(2)}, u32[]{:S(2)}) %all-to-all-start) | async-done | bytes 1376288 | tf_op jit(solution)/shard_map/all_to_all | solution.py:357
  48.1 4.3 %all-to-all-start.1 = ((bf16[4,2,2,48,768]{4,3,2,1,0:T(8,128)(2,1)}), bf16[4,2,2,48,768]{4,3,2,1,0:T(8,128)(2,1)}, u32[]{:S(2)}, u32[]{:S(2)}) async-start(bf16[4,2,2,48,768]{4,3,2,1,0:T(8,128)(2,1)} %get-tuple-element.19), calls=%async_computation.1 | async-start | bytes 2359296 | tf_op jit(solution)/shard_map/all_to_all | solution.py:357
  52.4 11.3 %collective-permute-done.4.refs_1_ = bf16[2,4,48,1536]{3,2,1,0:T(8,128)(2,1)} collective-permute-done((bf16[2,4,48,1536]{3,2,1,0:T(8,128)(2,1)}, bf16[2,4,48,1536]{3,2,1,0:T(8,128)(2,1)}, u32[]{:S(2)}, u32[]{:S(2)}) %collective-permute-start.4) | collective-permute-done | bytes 1179680 | tf_op jit(solution)/shard_map/ppermute | solution.py:319
  68.3 12.2 %all-to-all-done.1 = bf16[4,2,2,48,768]{4,3,2,1,0:T(8,128)(2,1)} async-done(((bf16[4,2,2,48,768]{4,3,2,1,0:T(8,128)(2,1)}), bf16[4,2,2,48,768]{4,3,2,1,0:T(8,128)(2,1)}, u32[]{:S(2)}, u32[]{:S(2)}) %all-to-all-start.1) | async-done | bytes 1179680 | tf_op jit(solution)/shard_map/all_to_all | solution.py:357
  86.5 4.9 %all-to-all-start.2 = ((bf16[4,128,1664]{2,1,0:T(8,128)(2,1)}), bf16[4,128,1664]{2,1,0:T(8,128)(2,1)S(1)}, u32[]{:S(2)}, u32[]{:S(2)}) async-start(bf16[4,128,1664]{2,1,0:T(8,128)(2,1)} %broadcast_in_dim.46), calls=%async_computation.2 | async-start | bytes 3407872 | tf_op jit(solution)/shard_map/all_to_all | solution.py:357
  102.9 26.8 %all-to-all-done.2 = bf16[4,128,1664]{2,1,0:T(8,128)(2,1)S(1)} async-done(((bf16[4,128,1664]{2,1,0:T(8,128)(2,1)}), bf16[4,128,1664]{2,1,0:T(8,128)(2,1)S(1)}, u32[]{:S(2)}, u32[]{:S(2)}) %all-to-all-start.2) | async-done | bytes 1703968 | tf_op jit(solution)/shard_map/all_to_all | solution.py:357
  129.8 4.5 %all-to-all-start.3 = ((bf16[4,2,2,48,768]{4,3,2,1,0:T(8,128)(2,1)}), bf16[4,2,2,48,768]{4,3,2,1,0:T(8,128)(2,1)}, u32[]{:S(2)}, u32[]{:S(2)}) async-start(bf16[4,2,2,48,768]{4,3,2,1,0:T(8,128)(2,1)} %get-tuple-element.28), calls=%async_computation.3 | async-start | bytes 2359296 | tf_op jit(solution)/shard_map/all_to_all | solution.py:357
  146.9 8.9 %project.1.q_ref.k_ref.v_ref = bf16[512,2048]{1,0:T(8,128)(2,1)} custom-call(s32[8]{0:T(128)} %mul.141.spots, bf16[512,1536]{1,0:T(8,128)(2,1)} %fusion.5.refs_0_, f32[512,128]{1,0:T(8,128)} %get-tuple-element.74.refs_1_, f32[512,128]{1,0:T(8,128)} %get-tuple-element.75.refs_2_, bf16[2,192,2048]{2,1,0:T(8,128)(2,1)} %copy-done.3, ...), custom_call_target="tpu_custom_call" | custom-call | flops 201326592 | bytes 589824 | tf_op jit(solution)/shard_map/project/pallas_call | solution.py:95
  156.4 11.5 %attend.1.x_ref = bf16[512,1536]{1,0:T(8,128)(2,1)} custom-call(bf16[512,2048]{1,0:T(8,128)(2,1)} %project.1.q_ref.k_ref.v_ref, bf16[512,2048]{1,0:T(8,128)(2,1)} %project.1.q_ref.k_ref.v_ref, bf16[512,2048]{1,0:T(8,128)(2,1)} %project.1.q_ref.k_ref.v_ref, s32[512,1]{1,0:T(8,128)} %copy.66.begin_ref, s32[1,512]{1,0:T(1,128)} %iota.47.across_ref), custom_call_target="tpu_custom_call" | custom-call | flops 100663296 | bytes 229376 | tf_op jit(solution)/shard_map/attend/pallas_call | solution.py:141
  175.5 9.4 %mix.1 = (f32[512,1536]{1,0:T(8,128)}, bf16[512,1536]{1,0:T(8,128)(2,1)}) custom-call(s32[8]{0:T(128)} %mul.137.spots, s32[4]{0:T(128)} %fusion.36.up_spots, bf16[512,1536]{1,0:T(8,128)(2,1)} %attend.1.x_ref, bf16[512,1536]{1,0:T(8,128)(2,1)} %slice.130.tokens_ref, f32[1,1536]{1,0:T(1,128)} %broadcast_in_dim.48.gain_ref, ...), custom_call_target="tpu_custom_call" | custom-call | flops 150994944 | bytes 786432 | tf_op jit(solution)/shard_map/mix/pallas_call | solution.py:187
  191.7 10.1 %gate_up.2.act_ref = bf16[1024,768]{1,0:T(8,128)(2,1)} custom-call(bf16[512,1536]{1,0:T(8,128)(2,1)} %get-tuple-element.27.mine_ref, bf16[512,1536]{1,0:T(8,128)(2,1)} %copy-done.2, f32[1024,4]{1,0:T(8,128)} %get-tuple-element.61.gate_ref, bf16[768,768]{1,0:T(8,128)(2,1)} %bitcast.34.refs_0_, bf16[768,768]{1,0:T(8,128)(2,1)} %bitcast.35.refs_1_, ...), custom_call_target="tpu_custom_call" | custom-call | flops 301989888 | bytes 491520 | tf_op jit(solution)/shard_map/gate_up/pallas_call | solution.py:259
  201.9 7.3 %down.3.refs_2_ = f32[1024,1536]{1,0:T(8,128)} custom-call(s32[4]{0:T(128)} %fusion.34.spots, bf16[1024,768]{1,0:T(8,128)(2,1)} %gate_up.2.act_ref, bf16[2,4,48,1536]{3,2,1,0:T(8,128)(2,1)} %pad_maximum_fusion.3.refs_0_, bf16[2,4,48,1536]{3,2,1,0:T(8,128)(2,1)} %collective-permute-done.4.refs_1_), custom_call_target="tpu_custom_call" | custom-call | flops 150994944 | bytes 1032192 | tf_op jit(solution)/shard_map/down/pallas_call | solution.py:292
  209.2 4.3 %collective-permute-done.21 = bf16[2,384,768]{2,1,0:T(8,128)(2,1)S(1)} collective-permute-done((bf16[2,384,768]{2,1,0:T(8,128)(2,1)S(1)}, bf16[2,384,768]{2,1,0:T(8,128)(2,1)S(1)}, u32[]{:S(2)}, u32[]{:S(2)}) %collective-permute-start.21) | collective-permute-done | bytes 1179680 | tf_op jit(solution)/shard_map/ppermute | solution.py:319
  215.2 10.1 %gate_up.3.act_ref = bf16[1024,768]{1,0:T(8,128)(2,1)} custom-call(bf16[512,1536]{1,0:T(8,128)(2,1)} %get-tuple-element.27.mine_ref, bf16[512,1536]{1,0:T(8,128)(2,1)} %copy-done.2, f32[1024,4]{1,0:T(8,128)} %get-tuple-element.62.gate_ref, bf16[768,768]{1,0:T(8,128)(2,1)} %bitcast.70, bf16[768,768]{1,0:T(8,128)(2,1)} %bitcast.82, bf16[768,768]{1,0:T(8,128)(2,1)} %bitcast.71, ...), custom_call_target="tpu_custom_call" | custom-call | flops 301989888 | bytes 491520 | tf_op jit(solution)/shard_map/gate_up/pallas_call | solution.py:259
  225.2 5.7 %down.5 = bf16[512,1536]{1,0:T(8,128)(2,1)} custom-call(s32[4]{0:T(128)} %get-tuple-element.69.spots, bf16[1024,768]{1,0:T(8,128)(2,1)} %gate_up.3.act_ref, bf16[2,4,48,1536]{3,2,1,0:T(8,128)(2,1)} %copy-done, bf16[2,4,48,1536]{3,2,1,0:T(8,128)(2,1)} %collective-permute-done.5.refs_1_, f32[1024,1536]{1,0:T(8,128)} %down.3.refs_2_), custom_call_target="tpu_custom_call" | custom-call | flops 75497472 | bytes 589824 | tf_op jit(solution)/shard_map/down/pallas_call | solution.py:292
  231.0 6.0 %down.4 = f32[512,1536]{1,0:T(8,128)} custom-call(s32[4]{0:T(128)} %get-tuple-element.69.spots, bf16[1024,768]{1,0:T(8,128)(2,1)} %gate_up.3.act_ref, bf16[2,4,48,1536]{3,2,1,0:T(8,128)(2,1)} %copy-done, bf16[2,4,48,1536]{3,2,1,0:T(8,128)(2,1)} %collective-permute-done.5.refs_1_, f32[1024,1536]{1,0:T(8,128)} %down.3.refs_2_), custom_call_target="tpu_custom_call" | custom-call | flops 75497472 | bytes 589824 | tf_op jit(solution)/shard_map/down/pallas_call | solution.py:292
  237.0 2.8 %add_convert_fusion.3 = (bf16[128,1536]{1,0:T(8,128)(2,1)}, bf16[128,1536]{1,0:T(8,128)(2,1)}, bf16[128,1536]{1,0:T(8,128)(2,1)}) fusion(f32[512,1536]{1,0:T(8,128)} %down.4, s32[]{:T(128)S(6)} %select_n.150, bf16[512,1536]{1,0:T(8,128)(2,1)S(1)} %collective-permute-done.24, s32[]{:T(128)S(6)} %select_n.152, s32[]{:T(128)S(6)} %select_n.151), kind=kLoop, calls=%fused_computation.35 | loop fusion | flops 1769472 | bytes 4718604 | tf_op jit(solution)/shard_map/convert_element_type | solution.py:542
  239.8 3.5 %collective-permute-start.27 = (bf16[128,1536]{1,0:T(8,128)(2,1)}, bf16[128,1536]{1,0:T(8,128)(2,1)S(1)}, u32[]{:S(2)}, u32[]{:S(2)}) collective-permute-start(bf16[128,1536]{1,0:T(8,128)(2,1)} %get-tuple-element.35), channel_id=1, source_target_pairs={{0,3},{1,2},{2,1},{3,0},{4,7},{5,6},{6,5},{7,4},{8,11},{9,10},{10,... | collective-permute-start | bytes 1179656 | tf_op jit(solution)/shard_map/ppermute | solution.py:315
  246.1 7.7 %collective-permute-done.27 = bf16[128,1536]{1,0:T(8,128)(2,1)S(1)} collective-permute-done((bf16[128,1536]{1,0:T(8,128)(2,1)}, bf16[128,1536]{1,0:T(8,128)(2,1)S(1)}, u32[]{:S(2)}, u32[]{:S(2)}) %collective-permute-start.27) | collective-permute-done | bytes 393248 | tf_op jit(solution)/shard_map/ppermute | solution.py:315
  253.8 24.1 %collective-permute-done.26 = bf16[128,1536]{1,0:T(8,128)(2,1)S(1)} collective-permute-done((bf16[128,1536]{1,0:T(8,128)(2,1)}, bf16[128,1536]{1,0:T(8,128)(2,1)S(1)}, u32[]{:S(2)}, u32[]{:S(2)}) %collective-permute-start.26) | collective-permute-done | bytes 393248 | tf_op jit(solution)/shard_map/ppermute | solution.py:315
  (167 shorter events, 79.0 us)
Async XLA Ops:
  4.9 16.7 %collective-permute-start.1 = (bf16[1,4,48,1536]{3,2,1,0:T(8,128)(2,1)S(1)}, bf16[1,4,48,1536]{3,2,1,0:T(8,128)(2,1)}, u32[]{:S(2)}, u32[]{:S(2)}) collective-permute-start(bf16[1,4,48,1536]{3,2,1,0:T(8,128)(2,1)S(1)} %bitcast.76), channel_id=1, source_target_pairs={{0,8},{4,12},{8,0},{12,4},{16,24},{20,28},{24,16},{28,20},{1,9},{5... | collective-permute-start | bytes 1769480 | tf_op jit(solution)/shard_map/ppermute | solution.py:319
  7.9 15.3 %collective-permute-start.2 = (bf16[1,4,48,1536]{3,2,1,0:T(8,128)(2,1)S(1)}, bf16[1,4,48,1536]{3,2,1,0:T(8,128)(2,1)}, u32[]{:S(2)}, u32[]{:S(2)}) collective-permute-start(bf16[1,4,48,1536]{3,2,1,0:T(8,128)(2,1)S(1)} %bitcast.78), channel_id=1, source_target_pairs={{0,16},{4,20},{8,24},{12,28},{16,0},{20,4},{24,8},{28,12},{1,17},{... | collective-permute-start | bytes 1769480 | tf_op jit(solution)/shard_map/ppermute | solution.py:319
  10.8 37.4 %all-to-all-start = ((bf16[4,48,3584]{2,1,0:T(8,128)(2,1)}), bf16[4,48,3584]{2,1,0:T(8,128)(2,1)S(1)}, u32[]{:S(2)}, u32[]{:S(2)}) async-start(bf16[4,48,3584]{2,1,0:T(8,128)(2,1)} %broadcast_in_dim.43), calls=%async_computation | async-start | bytes 2752512 | tf_op jit(solution)/shard_map/all_to_all | solution.py:357
  35.0 28.7 %collective-permute-start.4 = (bf16[2,4,48,1536]{3,2,1,0:T(8,128)(2,1)}, bf16[2,4,48,1536]{3,2,1,0:T(8,128)(2,1)}, u32[]{:S(2)}, u32[]{:S(2)}) collective-permute-start(bf16[2,4,48,1536]{3,2,1,0:T(8,128)(2,1)} %pad_maximum_fusion.3.refs_0_), channel_id=1, source_target_pairs={{0,16},{4,20},{8,24},{12,28},{16,0},{20,4},{24,8},{28,12},{1,17},{... | collective-permute-start | bytes 3538952 | tf_op jit(solution)/shard_map/ppermute | solution.py:319
  37.7 28.3 %collective-permute-start.5 = (bf16[2,4,48,1536]{3,2,1,0:T(8,128)(2,1)S(1)}, bf16[2,4,48,1536]{3,2,1,0:T(8,128)(2,1)}, u32[]{:S(2)}, u32[]{:S(2)}) collective-permute-start(bf16[2,4,48,1536]{3,2,1,0:T(8,128)(2,1)S(1)} %pad_maximum_fusion.4.refs_0_), channel_id=1, source_target_pairs={{0,8},{4,12},{8,0},{12,4},{16,24},{20,28},{24,16},{28,20},{1,9},{5... | collective-permute-start | bytes 3538952 | tf_op jit(solution)/shard_map/ppermute | solution.py:319
  48.1 32.4 %all-to-all-start.1 = ((bf16[4,2,2,48,768]{4,3,2,1,0:T(8,128)(2,1)}), bf16[4,2,2,48,768]{4,3,2,1,0:T(8,128)(2,1)}, u32[]{:S(2)}, u32[]{:S(2)}) async-start(bf16[4,2,2,48,768]{4,3,2,1,0:T(8,128)(2,1)} %get-tuple-element.19), calls=%async_computation.1 | async-start | bytes 2359296 | tf_op jit(solution)/shard_map/all_to_all | solution.py:357
  66.1 18.9 %collective-permute-start.6 = (bf16[1,192,2048]{2,1,0:T(8,128)(2,1)S(1)}, bf16[1,192,2048]{2,1,0:T(8,128)(2,1)S(1)}, u32[]{:S(2)}, u32[]{:S(2)}) collective-permute-start(bf16[1,192,2048]{2,1,0:T(8,128)(2,1)S(1)} %slice_bitcast_fusion.2), channel_id=1, source_target_pairs={{0,8},{4,12},{8,0},{12,4},{16,24},{20,28},{24,16},{28,20},{1,9},{5... | collective-permute-start | bytes 2359304 | tf_op jit(solution)/shard_map/ppermute | solution.py:319
  66.7 16.1 %collective-permute-start.7 = (bf16[1,192,1536]{2,1,0:T(8,128)(2,1)S(1)}, bf16[1,192,1536]{2,1,0:T(8,128)(2,1)S(1)}, u32[]{:S(2)}, u32[]{:S(2)}) collective-permute-start(bf16[1,192,1536]{2,1,0:T(8,128)(2,1)S(1)} %slice_bitcast_fusion.3), channel_id=1, source_target_pairs={{0,16},{4,20},{8,24},{12,28},{16,0},{20,4},{24,8},{28,12},{1,17},{... | collective-permute-start | bytes 1769480 | tf_op jit(solution)/shard_map/ppermute | solution.py:319
  86.5 43.3 %all-to-all-start.2 = ((bf16[4,128,1664]{2,1,0:T(8,128)(2,1)}), bf16[4,128,1664]{2,1,0:T(8,128)(2,1)S(1)}, u32[]{:S(2)}, u32[]{:S(2)}) async-start(bf16[4,128,1664]{2,1,0:T(8,128)(2,1)} %broadcast_in_dim.46), calls=%async_computation.2 | async-start | bytes 3407872 | tf_op jit(solution)/shard_map/all_to_all | solution.py:357
  93.1 41.2 %collective-permute-start.10 = (bf16[2,192,2048]{2,1,0:T(8,128)(2,1)S(1)}, bf16[2,192,2048]{2,1,0:T(8,128)(2,1)}, u32[]{:S(2)}, u32[]{:S(2)}) collective-permute-start(bf16[2,192,2048]{2,1,0:T(8,128)(2,1)S(1)} %pad_maximum_fusion.1.refs_3_), channel_id=1, source_target_pairs={{0,16},{4,20},{8,24},{12,28},{16,0},{20,4},{24,8},{28,12},{1,17},{... | collective-permute-start | bytes 4718600 | tf_op jit(solution)/shard_map/ppermute | solution.py:319
  96.2 40.1 %collective-permute-start.15 = (bf16[2,192,1536]{2,1,0:T(8,128)(2,1)}, bf16[2,192,1536]{2,1,0:T(8,128)(2,1)}, u32[]{:S(2)}, u32[]{:S(2)}) collective-permute-start(bf16[2,192,1536]{2,1,0:T(8,128)(2,1)} %pad_maximum_fusion.7.refs_0_), channel_id=1, source_target_pairs={{0,8},{4,12},{8,0},{12,4},{16,24},{20,28},{24,16},{28,20},{1,9},{5... | collective-permute-start | bytes 3538952 | tf_op jit(solution)/shard_map/ppermute | solution.py:319
  97.3 46.2 %collective-permute-start.11 = (bf16[2,192,2048]{2,1,0:T(8,128)(2,1)S(1)}, bf16[2,192,2048]{2,1,0:T(8,128)(2,1)}, u32[]{:S(2)}, u32[]{:S(2)}) collective-permute-start(bf16[2,192,2048]{2,1,0:T(8,128)(2,1)S(1)} %pad_maximum_fusion.1.refs_3_), channel_id=1, source_target_pairs={{0,4},{4,0},{8,12},{12,8},{16,20},{20,16},{24,28},{28,24},{1,5},{5... | collective-permute-start | bytes 4718600 | tf_op jit(solution)/shard_map/ppermute | solution.py:319
  98.4 38.5 %collective-permute-start.8 = (bf16[1,384,768]{2,1,0:T(8,128)(2,1)}, bf16[1,384,768]{2,1,0:T(8,128)(2,1)}, u32[]{:S(2)}, u32[]{:S(2)}) collective-permute-start(bf16[1,384,768]{2,1,0:T(8,128)(2,1)} %bitcast.22), channel_id=1, source_target_pairs={{0,8},{4,12},{8,0},{12,4},{16,24},{20,28},{24,16},{28,20},{1,9},{5... | collective-permute-start | bytes 1769480 | tf_op jit(solution)/shard_map/ppermute | solution.py:319
  101.4 39.0 %collective-permute-start.9 = (bf16[1,384,768]{2,1,0:T(8,128)(2,1)}, bf16[1,384,768]{2,1,0:T(8,128)(2,1)}, u32[]{:S(2)}, u32[]{:S(2)}) collective-permute-start(bf16[1,384,768]{2,1,0:T(8,128)(2,1)} %bitcast.80), channel_id=1, source_target_pairs={{0,16},{4,20},{8,24},{12,28},{16,0},{20,4},{24,8},{28,12},{1,17},{... | collective-permute-start | bytes 1769480 | tf_op jit(solution)/shard_map/ppermute | solution.py:319
  129.8 38.1 %all-to-all-start.3 = ((bf16[4,2,2,48,768]{4,3,2,1,0:T(8,128)(2,1)}), bf16[4,2,2,48,768]{4,3,2,1,0:T(8,128)(2,1)}, u32[]{:S(2)}, u32[]{:S(2)}) async-start(bf16[4,2,2,48,768]{4,3,2,1,0:T(8,128)(2,1)} %get-tuple-element.28), calls=%async_computation.3 | async-start | bytes 2359296 | tf_op jit(solution)/shard_map/all_to_all | solution.py:357
  136.3 39.1 %collective-permute-start.16 = (bf16[2,192,1536]{2,1,0:T(8,128)(2,1)}, bf16[2,192,1536]{2,1,0:T(8,128)(2,1)}, u32[]{:S(2)}, u32[]{:S(2)}) collective-permute-start(bf16[2,192,1536]{2,1,0:T(8,128)(2,1)} %pad_maximum_fusion.7.refs_0_), channel_id=1, source_target_pairs={{0,4},{4,0},{8,12},{12,8},{16,20},{20,16},{24,28},{28,24},{1,5},{5... | collective-permute-start | bytes 3538952 | tf_op jit(solution)/shard_map/ppermute | solution.py:319
  136.8 38.7 %collective-permute-start.17 = (bf16[2,192,1536]{2,1,0:T(8,128)(2,1)}, bf16[2,192,1536]{2,1,0:T(8,128)(2,1)}, u32[]{:S(2)}, u32[]{:S(2)}) collective-permute-start(bf16[2,192,1536]{2,1,0:T(8,128)(2,1)} %collective-permute-done.15.refs_1_), channel_id=1, source_target_pairs={{0,4},{4,0},{8,12},{12,8},{16,20},{20,16},{24,28},{28,24},{1,5},{5... | collective-permute-start | bytes 3538952 | tf_op jit(solution)/shard_map/ppermute | solution.py:319
  140.4 30.5 %collective-permute-start.13 = (bf16[2,384,768]{2,1,0:T(8,128)(2,1)}, bf16[2,384,768]{2,1,0:T(8,128)(2,1)}, u32[]{:S(2)}, u32[]{:S(2)}) collective-permute-start(bf16[2,384,768]{2,1,0:T(8,128)(2,1)} %pad_maximum_fusion.5), channel_id=1, source_target_pairs={{0,16},{4,20},{8,24},{12,28},{16,0},{20,4},{24,8},{28,12},{1,17},{... | collective-permute-start | bytes 3538952 | tf_op jit(solution)/shard_map/ppermute | solution.py:319
  143.5 32.0 %collective-permute-start.14 = (bf16[2,384,768]{2,1,0:T(8,128)(2,1)}, bf16[2,384,768]{2,1,0:T(8,128)(2,1)}, u32[]{:S(2)}, u32[]{:S(2)}) collective-permute-start(bf16[2,384,768]{2,1,0:T(8,128)(2,1)} %pad_maximum_fusion.6), channel_id=1, source_target_pairs={{0,8},{4,12},{8,0},{12,4},{16,24},{20,28},{24,16},{28,20},{1,9},{5... | collective-permute-start | bytes 3538952 | tf_op jit(solution)/shard_map/ppermute | solution.py:319
  169.3 15.5 %collective-permute-start.20 = (bf16[1,384,768]{2,1,0:T(8,128)(2,1)S(1)}, bf16[1,384,768]{2,1,0:T(8,128)(2,1)S(1)}, u32[]{:S(2)}, u32[]{:S(2)}) collective-permute-start(bf16[1,384,768]{2,1,0:T(8,128)(2,1)S(1)} %get-tuple-element.46), channel_id=1, source_target_pairs={{0,8},{4,12},{8,0},{12,4},{16,24},{20,28},{24,16},{28,20},{1,9},{5... | collective-permute-start | bytes 1769480 | tf_op jit(solution)/shard_map/ppermute | solution.py:319
  185.0 28.4 %collective-permute-start.21 = (bf16[2,384,768]{2,1,0:T(8,128)(2,1)S(1)}, bf16[2,384,768]{2,1,0:T(8,128)(2,1)S(1)}, u32[]{:S(2)}, u32[]{:S(2)}) collective-permute-start(bf16[2,384,768]{2,1,0:T(8,128)(2,1)S(1)} %pad_maximum_fusion.8), channel_id=1, source_target_pairs={{0,16},{4,20},{8,24},{12,28},{16,0},{20,4},{24,8},{28,12},{1,17},{... | collective-permute-start | bytes 3538952 | tf_op jit(solution)/shard_map/ppermute | solution.py:319
  186.8 28.4 %collective-permute-start.23 = (bf16[2,384,768]{2,1,0:T(8,128)(2,1)S(1)}, bf16[2,384,768]{2,1,0:T(8,128)(2,1)}, u32[]{:S(2)}, u32[]{:S(2)}) collective-permute-start(bf16[2,384,768]{2,1,0:T(8,128)(2,1)S(1)} %pad_maximum_fusion.9), channel_id=1, source_target_pairs={{0,8},{4,12},{8,0},{12,4},{16,24},{20,28},{24,16},{28,20},{1,9},{5... | collective-permute-start | bytes 3538952 | tf_op jit(solution)/shard_map/ppermute | solution.py:319
  243.3 34.7 %collective-permute-start.26 = (bf16[128,1536]{1,0:T(8,128)(2,1)}, bf16[128,1536]{1,0:T(8,128)(2,1)S(1)}, u32[]{:S(2)}, u32[]{:S(2)}) collective-permute-start(bf16[128,1536]{1,0:T(8,128)(2,1)} %get-tuple-element.36), channel_id=1, source_target_pairs={{0,2},{1,3},{2,0},{3,1},{4,6},{5,7},{6,4},{7,5},{8,10},{9,11},{10,... | collective-permute-start | bytes 1179656 | tf_op jit(solution)/shard_map/ppermute | solution.py:315
  243.3 34.7 %collective-permute-start.25 = (bf16[128,1536]{1,0:T(8,128)(2,1)}, bf16[128,1536]{1,0:T(8,128)(2,1)S(1)}, u32[]{:S(2)}, u32[]{:S(2)}) collective-permute-start(bf16[128,1536]{1,0:T(8,128)(2,1)} %get-tuple-element.34), channel_id=1, source_target_pairs={{0,1},{1,0},{2,3},{3,2},{4,5},{5,4},{6,7},{7,6},{8,9},{9,8},{10,11... | collective-permute-start | bytes 1179656 | tf_op jit(solution)/shard_map/ppermute | solution.py:315
  (32 other events, 192.2 us)

commit v6 on v5

--- a/solution.py
+++ b/solution.py
@@ -117,7 +117,7 @@
 
 def attend_kernel(q_ref, k_ref, v_ref, begin_ref, across_ref, out_ref):
     count = q_ref.shape[0]
-    for first, h in [(f, h) for f in range(0, count, ROWS) for h in range(2)]:
+    for first, h in [(f, h) for f in range(0, count, ROWS) for h in range(3)]:
         rows, seen = slice(first, first + ROWS), first + ROWS
         head = slice(h * HD, (h + 1) * HD)
         scores = lax.dot_general(
@@ -140,15 +140,15 @@
     column = pl.BlockSpec((count, 1), lambda h: (0, 0))
     return pl.pallas_call(
         attend_kernel,
-        grid=(QH // 2,),
+        grid=(QH // 3,),
         in_specs=[
-            pl.BlockSpec((count, 2 * HD), lambda h: (0, h)),
-            pl.BlockSpec((count, HD), lambda h: (0, QH + 2 * h // per)),
-            pl.BlockSpec((count, HD), lambda h: (0, QH + KVH + 2 * h // per)),
+            pl.BlockSpec((count, 3 * HD), lambda h: (0, h)),
+            pl.BlockSpec((count, HD), lambda h: (0, QH + 3 * h // per)),
+            pl.BlockSpec((count, HD), lambda h: (0, QH + KVH + 3 * h // per)),
             column,
             pl.BlockSpec((1, count), lambda h: (0, 0)),
         ],
-        out_specs=pl.BlockSpec((count, 2 * HD), lambda h: (0, h)),
+        out_specs=pl.BlockSpec((count, 3 * HD), lambda h: (0, h)),
         out_shape=jax.ShapeDtypeStruct((count, QW), BF),
         compiler_params=pltpu.CompilerParams(vmem_limit_bytes=VMEM),
         cost_estimate=cost(

time: 281 us -> 282 us (level)
  no operation moved by 1% of the time
where the time goes in v6:
time: 282 us; the launch traced here: 281 us
  waiting for transfers between devices  110 us (39%)
  Pallas kernels  69.3 us (25%)
  starting transfers between devices  41.7 us (15%)
  other arithmetic  34.9 us (12%)
  local copies, waits for them, and re-layouts  18.9 us (7%)
  matrix products  4.14 us (1%)
    all_to_all x4, waiting for transfers between devices, exchange_blk(): return lax.all_to_all(value, 'blk', 0, 0, tiled=True)  45.4 us
    ppermute x25, waiting for transfers between devices, across_rep(): lax.ppermute(value, 'rep', [(i, i ^ mask) for i in range(lax.axis_size('r...  32.7 us
    ppermute x3, waiting for transfers between devices, across_blk(): lax.ppermute(value, 'blk', [(i, i ^ mask) for i in range(lax.axis_size('b...  31.8 us
    pallas_call x2, Pallas kernels, gate_up(): pl.pallas_call(functools.partial(gate_up_kernel, orders), grid=(2,), in_s...  20.2 us
    pallas_call x3, Pallas kernels, down_project(): pl.pallas_call(functools.partial(down_kernel, block, len(weights)), grid_...  19 us
    ppermute x25, starting transfers between devices, across_rep(): lax.ppermute(value, 'rep', [(i, i ^ mask) for i in range(lax.axis_size('r...  18.8 us
    all_to_all x4, starting transfers between devices, exchange_blk(): return lax.all_to_all(value, 'blk', 0, 0, tiled=True)  18.5 us
    concatenate x8, other arithmetic, chip_gather(): held = jnp.concatenate([held, came], axis=0)  13.2 us
  transfers between devices with their start and end apart: 32, of which 15 were waited for; matrix products, arithmetic and copies ran while one was open for 16% of the time, Pallas kernels for 19%

profile of v6, /device:TPU:0, one launch (start us, length us, event | category | flops | bytes accessed | tf_op | source)
XLA Modules:
  0.0 280.7 jit_solution(18028988439548421266)
XLA Ops:
  4.9 2.9 %collective-permute-start.1 = (bf16[1,4,48,1536]{3,2,1,0:T(8,128)(2,1)S(1)}, bf16[1,4,48,1536]{3,2,1,0:T(8,128)(2,1)}, u32[]{:S(2)}, u32[]{:S(2)}) collective-permute-start(bf16[1,4,48,1536]{3,2,1,0:T(8,128)(2,1)S(1)} %bitcast.76), channel_id=1, source_target_pairs={{0,8},{4,12},{8,0},{12,4},{16,24},{20,28},{24,16},{28,20},{1,9},{5... | collective-permute-start | bytes 1769480 | tf_op jit(solution)/shard_map/ppermute | solution.py:319
  10.8 4.9 %all-to-all-start = ((bf16[4,48,3584]{2,1,0:T(8,128)(2,1)}), bf16[4,48,3584]{2,1,0:T(8,128)(2,1)S(1)}, u32[]{:S(2)}, u32[]{:S(2)}) async-start(bf16[4,48,3584]{2,1,0:T(8,128)(2,1)} %broadcast_in_dim.43), calls=%async_computation | async-start | bytes 2752512 | tf_op jit(solution)/shard_map/all_to_all | solution.py:357
  15.7 5.9 %collective-permute-done.1 = bf16[1,4,48,1536]{3,2,1,0:T(8,128)(2,1)} collective-permute-done((bf16[1,4,48,1536]{3,2,1,0:T(8,128)(2,1)S(1)}, bf16[1,4,48,1536]{3,2,1,0:T(8,128)(2,1)}, u32[]{:S(2)}, u32[]{:S(2)}) %collective-permute-start.1) | collective-permute-done | bytes 589856 | tf_op jit(solution)/shard_map/ppermute | solution.py:319
  25.8 4.1 %fusion.2 = bf16[768,1536]{1,0:T(8,128)(2,1)S(1)} fusion(bf16[768,1536]{1,0:T(8,128)(2,1)S(1)} %bitcast.74, s32[1536]{0:T(1024)S(1)} %fusion.23), kind=kOutput, calls=%fused_computation.5 | convolution fusion | flops 3627417600 | bytes 4724736 | tf_op jit(solution)/shard_map/dot_general | solution.py:409
  41.8 6.3 %all-to-all-done = bf16[4,48,3584]{2,1,0:T(8,128)(2,1)S(1)} async-done(((bf16[4,48,3584]{2,1,0:T(8,128)(2,1)}), bf16[4,48,3584]{2,1,0:T(8,128)(2,1)S(1)}, u32[]{:S(2)}, u32[]{:S(2)}) %all-to-all-start) | async-done | bytes 1376288 | tf_op jit(solution)/shard_map/all_to_all | solution.py:357
  48.1 4.3 %all-to-all-start.1 = ((bf16[4,2,2,48,768]{4,3,2,1,0:T(8,128)(2,1)}), bf16[4,2,2,48,768]{4,3,2,1,0:T(8,128)(2,1)}, u32[]{:S(2)}, u32[]{:S(2)}) async-start(bf16[4,2,2,48,768]{4,3,2,1,0:T(8,128)(2,1)} %get-tuple-element.19), calls=%async_computation.1 | async-start | bytes 2359296 | tf_op jit(solution)/shard_map/all_to_all | solution.py:357
  52.4 11.3 %collective-permute-done.4.refs_1_ = bf16[2,4,48,1536]{3,2,1,0:T(8,128)(2,1)} collective-permute-done((bf16[2,4,48,1536]{3,2,1,0:T(8,128)(2,1)}, bf16[2,4,48,1536]{3,2,1,0:T(8,128)(2,1)}, u32[]{:S(2)}, u32[]{:S(2)}) %collective-permute-start.4) | collective-permute-done | bytes 1179680 | tf_op jit(solution)/shard_map/ppermute | solution.py:319
  68.3 12.2 %all-to-all-done.1 = bf16[4,2,2,48,768]{4,3,2,1,0:T(8,128)(2,1)} async-done(((bf16[4,2,2,48,768]{4,3,2,1,0:T(8,128)(2,1)}), bf16[4,2,2,48,768]{4,3,2,1,0:T(8,128)(2,1)}, u32[]{:S(2)}, u32[]{:S(2)}) %all-to-all-start.1) | async-done | bytes 1179680 | tf_op jit(solution)/shard_map/all_to_all | solution.py:357
  86.5 4.9 %all-to-all-start.2 = ((bf16[4,128,1664]{2,1,0:T(8,128)(2,1)}), bf16[4,128,1664]{2,1,0:T(8,128)(2,1)S(1)}, u32[]{:S(2)}, u32[]{:S(2)}) async-start(bf16[4,128,1664]{2,1,0:T(8,128)(2,1)} %broadcast_in_dim.46), calls=%async_computation.2 | async-start | bytes 3407872 | tf_op jit(solution)/shard_map/all_to_all | solution.py:357
  102.9 26.8 %all-to-all-done.2 = bf16[4,128,1664]{2,1,0:T(8,128)(2,1)S(1)} async-done(((bf16[4,128,1664]{2,1,0:T(8,128)(2,1)}), bf16[4,128,1664]{2,1,0:T(8,128)(2,1)S(1)}, u32[]{:S(2)}, u32[]{:S(2)}) %all-to-all-start.2) | async-done | bytes 1703968 | tf_op jit(solution)/shard_map/all_to_all | solution.py:357
  129.8 4.5 %all-to-all-start.3 = ((bf16[4,2,2,48,768]{4,3,2,1,0:T(8,128)(2,1)}), bf16[4,2,2,48,768]{4,3,2,1,0:T(8,128)(2,1)}, u32[]{:S(2)}, u32[]{:S(2)}) async-start(bf16[4,2,2,48,768]{4,3,2,1,0:T(8,128)(2,1)} %get-tuple-element.28), calls=%async_computation.3 | async-start | bytes 2359296 | tf_op jit(solution)/shard_map/all_to_all | solution.py:357
  146.9 8.9 %project.1.q_ref.k_ref.v_ref = bf16[512,2048]{1,0:T(8,128)(2,1)} custom-call(s32[8]{0:T(128)} %mul.141.spots, bf16[512,1536]{1,0:T(8,128)(2,1)} %fusion.5.refs_0_, f32[512,128]{1,0:T(8,128)} %get-tuple-element.74.refs_1_, f32[512,128]{1,0:T(8,128)} %get-tuple-element.75.refs_2_, bf16[2,192,2048]{2,1,0:T(8,128)(2,1)} %copy-done.3, ...), custom_call_target="tpu_custom_call" | custom-call | flops 201326592 | bytes 589824 | tf_op jit(solution)/shard_map/project/pallas_call | solution.py:95
  156.4 11.8 %attend.1.x_ref = bf16[512,1536]{1,0:T(8,128)(2,1)} custom-call(bf16[512,2048]{1,0:T(8,128)(2,1)} %project.1.q_ref.k_ref.v_ref, bf16[512,2048]{1,0:T(8,128)(2,1)} %project.1.q_ref.k_ref.v_ref, bf16[512,2048]{1,0:T(8,128)(2,1)} %project.1.q_ref.k_ref.v_ref, s32[512,1]{1,0:T(8,128)} %copy.66.begin_ref, s32[1,512]{1,0:T(1,128)} %iota.47.across_ref), custom_call_target="tpu_custom_call" | custom-call | flops 100663296 | bytes 229376 | tf_op jit(solution)/shard_map/attend/pallas_call | solution.py:141
  175.8 9.4 %mix.1 = (f32[512,1536]{1,0:T(8,128)}, bf16[512,1536]{1,0:T(8,128)(2,1)}) custom-call(s32[8]{0:T(128)} %mul.137.spots, s32[4]{0:T(128)} %fusion.36.up_spots, bf16[512,1536]{1,0:T(8,128)(2,1)} %attend.1.x_ref, bf16[512,1536]{1,0:T(8,128)(2,1)} %slice.130.tokens_ref, f32[1,1536]{1,0:T(1,128)} %broadcast_in_dim.48.gain_ref, ...), custom_call_target="tpu_custom_call" | custom-call | flops 150994944 | bytes 786432 | tf_op jit(solution)/shard_map/mix/pallas_call | solution.py:187
  192.1 10.1 %gate_up.2.act_ref = bf16[1024,768]{1,0:T(8,128)(2,1)} custom-call(bf16[512,1536]{1,0:T(8,128)(2,1)} %get-tuple-element.27.mine_ref, bf16[512,1536]{1,0:T(8,128)(2,1)} %copy-done.2, f32[1024,4]{1,0:T(8,128)} %get-tuple-element.61.gate_ref, bf16[768,768]{1,0:T(8,128)(2,1)} %bitcast.34.refs_0_, bf16[768,768]{1,0:T(8,128)(2,1)} %bitcast.35.refs_1_, ...), custom_call_target="tpu_custom_call" | custom-call | flops 301989888 | bytes 491520 | tf_op jit(solution)/shard_map/gate_up/pallas_call | solution.py:259
  202.2 7.3 %down.3.refs_2_ = f32[1024,1536]{1,0:T(8,128)} custom-call(s32[4]{0:T(128)} %fusion.34.spots, bf16[1024,768]{1,0:T(8,128)(2,1)} %gate_up.2.act_ref, bf16[2,4,48,1536]{3,2,1,0:T(8,128)(2,1)} %pad_maximum_fusion.3.refs_0_, bf16[2,4,48,1536]{3,2,1,0:T(8,128)(2,1)} %collective-permute-done.4.refs_1_), custom_call_target="tpu_custom_call" | custom-call | flops 150994944 | bytes 1032192 | tf_op jit(solution)/shard_map/down/pallas_call | solution.py:292
  209.5 4.3 %collective-permute-done.21 = bf16[2,384,768]{2,1,0:T(8,128)(2,1)S(1)} collective-permute-done((bf16[2,384,768]{2,1,0:T(8,128)(2,1)S(1)}, bf16[2,384,768]{2,1,0:T(8,128)(2,1)S(1)}, u32[]{:S(2)}, u32[]{:S(2)}) %collective-permute-start.21) | collective-permute-done | bytes 1179680 | tf_op jit(solution)/shard_map/ppermute | solution.py:319
  215.5 10.1 %gate_up.3.act_ref = bf16[1024,768]{1,0:T(8,128)(2,1)} custom-call(bf16[512,1536]{1,0:T(8,128)(2,1)} %get-tuple-element.27.mine_ref, bf16[512,1536]{1,0:T(8,128)(2,1)} %copy-done.2, f32[1024,4]{1,0:T(8,128)} %get-tuple-element.62.gate_ref, bf16[768,768]{1,0:T(8,128)(2,1)} %bitcast.70, bf16[768,768]{1,0:T(8,128)(2,1)} %bitcast.82, bf16[768,768]{1,0:T(8,128)(2,1)} %bitcast.71, ...), custom_call_target="tpu_custom_call" | custom-call | flops 301989888 | bytes 491520 | tf_op jit(solution)/shard_map/gate_up/pallas_call | solution.py:259
  225.6 5.7 %down.5 = bf16[512,1536]{1,0:T(8,128)(2,1)} custom-call(s32[4]{0:T(128)} %get-tuple-element.69.spots, bf16[1024,768]{1,0:T(8,128)(2,1)} %gate_up.3.act_ref, bf16[2,4,48,1536]{3,2,1,0:T(8,128)(2,1)} %copy-done, bf16[2,4,48,1536]{3,2,1,0:T(8,128)(2,1)} %collective-permute-done.5.refs_1_, f32[1024,1536]{1,0:T(8,128)} %down.3.refs_2_), custom_call_target="tpu_custom_call" | custom-call | flops 75497472 | bytes 589824 | tf_op jit(solution)/shard_map/down/pallas_call | solution.py:292
  231.3 6.0 %down.4 = f32[512,1536]{1,0:T(8,128)} custom-call(s32[4]{0:T(128)} %get-tuple-element.69.spots, bf16[1024,768]{1,0:T(8,128)(2,1)} %gate_up.3.act_ref, bf16[2,4,48,1536]{3,2,1,0:T(8,128)(2,1)} %copy-done, bf16[2,4,48,1536]{3,2,1,0:T(8,128)(2,1)} %collective-permute-done.5.refs_1_, f32[1024,1536]{1,0:T(8,128)} %down.3.refs_2_), custom_call_target="tpu_custom_call" | custom-call | flops 75497472 | bytes 589824 | tf_op jit(solution)/shard_map/down/pallas_call | solution.py:292
  237.3 2.8 %add_convert_fusion.3 = (bf16[128,1536]{1,0:T(8,128)(2,1)}, bf16[128,1536]{1,0:T(8,128)(2,1)}, bf16[128,1536]{1,0:T(8,128)(2,1)}) fusion(f32[512,1536]{1,0:T(8,128)} %down.4, s32[]{:T(128)S(6)} %select_n.150, bf16[512,1536]{1,0:T(8,128)(2,1)S(1)} %collective-permute-done.24, s32[]{:T(128)S(6)} %select_n.152, s32[]{:T(128)S(6)} %select_n.151), kind=kLoop, calls=%fused_computation.35 | loop fusion | flops 1769472 | bytes 4718604 | tf_op jit(solution)/shard_map/convert_element_type | solution.py:542
  240.1 3.5 %collective-permute-start.27 = (bf16[128,1536]{1,0:T(8,128)(2,1)}, bf16[128,1536]{1,0:T(8,128)(2,1)S(1)}, u32[]{:S(2)}, u32[]{:S(2)}) collective-permute-start(bf16[128,1536]{1,0:T(8,128)(2,1)} %get-tuple-element.35), channel_id=1, source_target_pairs={{0,3},{1,2},{2,1},{3,0},{4,7},{5,6},{6,5},{7,4},{8,11},{9,10},{10,... | collective-permute-start | bytes 1179656 | tf_op jit(solution)/shard_map/ppermute | solution.py:315
  246.4 7.7 %collective-permute-done.27 = bf16[128,1536]{1,0:T(8,128)(2,1)S(1)} collective-permute-done((bf16[128,1536]{1,0:T(8,128)(2,1)}, bf16[128,1536]{1,0:T(8,128)(2,1)S(1)}, u32[]{:S(2)}, u32[]{:S(2)}) %collective-permute-start.27) | collective-permute-done | bytes 393248 | tf_op jit(solution)/shard_map/ppermute | solution.py:315
  254.1 24.1 %collective-permute-done.26 = bf16[128,1536]{1,0:T(8,128)(2,1)S(1)} collective-permute-done((bf16[128,1536]{1,0:T(8,128)(2,1)}, bf16[128,1536]{1,0:T(8,128)(2,1)S(1)}, u32[]{:S(2)}, u32[]{:S(2)}) %collective-permute-start.26) | collective-permute-done | bytes 393248 | tf_op jit(solution)/shard_map/ppermute | solution.py:315
  (167 shorter events, 79.0 us)
Async XLA Ops:
  4.9 16.7 %collective-permute-start.1 = (bf16[1,4,48,1536]{3,2,1,0:T(8,128)(2,1)S(1)}, bf16[1,4,48,1536]{3,2,1,0:T(8,128)(2,1)}, u32[]{:S(2)}, u32[]{:S(2)}) collective-permute-start(bf16[1,4,48,1536]{3,2,1,0:T(8,128)(2,1)S(1)} %bitcast.76), channel_id=1, source_target_pairs={{0,8},{4,12},{8,0},{12,4},{16,24},{20,28},{24,16},{28,20},{1,9},{5... | collective-permute-start | bytes 1769480 | tf_op jit(solution)/shard_map/ppermute | solution.py:319
  7.9 15.3 %collective-permute-start.2 = (bf16[1,4,48,1536]{3,2,1,0:T(8,128)(2,1)S(1)}, bf16[1,4,48,1536]{3,2,1,0:T(8,128)(2,1)}, u32[]{:S(2)}, u32[]{:S(2)}) collective-permute-start(bf16[1,4,48,1536]{3,2,1,0:T(8,128)(2,1)S(1)} %bitcast.78), channel_id=1, source_target_pairs={{0,16},{4,20},{8,24},{12,28},{16,0},{20,4},{24,8},{28,12},{1,17},{... | collective-permute-start | bytes 1769480 | tf_op jit(solution)/shard_map/ppermute | solution.py:319
  10.8 37.4 %all-to-all-start = ((bf16[4,48,3584]{2,1,0:T(8,128)(2,1)}), bf16[4,48,3584]{2,1,0:T(8,128)(2,1)S(1)}, u32[]{:S(2)}, u32[]{:S(2)}) async-start(bf16[4,48,3584]{2,1,0:T(8,128)(2,1)} %broadcast_in_dim.43), calls=%async_computation | async-start | bytes 2752512 | tf_op jit(solution)/shard_map/all_to_all | solution.py:357
  35.0 28.7 %collective-permute-start.4 = (bf16[2,4,48,1536]{3,2,1,0:T(8,128)(2,1)}, bf16[2,4,48,1536]{3,2,1,0:T(8,128)(2,1)}, u32[]{:S(2)}, u32[]{:S(2)}) collective-permute-start(bf16[2,4,48,1536]{3,2,1,0:T(8,128)(2,1)} %pad_maximum_fusion.3.refs_0_), channel_id=1, source_target_pairs={{0,16},{4,20},{8,24},{12,28},{16,0},{20,4},{24,8},{28,12},{1,17},{... | collective-permute-start | bytes 3538952 | tf_op jit(solution)/shard_map/ppermute | solution.py:319
  37.7 28.3 %collective-permute-start.5 = (bf16[2,4,48,1536]{3,2,1,0:T(8,128)(2,1)S(1)}, bf16[2,4,48,1536]{3,2,1,0:T(8,128)(2,1)}, u32[]{:S(2)}, u32[]{:S(2)}) collective-permute-start(bf16[2,4,48,1536]{3,2,1,0:T(8,128)(2,1)S(1)} %pad_maximum_fusion.4.refs_0_), channel_id=1, source_target_pairs={{0,8},{4,12},{8,0},{12,4},{16,24},{20,28},{24,16},{28,20},{1,9},{5... | collective-permute-start | bytes 3538952 | tf_op jit(solution)/shard_map/ppermute | solution.py:319
  48.1 32.4 %all-to-all-start.1 = ((bf16[4,2,2,48,768]{4,3,2,1,0:T(8,128)(2,1)}), bf16[4,2,2,48,768]{4,3,2,1,0:T(8,128)(2,1)}, u32[]{:S(2)}, u32[]{:S(2)}) async-start(bf16[4,2,2,48,768]{4,3,2,1,0:T(8,128)(2,1)} %get-tuple-element.19), calls=%async_computation.1 | async-start | bytes 2359296 | tf_op jit(solution)/shard_map/all_to_all | solution.py:357
  66.1 18.9 %collective-permute-start.6 = (bf16[1,192,2048]{2,1,0:T(8,128)(2,1)S(1)}, bf16[1,192,2048]{2,1,0:T(8,128)(2,1)S(1)}, u32[]{:S(2)}, u32[]{:S(2)}) collective-permute-start(bf16[1,192,2048]{2,1,0:T(8,128)(2,1)S(1)} %slice_bitcast_fusion.2), channel_id=1, source_target_pairs={{0,8},{4,12},{8,0},{12,4},{16,24},{20,28},{24,16},{28,20},{1,9},{5... | collective-permute-start | bytes 2359304 | tf_op jit(solution)/shard_map/ppermute | solution.py:319
  66.7 16.1 %collective-permute-start.7 = (bf16[1,192,1536]{2,1,0:T(8,128)(2,1)S(1)}, bf16[1,192,1536]{2,1,0:T(8,128)(2,1)S(1)}, u32[]{:S(2)}, u32[]{:S(2)}) collective-permute-start(bf16[1,192,1536]{2,1,0:T(8,128)(2,1)S(1)} %slice_bitcast_fusion.3), channel_id=1, source_target_pairs={{0,16},{4,20},{8,24},{12,28},{16,0},{20,4},{24,8},{28,12},{1,17},{... | collective-permute-start | bytes 1769480 | tf_op jit(solution)/shard_map/ppermute | solution.py:319
  86.5 43.3 %all-to-all-start.2 = ((bf16[4,128,1664]{2,1,0:T(8,128)(2,1)}), bf16[4,128,1664]{2,1,0:T(8,128)(2,1)S(1)}, u32[]{:S(2)}, u32[]{:S(2)}) async-start(bf16[4,128,1664]{2,1,0:T(8,128)(2,1)} %broadcast_in_dim.46), calls=%async_computation.2 | async-start | bytes 3407872 | tf_op jit(solution)/shard_map/all_to_all | solution.py:357
  93.1 41.2 %collective-permute-start.10 = (bf16[2,192,2048]{2,1,0:T(8,128)(2,1)S(1)}, bf16[2,192,2048]{2,1,0:T(8,128)(2,1)}, u32[]{:S(2)}, u32[]{:S(2)}) collective-permute-start(bf16[2,192,2048]{2,1,0:T(8,128)(2,1)S(1)} %pad_maximum_fusion.1.refs_3_), channel_id=1, source_target_pairs={{0,16},{4,20},{8,24},{12,28},{16,0},{20,4},{24,8},{28,12},{1,17},{... | collective-permute-start | bytes 4718600 | tf_op jit(solution)/shard_map/ppermute | solution.py:319
  96.2 40.1 %collective-permute-start.15 = (bf16[2,192,1536]{2,1,0:T(8,128)(2,1)}, bf16[2,192,1536]{2,1,0:T(8,128)(2,1)}, u32[]{:S(2)}, u32[]{:S(2)}) collective-permute-start(bf16[2,192,1536]{2,1,0:T(8,128)(2,1)} %pad_maximum_fusion.7.refs_0_), channel_id=1, source_target_pairs={{0,8},{4,12},{8,0},{12,4},{16,24},{20,28},{24,16},{28,20},{1,9},{5... | collective-permute-start | bytes 3538952 | tf_op jit(solution)/shard_map/ppermute | solution.py:319
  97.3 46.2 %collective-permute-start.11 = (bf16[2,192,2048]{2,1,0:T(8,128)(2,1)S(1)}, bf16[2,192,2048]{2,1,0:T(8,128)(2,1)}, u32[]{:S(2)}, u32[]{:S(2)}) collective-permute-start(bf16[2,192,2048]{2,1,0:T(8,128)(2,1)S(1)} %pad_maximum_fusion.1.refs_3_), channel_id=1, source_target_pairs={{0,4},{4,0},{8,12},{12,8},{16,20},{20,16},{24,28},{28,24},{1,5},{5... | collective-permute-start | bytes 4718600 | tf_op jit(solution)/shard_map/ppermute | solution.py:319
  98.4 38.5 %collective-permute-start.8 = (bf16[1,384,768]{2,1,0:T(8,128)(2,1)}, bf16[1,384,768]{2,1,0:T(8,128)(2,1)}, u32[]{:S(2)}, u32[]{:S(2)}) collective-permute-start(bf16[1,384,768]{2,1,0:T(8,128)(2,1)} %bitcast.22), channel_id=1, source_target_pairs={{0,8},{4,12},{8,0},{12,4},{16,24},{20,28},{24,16},{28,20},{1,9},{5... | collective-permute-start | bytes 1769480 | tf_op jit(solution)/shard_map/ppermute | solution.py:319
  101.4 39.0 %collective-permute-start.9 = (bf16[1,384,768]{2,1,0:T(8,128)(2,1)}, bf16[1,384,768]{2,1,0:T(8,128)(2,1)}, u32[]{:S(2)}, u32[]{:S(2)}) collective-permute-start(bf16[1,384,768]{2,1,0:T(8,128)(2,1)} %bitcast.80), channel_id=1, source_target_pairs={{0,16},{4,20},{8,24},{12,28},{16,0},{20,4},{24,8},{28,12},{1,17},{... | collective-permute-start | bytes 1769480 | tf_op jit(solution)/shard_map/ppermute | solution.py:319
  129.8 38.4 %all-to-all-start.3 = ((bf16[4,2,2,48,768]{4,3,2,1,0:T(8,128)(2,1)}), bf16[4,2,2,48,768]{4,3,2,1,0:T(8,128)(2,1)}, u32[]{:S(2)}, u32[]{:S(2)}) async-start(bf16[4,2,2,48,768]{4,3,2,1,0:T(8,128)(2,1)} %get-tuple-element.28), calls=%async_computation.3 | async-start | bytes 2359296 | tf_op jit(solution)/shard_map/all_to_all | solution.py:357
  136.3 39.5 %collective-permute-start.16 = (bf16[2,192,1536]{2,1,0:T(8,128)(2,1)}, bf16[2,192,1536]{2,1,0:T(8,128)(2,1)}, u32[]{:S(2)}, u32[]{:S(2)}) collective-permute-start(bf16[2,192,1536]{2,1,0:T(8,128)(2,1)} %pad_maximum_fusion.7.refs_0_), channel_id=1, source_target_pairs={{0,4},{4,0},{8,12},{12,8},{16,20},{20,16},{24,28},{28,24},{1,5},{5... | collective-permute-start | bytes 3538952 | tf_op jit(solution)/shard_map/ppermute | solution.py:319
  136.8 39.0 %collective-permute-start.17 = (bf16[2,192,1536]{2,1,0:T(8,128)(2,1)}, bf16[2,192,1536]{2,1,0:T(8,128)(2,1)}, u32[]{:S(2)}, u32[]{:S(2)}) collective-permute-start(bf16[2,192,1536]{2,1,0:T(8,128)(2,1)} %collective-permute-done.15.refs_1_), channel_id=1, source_target_pairs={{0,4},{4,0},{8,12},{12,8},{16,20},{20,16},{24,28},{28,24},{1,5},{5... | collective-permute-start | bytes 3538952 | tf_op jit(solution)/shard_map/ppermute | solution.py:319
  140.4 30.8 %collective-permute-start.13 = (bf16[2,384,768]{2,1,0:T(8,128)(2,1)}, bf16[2,384,768]{2,1,0:T(8,128)(2,1)}, u32[]{:S(2)}, u32[]{:S(2)}) collective-permute-start(bf16[2,384,768]{2,1,0:T(8,128)(2,1)} %pad_maximum_fusion.5), channel_id=1, source_target_pairs={{0,16},{4,20},{8,24},{12,28},{16,0},{20,4},{24,8},{28,12},{1,17},{... | collective-permute-start | bytes 3538952 | tf_op jit(solution)/shard_map/ppermute | solution.py:319
  143.5 32.3 %collective-permute-start.14 = (bf16[2,384,768]{2,1,0:T(8,128)(2,1)}, bf16[2,384,768]{2,1,0:T(8,128)(2,1)}, u32[]{:S(2)}, u32[]{:S(2)}) collective-permute-start(bf16[2,384,768]{2,1,0:T(8,128)(2,1)} %pad_maximum_fusion.6), channel_id=1, source_target_pairs={{0,8},{4,12},{8,0},{12,4},{16,24},{20,28},{24,16},{28,20},{1,9},{5... | collective-permute-start | bytes 3538952 | tf_op jit(solution)/shard_map/ppermute | solution.py:319
  169.6 15.5 %collective-permute-start.20 = (bf16[1,384,768]{2,1,0:T(8,128)(2,1)S(1)}, bf16[1,384,768]{2,1,0:T(8,128)(2,1)S(1)}, u32[]{:S(2)}, u32[]{:S(2)}) collective-permute-start(bf16[1,384,768]{2,1,0:T(8,128)(2,1)S(1)} %get-tuple-element.46), channel_id=1, source_target_pairs={{0,8},{4,12},{8,0},{12,4},{16,24},{20,28},{24,16},{28,20},{1,9},{5... | collective-permute-start | bytes 1769480 | tf_op jit(solution)/shard_map/ppermute | solution.py:319
  185.3 28.4 %collective-permute-start.21 = (bf16[2,384,768]{2,1,0:T(8,128)(2,1)S(1)}, bf16[2,384,768]{2,1,0:T(8,128)(2,1)S(1)}, u32[]{:S(2)}, u32[]{:S(2)}) collective-permute-start(bf16[2,384,768]{2,1,0:T(8,128)(2,1)S(1)} %pad_maximum_fusion.8), channel_id=1, source_target_pairs={{0,16},{4,20},{8,24},{12,28},{16,0},{20,4},{24,8},{28,12},{1,17},{... | collective-permute-start | bytes 3538952 | tf_op jit(solution)/shard_map/ppermute | solution.py:319
  187.1 28.4 %collective-permute-start.23 = (bf16[2,384,768]{2,1,0:T(8,128)(2,1)S(1)}, bf16[2,384,768]{2,1,0:T(8,128)(2,1)}, u32[]{:S(2)}, u32[]{:S(2)}) collective-permute-start(bf16[2,384,768]{2,1,0:T(8,128)(2,1)S(1)} %pad_maximum_fusion.9), channel_id=1, source_target_pairs={{0,8},{4,12},{8,0},{12,4},{16,24},{20,28},{24,16},{28,20},{1,9},{5... | collective-permute-start | bytes 3538952 | tf_op jit(solution)/shard_map/ppermute | solution.py:319
  243.6 34.7 %collective-permute-start.26 = (bf16[128,1536]{1,0:T(8,128)(2,1)}, bf16[128,1536]{1,0:T(8,128)(2,1)S(1)}, u32[]{:S(2)}, u32[]{:S(2)}) collective-permute-start(bf16[128,1536]{1,0:T(8,128)(2,1)} %get-tuple-element.36), channel_id=1, source_target_pairs={{0,2},{1,3},{2,0},{3,1},{4,6},{5,7},{6,4},{7,5},{8,10},{9,11},{10,... | collective-permute-start | bytes 1179656 | tf_op jit(solution)/shard_map/ppermute | solution.py:315
  243.6 34.7 %collective-permute-start.25 = (bf16[128,1536]{1,0:T(8,128)(2,1)}, bf16[128,1536]{1,0:T(8,128)(2,1)S(1)}, u32[]{:S(2)}, u32[]{:S(2)}) collective-permute-start(bf16[128,1536]{1,0:T(8,128)(2,1)} %get-tuple-element.34), channel_id=1, source_target_pairs={{0,1},{1,0},{2,3},{3,2},{4,5},{5,4},{6,7},{7,6},{8,9},{9,8},{10,11... | collective-permute-start | bytes 1179656 | tf_op jit(solution)/shard_map/ppermute | solution.py:315
  (32 other events, 192.2 us)
